TPU v7x, 512 devices: a whole 4x8x8 slice. The times are simulated.
512 devices in a mesh: dp: 16 (over z, core), latent: 32 (over x, y).
Axes of the slice: x: 4, y: 8, z: 8, core: 2. Of those that a mesh axis runs over, the one named last changes fastest.
Arguments:
- activations: bfloat16 [16384, 8192], P('latent', 'dp'), may hold values from -6 to 6
- weight: bfloat16 [8192, 8192], P('dp', 'latent'), may hold values from -0.0625 to 0.0625
- enc_bias: float32 [8192], replicated, may hold values from -3 to 3
- dec_bias: float32 [8192], P('dp'), may hold values from -3 to 3
- block_ids: int32 [32, 8], P('latent'), may hold values from 0 to 63, as said below
- counts: int32 [32], P('latent'), may hold values from 1 to 8, as said below
Outputs:
- weight_grad: float32 [8192, 8192], P('dp', 'latent')
- row_error: float32 [16384], P(('latent', 'dp'))
Inputs may be any that keep to these rules, and one draw needn't show every extreme that they name: `block_ids`: each row block's list names 8 latent blocks of 8 different owners (block k belongs to owner k // 2); only its first counts entries are active, and some blocks are listed far more often than others. `counts`: some row block has all 8 entries active.
All inputs are finite; a program needn't handle non-finite values.
Results may differ from a plain program's by a relative error of at most 0.0028.
Values may be sent and summed in bfloat16 or wider, within the bound.
No kernel may reach another device: no remote copies, remote signals or barrier semaphores. Data moves between devices by JAX's collectives and lax.ppermute only.
A program may use at most 64 MiB of HBM per device.

v0:
```python
import math

import jax
import jax.numpy as jnp
from jax import lax
from jax.sharding import PartitionSpec as P

BLK = 128


def on_device(activations, weight, enc_bias, dec_bias, block_ids, counts):
    rows, width = activations.shape
    block = BLK
    per_owner = weight.shape[1] // block
    owners = lax.axis_size("latent")
    groups = lax.axis_size("dp")
    share = rows // groups
    myself = lax.axis_index("latent")
    all_ids, all_counts = (
        lax.all_gather(block_ids, "latent", axis=0, tiled=True),
        lax.all_gather(counts, "latent", axis=0, tiled=True),
    )
    ids = block_ids[0]
    slots = ids.shape[0]
    live = (jnp.arange(slots) < counts[0]).astype(jnp.float32)
    live_cols = live[:, None, None]
    all_live = (jnp.arange(slots)[None, :] < all_counts[:, None]).astype(jnp.float32)
    own_blocks = myself * per_owner + jnp.arange(per_owner)
    matches = (all_ids[:, :, None] == own_blocks[None, None, :]).astype(jnp.float32) * all_live[
        :, :, None
    ]
    selection = jnp.sum(matches, axis=1).astype(jnp.bfloat16)
    source = (
        (ids[:, None] // per_owner == jnp.arange(owners)[None, :]).astype(jnp.float32)
        * live[:, None]
    ).astype(jnp.bfloat16)
    scale_grad = 2.0 / math.sqrt(rows * owners)
    centered = (activations.astype(jnp.float32) - dec_bias).astype(jnp.bfloat16)
    piece = lax.all_gather(weight, "latent", axis=1, tiled=True)
    number = piece.shape[1] // block
    wanted = (ids[:, None] == jnp.arange(number)[None, :]).astype(jnp.bfloat16)
    picked = jnp.einsum(
        "sb,dbk->sdk",
        wanted,
        piece.reshape(width, number, block),
        preferred_element_type=jnp.float32,
    )
    tiles = picked.astype(jnp.bfloat16)
    bias_rows = jnp.take(enc_bias.reshape(-1, block), ids, axis=0)[:, None, :]
    part_pre = jnp.einsum("rd,sdk->srk", centered, tiles, preferred_element_type=jnp.float32)
    pre = lax.psum(part_pre, "dp") + bias_rows
    act = (jnp.maximum(pre, 0.0) * live_cols).astype(jnp.bfloat16)
    recon = jnp.einsum("srk,sdk->rd", act, tiles, preferred_element_type=jnp.float32) + dec_bias
    err = recon - activations.astype(jnp.float32)
    grad_out = (err * scale_grad).astype(jnp.bfloat16)
    part_loss = jnp.sum(err * err, axis=1) / (width * groups)
    part_grad = jnp.einsum("rd,sdk->srk", grad_out, tiles, preferred_element_type=jnp.float32)
    grad_act, row_total = lax.psum((part_grad, part_loss), "dp")
    grad_pre = (jnp.where(pre > 0, grad_act, 0.0) * live_cols).astype(jnp.bfloat16)
    row_error = lax.dynamic_slice_in_dim(row_total, lax.axis_index("dp") * share, share)
    first = jnp.einsum("rd,srk->sdk", centered, grad_pre, preferred_element_type=jnp.float32)
    second = jnp.einsum("rd,srk->sdk", grad_out, act, preferred_element_type=jnp.float32)
    contribution = (first + second).astype(jnp.bfloat16)
    sending = jnp.einsum(
        "sj,sdk->jdk", source, contribution, preferred_element_type=jnp.float32
    ).astype(jnp.bfloat16)
    received = lax.all_to_all(sending, "latent", split_axis=0, concat_axis=0, tiled=True)
    weight_grad = jnp.einsum("rb,rdk->dbk", selection, received, preferred_element_type=jnp.float32)
    return (weight_grad.reshape(width, per_owner * block), row_error)


def solution(mesh):
    placed = (P("latent", "dp"), P("dp", "latent"), P(), P("dp"), P("latent", None), P("latent"))
    return jax.shard_map(
        on_device,
        mesh=mesh,
        in_specs=placed,
        out_specs=(P("dp", "latent"), P(("latent", "dp"))),
        check_vma=False,
    )
```

profile of v0, /device:TPU:1, one launch (start us, length us, event | category | flops | bytes accessed | tf_op | source)
XLA Modules:
  0.0 583.5 jit_solution(1190068990571921230)
XLA Ops:
  7.2 0.0 copy-start
  7.2 0.0 all-gather.3.cloned.1.call-start
  7.2 0.7 all-gather.3.cloned.1.call-update
  7.9 0.0 all-reduce.4.cloned.1.call-start
  8.0 1.3 copy.19
  9.2 113.8 %all-gather.3.cloned.1.call-done = bf16[512,8192]{1,0:T(8,128)(2,1)} async-done(((bf16[512,256]{1,0:T(8,128)(2,1)}), bf16[512,8192]{1,0:T(8,128)(2,1)}) %all-gather.3.cloned.1.call-update) | async-done | bytes 8388624 | tf_op jit(solution)/shard_map/all_gather | solution.py:39
  123.0 0.0 copy-start.5
  123.0 9.3 %copy.41 = bf16[64,8,64,128]{3,2,1,0:T(8,128)(2,1)} copy(bf16[64,8,64,128]{3,1,2,0:T(8,128)(2,1)} %bitcast.55) | data formatting | bytes 16777216
  132.3 0.0 copy-done.5
  132.3 0.0 copy-start.4
  132.3 4.6 convolution_convert_fusion.1
  136.9 0.0 copy-done.4
  136.9 2.1 convolution_bitcast_fusion.1
  139.1 0.0 all-reduce.4.cloned.1.call-update
  139.1 0.0 all-reduce.6.cloned.1.call-start
  139.8 0.0 copy-done
  139.8 0.6 gather_fusion
  140.4 0.1 broadcast_select_fusion
  140.5 120.1 %all-reduce.4.cloned.1.call-done = f32[8,512,128]{1,2,0:T(8,128)} async-done(((f32[8,512,128]{1,2,0:T(8,128)}), f32[8,512,128]{1,2,0:T(8,128)}) %all-reduce.4.cloned.1.call-update) | async-done | bytes 2097168 | tf_op jit(solution)/shard_map/psum | solution.py:51
  260.6 2.5 multiply_reduce_fusion
  263.1 0.0 copy-start.2
  263.1 1.0 copy-done.2
  264.1 2.1 convolution_bitcast_fusion
  266.1 0.0 copy-start.1
  266.1 0.0 all-reduce.6.cloned.1.call-update
  266.2 120.7 %all-reduce.6.cloned.1.call-done = f32[8,512,128]{1,2,0:T(8,128)} async-done(((f32[8,512,128]{1,2,0:T(8,128)}), f32[8,512,128]{1,2,0:T(8,128)}) %all-reduce.6.cloned.1.call-update) | async-done | bytes 2097168 | tf_op jit(solution)/shard_map/psum | solution.py:58
  386.9 0.0 copy-done.1
  386.9 0.0 copy-start.3
  386.9 2.5 fusion.5
  389.4 0.0 copy-done.3
  389.4 0.8 fusion.2
  390.3 0.8 copy.28
  391.0 1.3 convolution_convert_fusion
  392.4 3.6 copy.29
  396.0 9.4 %all-to-all-start = ((bf16[32,512,128]{2,1,0:T(8,128)(2,1)}), bf16[32,512,128]{2,1,0:T(8,128)(2,1)}, u32[]{:S(2)}, u32[]{:S(2)}) async-start(bf16[32,512,128]{2,1,0:T(8,128)(2,1)} %copy.29), calls=%async_computation | async-start | bytes 8388608 | tf_op jit(solution)/shard_map/all_to_all | solution.py:67
  405.4 116.0 %all-gather = s32[32,1,8]{2,1,0:T(1,128)S(1)} all-gather(s32[1,1,8]{2,1,0:T(1,128)S(1)} %bitcast.60), channel_id=1, replica_groups=mesh['dp'=16,'latent'=32] {'latent'}, dimensions={0}, use_global_device_ids=true | all-gather | bytes 1056 | tf_op jit(solution)/shard_map/all_gather | solution.py:20
  521.4 0.1 copy.30
  521.5 1.3 dynamic-slice
  522.7 0.8 dynamic-update-slice
  523.5 12.8 %all-reduce = s32[32]{0:T(128)S(1)} all-reduce(s32[32]{0:T(128)S(1)} %dynamic-update-slice), channel_id=1, replica_groups=mesh['dp'=16,'latent'=32] {'latent'}, use_global_device_ids=true, to_apply=%add | all-reduce | flops 32 | bytes 256
  536.3 0.1 select_reduce_fusion
  536.4 34.6 %psum.23 = f32[512]{0:T(512)S(1)} all-reduce(f32[512]{0:T(512)S(1)} %broadcast_multiply_fusion), channel_id=1, replica_groups=mesh['dp'=16,'latent'=32] {'dp'}, use_global_device_ids=true, to_apply=%region_4.5 | all-reduce | flops 512 | bytes 4096 | tf_op jit(solution)/shard_map/psum | solution.py:58
  571.0 0.6 dynamic_slice.3
  571.6 0.0 all-to-all-done
  571.6 4.6 fusion
  576.2 0.8 copy.54
  (9 shorter events, 0.0 us)
Async XLA Ops:
  7.2 132.6 %copy-start = (f32[8192]{0:T(1024)S(1)}, f32[8192]{0:T(1024)}, u32[]{:S(2)}) copy-start(f32[8192]{0:T(1024)} %param.8) | copy-start | bytes 98308
  7.2 115.8 %all-gather.3.cloned.1.call-start = ((), (), s32[]{:S(2)}) async-start(), calls=%async_computation.1 | async-start | bytes 8650752 | tf_op jit(solution)/shard_map/all_gather | solution.py:39
  7.9 252.7 %all-reduce.4.cloned.1.call-start = ((), (), s32[]{:S(2)}) async-start(), calls=%async_computation.2 | async-start | bytes 4194304 | tf_op jit(solution)/shard_map/psum | solution.py:51
  123.0 9.3 %copy-start.5 = (s32[1,8]{1,0:T(1,128)S(1)}, s32[1,8]{1,0:T(1,128)}, u32[]{:S(2)}) copy-start(s32[1,8]{1,0:T(1,128)} %param.10) | copy-start | bytes 100
  132.3 4.6 copy-start.4
  139.1 247.8 %all-reduce.6.cloned.1.call-start = ((), (), s32[]{:S(2)}) async-start(), calls=%async_computation.3 | async-start | bytes 4194304 | tf_op jit(solution)/shard_map/psum | solution.py:58
  263.1 1.0 copy-start.2
  266.1 120.8 %copy-start.1 = (f32[8,512,128]{1,2,0:T(8,128)S(1)}, f32[8,512,128]{1,2,0:T(8,128)}, u32[]{:S(2)}) copy-start(f32[8,512,128]{1,2,0:T(8,128)} %all-reduce.4.cloned.1.call-done) | copy-start | bytes 6291460
  386.9 2.6 copy-start.3
  396.0 175.6 %all-to-all-start = ((bf16[32,512,128]{2,1,0:T(8,128)(2,1)}), bf16[32,512,128]{2,1,0:T(8,128)(2,1)}, u32[]{:S(2)}, u32[]{:S(2)}) async-start(bf16[32,512,128]{2,1,0:T(8,128)(2,1)} %copy.29), calls=%async_computation | async-start | bytes 8388608 | tf_op jit(solution)/shard_map/all_to_all | solution.py:67
Sparse Core Ops, SparseCore 0:
  11.1 111.8 all-gather.2
  139.2 121.3 all-reduce.3
  266.3 120.5 all-reduce.5
where the time goes:
time: 584 us
  waiting for transfers between devices  355 us (61%)
  blocking collectives  163 us (28%)
  matrix products  20.6 us (4%)
  local copies, waits for them, and re-layouts  20 us (3%)
  between operations  14.5 us (2%)
  starting transfers between devices  9.52 us (2%)
    psum x1, waiting for transfers between devices, on_device(): grad_act, row_total = lax.psum((part_grad, part_loss), 'dp')  121 us
    psum x1, waiting for transfers between devices, on_device(): pre = lax.psum(part_pre, 'dp') + bias_rows  120 us
    all_gather x1, blocking collectives, on_device(): lax.all_gather(block_ids, 'latent', axis=0, tiled=True)  116 us
    all_gather x1, waiting for transfers between devices, on_device(): piece = lax.all_gather(weight, 'latent', axis=1, tiled=True)  114 us
    psum x1, blocking collectives, on_device(): grad_act, row_total = lax.psum((part_grad, part_loss), 'dp')  34.6 us
    unnamed x19, local copies, waits for them, and re-layouts  14.5 us
    unnamed x1, blocking collectives  12.8 us
  transfers between devices with their start and end apart: 4, of which 3 were waited for; matrix products, arithmetic and copies ran while one was open for 1% of the time, Pallas kernels for 0%

commit v1 on v0

v1 whole, which is shorter than its diff:
```python
import functools
import math

import jax
import jax.numpy as jnp
from jax import lax
from jax.experimental import pallas as pl
from jax.experimental.pallas import tpu as pltpu
from jax.sharding import PartitionSpec as P

BLK = 128
BF16 = jnp.bfloat16
F32 = jnp.float32
VMEM_LIMIT = 40 * 1024 * 1024
SMEM_SPEC = pl.BlockSpec(memory_space=pltpu.SMEM)
VMEM_SPEC = pl.BlockSpec(memory_space=pltpu.VMEM)
ANY_SPEC = pl.BlockSpec(memory_space=pl.ANY)


def contract(a, b, dim_a, dim_b):
    return lax.dot_general(a, b, (((dim_a,), (dim_b,)), ((), ())), preferred_element_type=F32)


def call(kernel, out_shape, in_specs, out_specs, flops=0, bytes_accessed=0, scratch=(), **more):
    return pl.pallas_call(
        kernel,
        out_shape=out_shape,
        in_specs=in_specs,
        out_specs=out_specs,
        scratch_shapes=list(scratch),
        compiler_params=pltpu.CompilerParams(vmem_limit_bytes=VMEM_LIMIT),
        cost_estimate=pl.CostEstimate(
            flops=flops, bytes_accessed=bytes_accessed, transcendentals=0
        ),
        **more,
    )


def encode_kernel(slots, ids, give_x, keep_x, head, tail, give, keep, tiles, sems):
    cut = head.shape[1]
    copies = []
    for s in range(slots):
        owner = ids[s] // 2
        lane = pl.multiple_of((ids[s] % 2) * BLK, BLK)
        columns = pl.ds(s * BLK, BLK)
        one = pltpu.make_async_copy(
            head.at[owner], tiles.at[pl.ds(0, cut), columns], sems.at[2 * s]
        )
        two = pltpu.make_async_copy(
            tail.at[owner, :, pl.ds(lane, BLK)],
            tiles.at[pl.ds(cut, tail.shape[1]), columns],
            sems.at[2 * s + 1],
        )
        one.start()
        two.start()
        copies.append((one, two))
    for s in range(0, slots, 2):
        for pair in copies[s : s + 2]:
            for copy in pair:
                copy.wait()
        columns = slice(s * BLK, (s + 2) * BLK)
        part = tiles[:, columns]
        give[:, columns] = contract(give_x[...], part, 1, 0)
        keep[:, columns] = contract(keep_x[...], part, 1, 0)


def activate_kernel(parts, bias, live, pre, spread):
    total = jnp.sum(parts[...], axis=0) + bias[...]
    pre[...] = total
    act = (jnp.maximum(total, 0.0) * live[...]).astype(BF16)
    spread[...] = jnp.broadcast_to(act[None], spread.shape)


def error_kernel(scale, loss_scale, act_g, act_k, tiles, x_g, x_k, bias, give, keep, out_g, out_k):
    latents = tiles.shape[1]
    for act, x, part, out in ((act_g, x_g, give, out_g), (act_k, x_k, keep, out_k)):
        err = contract(act[...], tiles[...], 1, 1) + bias[...] - x[...].astype(F32)
        loss = jnp.sum(err * err, axis=1, keepdims=True) * loss_scale
        grad = (err * scale).astype(BF16)
        out[...] = grad
        part[:, :latents] = contract(grad, tiles[...], 1, 0)
        part[:, latents:] = jnp.broadcast_to(loss, (loss.shape[0], BLK))


def second_kernel(out_g, out_k, act_g, act_k, second):
    latents = act_g.shape[1]
    for start in range(0, latents, 2 * BLK):
        columns = slice(start, start + 2 * BLK)
        second[:, columns] = contract(out_k[...], act_k[:, columns], 0, 0) + contract(
            out_g[...], act_g[:, columns], 0, 0
        )


def gate_kernel(parts, pre, live, spread, loss):
    latents = pre.shape[1]
    total = jnp.sum(parts[...], axis=0)
    grad = (jnp.where(pre[...] > 0, total[:, :latents], 0.0) * live[...]).astype(BF16)
    spread[...] = jnp.broadcast_to(grad[None], spread.shape)
    loss[...] = total[:, latents:]


def contribution_kernel(slots, ids, c_t, gp_g, gp_k, second, send, stage, sems):
    half = gp_g.shape[0]
    copies = []
    for s in range(0, slots, 2):
        columns = slice(s * BLK, (s + 2) * BLK)
        total = (
            contract(c_t[:, :half], gp_g[:, columns], 1, 0)
            + contract(c_t[:, half:], gp_k[:, columns], 1, 0)
            + second[:, columns]
        ).astype(BF16)
        for i in range(2):
            stage[s + i] = total[:, i * BLK : (i + 1) * BLK]
            copy = pltpu.make_async_copy(
                stage.at[s + i], send.at[ids[s + i] // 2], sems.at[s + i]
            )
            copy.start()
            copies.append(copy)
    for copy in copies:
        copy.wait()


def collect_kernel(owners, flags, parts, out):
    out[...] = jnp.zeros_like(out)

    def step(j, carry):
        flag = flags[j]
        for b in range(2):

            @pl.when(flag == b)
            def _():
                out[:, b * BLK : (b + 1) * BLK] += parts[j].astype(F32)

        return carry

    lax.fori_loop(0, owners, step, 0)


def on_device(activations, weight, enc_bias, dec_bias, block_ids, counts):
    rows, width = activations.shape
    owners = lax.axis_size("latent")
    groups = lax.axis_size("dp")
    share = rows // groups
    chips = groups // 2
    half = rows // 2
    slots = block_ids.shape[1]
    latents = slots * BLK
    myself = lax.axis_index("latent")
    core = lax.axis_index("dp") % 2
    same_core = [[2 * z + c for z in range(chips)] for c in range(2)]
    swap = [(q, q ^ 1) for q in range(groups)]
    cut = width * 5 // 8

    def across_chips(array):
        return lax.all_to_all(array, "dp", 0, 0, tiled=True, axis_index_groups=same_core)

    def shape(dims, dtype):
        return jax.ShapeDtypeStruct(dims, dtype)

    tail = lax.all_gather(weight[cut:], "latent", axis=0)

    ids = block_ids[0]
    note = jnp.concatenate([ids, counts])
    note = jnp.pad(note, (0, BLK - slots - 1))
    notes = lax.all_to_all(
        jnp.broadcast_to(note, (owners, 8, BLK)), "latent", 0, 0, tiled=True
    )[:, 0, :]
    all_ids = notes[:, :slots]
    all_counts = notes[:, slots]
    all_live = jnp.arange(slots)[None, :] < all_counts[:, None]
    mine = all_ids // 2 == myself
    upper = jnp.any(mine & (all_ids % 2 == 1), axis=1)
    flags = jnp.sum(jnp.where(mine & all_live, all_ids % 2 + 1, 0), axis=1) - 1

    head = jnp.where(upper[:, None, None], weight[None, :cut, BLK:], weight[None, :cut, :BLK])
    head = lax.all_to_all(head, "latent", 0, 0, tiled=True)

    live = (jnp.arange(slots) < counts[0]).astype(F32)
    live_row = jnp.repeat(live, BLK)[None, :]
    bias_row = jnp.take(enc_bias.reshape(-1, BLK), ids, axis=0).reshape(1, latents)
    by_chunk = activations.reshape(chips, 2, share, width)
    x_k = lax.dynamic_index_in_dim(by_chunk, core, 1, keepdims=False).reshape(half, width)
    x_g = lax.dynamic_index_in_dim(by_chunk, 1 - core, 1, keepdims=False).reshape(half, width)
    c_k = (x_k.astype(F32) - dec_bias).astype(BF16)
    c_g = (x_g.astype(F32) - dec_bias).astype(BF16)
    c_t = jnp.concatenate([c_g, c_k], axis=0).T

    matmul = 2 * half * width * latents
    give, keep, tiles = call(
        functools.partial(encode_kernel, slots),
        (shape((half, latents), F32), shape((half, latents), F32), shape((width, latents), BF16)),
        [SMEM_SPEC, VMEM_SPEC, VMEM_SPEC, ANY_SPEC, ANY_SPEC],
        (VMEM_SPEC, VMEM_SPEC, VMEM_SPEC),
        flops=2 * matmul,
        bytes_accessed=4 * half * latents * 4,
        scratch=[pltpu.SemaphoreType.DMA((2 * slots,))],
    )(ids, c_g, c_k, head, tail)

    keep = keep + lax.ppermute(give, "dp", swap)
    parts = across_chips(keep.reshape(chips, share, latents))
    pre, spread = call(
        activate_kernel,
        (shape((share, latents), F32), shape((chips, share, latents), BF16)),
        [VMEM_SPEC] * 3,
        (VMEM_SPEC, VMEM_SPEC),
        bytes_accessed=half * latents * 6,
    )(parts, bias_row, live_row)
    act_k = across_chips(spread).reshape(half, latents)
    act_g = lax.ppermute(act_k, "dp", swap)

    scale = 2.0 / math.sqrt(rows * owners)
    give, keep, out_g, out_k = call(
        functools.partial(error_kernel, scale, 1.0 / (width * groups)),
        (
            shape((half, latents + BLK), F32),
            shape((half, latents + BLK), F32),
            shape((half, width), BF16),
            shape((half, width), BF16),
        ),
        [VMEM_SPEC] * 6,
        (VMEM_SPEC,) * 4,
        flops=4 * matmul,
        bytes_accessed=half * latents * 14,
    )(act_g, act_k, tiles, x_g, x_k, dec_bias[None, :])
    keep = keep + lax.ppermute(give, "dp", swap)
    parts = across_chips(keep.reshape(chips, share, latents + BLK))
    second = call(
        second_kernel,
        shape((width, latents), F32),
        [VMEM_SPEC] * 4,
        VMEM_SPEC,
        flops=2 * matmul,
        bytes_accessed=half * latents * 16,
    )(out_g, out_k, act_g, act_k)
    spread, loss = call(
        gate_kernel,
        (shape((chips, share, latents), BF16), shape((share, BLK), F32)),
        [VMEM_SPEC] * 3,
        (VMEM_SPEC, VMEM_SPEC),
        bytes_accessed=half * latents * 6,
    )(parts, pre, live_row)
    row_error = loss[:, 0]
    gp_k = across_chips(spread).reshape(half, latents)
    gp_g = lax.ppermute(gp_k, "dp", swap)

    send = call(
        functools.partial(contribution_kernel, slots),
        shape((owners, width, BLK), BF16),
        [SMEM_SPEC] + [VMEM_SPEC] * 4,
        ANY_SPEC,
        flops=2 * matmul,
        bytes_accessed=half * latents * 16,
        scratch=[pltpu.VMEM((slots, width, BLK), BF16), pltpu.SemaphoreType.DMA((slots,))],
    )(ids, c_t, gp_g, gp_k, second)
    received = lax.all_to_all(send, "latent", 0, 0, tiled=True)

    chunk = min(width, 128)
    weight_grad = pl.pallas_call(
        functools.partial(collect_kernel, owners),
        grid=(width // chunk,),
        in_specs=[SMEM_SPEC, pl.BlockSpec((owners, chunk, BLK), lambda i: (0, i, 0))],
        out_specs=pl.BlockSpec((chunk, 2 * BLK), lambda i: (i, 0)),
        out_shape=shape((width, 2 * BLK), F32),
        compiler_params=pltpu.CompilerParams(vmem_limit_bytes=VMEM_LIMIT),
        cost_estimate=pl.CostEstimate(
            flops=owners * width * BLK, bytes_accessed=owners * width * BLK * 2, transcendentals=0
        ),
    )(flags, received)
    return (weight_grad, row_error)


def solution(mesh):
    placed = (P("latent", "dp"), P("dp", "latent"), P(), P("dp"), P("latent", None), P("latent"))
    return jax.shard_map(
        on_device,
        mesh=mesh,
        in_specs=placed,
        out_specs=(P("dp", "latent"), P(("latent", "dp"))),
        check_vma=False,
    )
```

time: 584 us -> 380 us (0.65)
  waiting for transfers between devices: 355 us -> 212 us
  blocking collectives: 163 us -> 74.9 us
  starting transfers between devices: 9.52 us -> 42.8 us
  matrix products: 20.6 us -> 0 us
  Pallas kernels: 0 us -> 13.6 us
  other arithmetic: 0.2 us -> 6.13 us
    psum x2 -> x0, waiting for transfers between devices: 241 us -> none  [the longest x1 121 us: on_device(): grad_act, row_total = lax.psum((part_grad, part_loss), 'dp')]
    all_to_all x1 -> x4, waiting for transfers between devices: 0.01 us -> 189 us  [the longest x1 93.3 us: on_device(): received = lax.all_to_all(send, 'latent', 0, 0, tiled=True)]
    all_gather x1 -> x0, blocking collectives: 116 us -> none  [on_device(): lax.all_gather(block_ids, 'latent', axis=0, tiled=True)]
    all_gather x1, waiting for transfers between devices: 114 us -> 15.9 us  [on_device(): tail = lax.all_gather(weight[cut:], 'latent', axis=0)]
    all_to_all x0 -> x3, blocking collectives: none -> 74.9 us  [across_chips(): lax.all_to_all(array, 'dp', 0, 0, tiled=True, axis_index_groups=same_core)]
    psum x1 -> x0, blocking collectives: 34.6 us -> none  [on_device(): grad_act, row_total = lax.psum((part_grad, part_loss), 'dp')]
    all_to_all x1 -> x4, starting transfers between devices: 9.4 us -> 31.3 us  [the longest x1 10.5 us: on_device(): lax.all_to_all(jnp.broadcast_to(note, (owners, 8, BLK)), 'latent', 0, 0,...]
    dot_general x8 -> x0, matrix products: 20.6 us -> none  [the longest x1 4.63 us: on_device(): jnp.einsum('sb,dbk->sdk', wanted, piece.reshape(width, number, block), pr...]
  transfers between devices with their start and end apart: 4 -> 9, of which waited for: 3 -> 9; matrix products, arithmetic and copies ran while one was open for 1% -> 3% of each run, Pallas kernels for 0% -> 0%
where the time goes in v1:
time: 380 us; the launch traced here: 378 us
  waiting for transfers between devices  212 us (56%)
  blocking collectives  74.9 us (20%)
  starting transfers between devices  42.8 us (11%)
  between operations  15 us (4%)
  local copies, waits for them, and re-layouts  14.4 us (4%)
  Pallas kernels  13.6 us (4%)
  other arithmetic  6.13 us (2%)
    all_to_all x1, waiting for transfers between devices, on_device(): received = lax.all_to_all(send, 'latent', 0, 0, tiled=True)  93.3 us
    all_to_all x3, blocking collectives, across_chips(): lax.all_to_all(array, 'dp', 0, 0, tiled=True, axis_index_groups=same_core)  74.9 us
    all_to_all x1, waiting for transfers between devices, on_device(): head = lax.all_to_all(head, 'latent', 0, 0, tiled=True)  58.7 us
    all_to_all x1, waiting for transfers between devices, across_chips(): lax.all_to_all(array, 'dp', 0, 0, tiled=True, axis_index_groups=same_core)  28.6 us
    all_gather x1, waiting for transfers between devices, on_device(): tail = lax.all_gather(weight[cut:], 'latent', axis=0)  15.9 us
    all_to_all x1, starting transfers between devices, on_device(): lax.all_to_all(jnp.broadcast_to(note, (owners, 8, BLK)), 'latent', 0, 0,...  10.5 us
    all_to_all x1, starting transfers between devices, across_chips(): lax.all_to_all(array, 'dp', 0, 0, tiled=True, axis_index_groups=same_core)  9.45 us
    all_to_all x1, waiting for transfers between devices, on_device(): lax.all_to_all(jnp.broadcast_to(note, (owners, 8, BLK)), 'latent', 0, 0,...  8.2 us
  transfers between devices with their start and end apart: 9, of which 9 were waited for; matrix products, arithmetic and copies ran while one was open for 3% of the time, Pallas kernels for 0%

profile of v1, /device:TPU:1, one launch (start us, length us, event | category | flops | bytes accessed | tf_op | source)
XLA Modules:
  0.0 378.4 jit_solution(1932779642910065038)
XLA Ops:
  7.2 0.0 copy-start
  7.2 0.0 all-gather.3.cloned.1.call-start
  7.2 1.5 slice.26
  8.8 0.0 all-gather.3.cloned.1.call-update
  9.4 0.7 pad_add_fusion
  10.2 0.7 broadcast_in_dim.51
  10.8 10.5 %all-to-all-start = ((s32[32,8,128]{2,1,0:T(8,128)}), s32[32,8,128]{2,1,0:T(8,128)S(1)}, u32[]{:S(2)}, u32[]{:S(2)}) async-start(s32[32,8,128]{2,1,0:T(8,128)} %broadcast_in_dim.51), calls=%async_computation | async-start | bytes 262144 | tf_op jit(solution)/shard_map/all_to_all | solution.py:165
  21.4 0.9 fusion.5
  22.3 8.2 %all-to-all-done = s32[32,8,128]{2,1,0:T(8,128)S(1)} async-done(((s32[32,8,128]{2,1,0:T(8,128)}), s32[32,8,128]{2,1,0:T(8,128)S(1)}, u32[]{:S(2)}, u32[]{:S(2)}) %all-to-all-start) | async-done | bytes 131104 | tf_op jit(solution)/shard_map/all_to_all | solution.py:165
  30.5 0.1 and_reduce_fusion
  30.7 1.8 broadcast_select_fusion
  32.4 4.2 %all-to-all-start.1 = ((bf16[32,320,128]{2,1,0:T(8,128)(2,1)}), bf16[32,320,128]{2,1,0:T(8,128)(2,1)S(1)}, u32[]{:S(2)}, u32[]{:S(2)}) async-start(bf16[32,320,128]{2,1,0:T(8,128)(2,1)} %broadcast_select_fusion), calls=%async_computation.1 | async-start | bytes 5242880 | tf_op jit(solution)/shard_map/all_to_all | solution.py:176
  36.6 0.0 copy-start.5
  36.7 1.1 constant_dynamic-slice_fusion.1
  37.7 0.1 copy.26
  37.9 0.8 copy.27
  38.7 0.0 copy-done.4
  38.7 1.9 subtract_convert_fusion.1
  40.6 1.1 copy.28.give_x
  41.7 1.8 copy.29.keep_x
  43.5 58.7 %all-to-all-done.1.head = bf16[32,320,128]{2,1,0:T(8,128)(2,1)S(1)} async-done(((bf16[32,320,128]{2,1,0:T(8,128)(2,1)}), bf16[32,320,128]{2,1,0:T(8,128)(2,1)S(1)}, u32[]{:S(2)}, u32[]{:S(2)}) %all-to-all-start.1) | async-done | bytes 2621472 | tf_op jit(solution)/shard_map/all_to_all | solution.py:176
  102.2 15.9 %all-gather.3.cloned.1.call-done = bf16[6144,256]{1,0:T(8,128)(2,1)} async-done(((bf16[192,256]{1,0:T(8,128)(2,1)}), bf16[6144,256]{1,0:T(8,128)(2,1)}) %all-gather.3.cloned.1.call-update) | async-done | bytes 3145744 | tf_op jit(solution)/shard_map/all_gather | solution.py:160
  118.1 0.0 copy-done.5
  118.1 1.9 copy-done.2
  120.0 0.9 copy-done.3
  121.0 2.2 shard_map.77
  123.2 0.0 copy-start.6
  123.2 4.1 %collective-permute-start = (f32[256,1024]{1,0:T(8,128)S(1)}, f32[256,1024]{1,0:T(8,128)S(1)}, u32[]{:S(2)}, u32[]{:S(2)}) collective-permute-start(f32[256,1024]{1,0:T(8,128)S(1)} %get-tuple-element.14), channel_id=1, source_target_pairs={{0,32},{32,0},{64,96},{96,64},{128,160},{160,128},{192,224},{224,1... | collective-permute-start | bytes 3145736 | tf_op jit(solution)/shard_map/ppermute | solution.py:199
  127.4 2.3 collective-permute-done
  129.6 1.2 add.53
  130.8 0.0 copy-done.6
  130.8 9.4 %all-to-all-start.2 = ((f32[8,32,1024]{2,1,0:T(8,128)}), f32[8,32,1024]{2,1,0:T(8,128)S(1)}, u32[]{:S(2)}, u32[]{:S(2)}) async-start(f32[8,32,1024]{2,1,0:T(8,128)} %bitcast.42), calls=%async_computation.2 | async-start | bytes 2097152 | tf_op jit(solution)/shard_map/all_to_all | solution.py:155
  140.3 0.0 copy-done
  140.3 0.6 gather_fusion
  140.8 0.1 broadcast_select_fusion.1
  140.9 28.6 %all-to-all-done.2.parts = f32[8,32,1024]{2,1,0:T(8,128)S(1)} async-done(((f32[8,32,1024]{2,1,0:T(8,128)}), f32[8,32,1024]{2,1,0:T(8,128)S(1)}, u32[]{:S(2)}, u32[]{:S(2)}) %all-to-all-start.2) | async-done | bytes 1048608 | tf_op jit(solution)/shard_map/all_to_all | solution.py:155
  169.5 0.1 broadcast_in_dim.57
  169.5 0.1 shard_map.78
  169.6 20.1 %all_to_all.35 = bf16[8,32,1024]{2,1,0:T(8,128)(2,1)S(1)} all-to-all(bf16[8,32,1024]{2,1,0:T(8,128)(2,1)S(1)} %get-tuple-element.15), channel_id=1, replica_groups={{0,64,128,192,256,320,384,448},{32,96,160,224,288,352,416,480},{1,65,12..., dimensions={0} | all-to-all | bytes 1048576 | tf_op jit(solution)/shard_map/all_to_all | solution.py:155
  189.8 2.6 collective-permute-start.1
  192.4 1.5 collective-permute-done.1.act_g
  193.9 0.0 copy-done.7
  193.9 1.5 shard_map.79
  195.4 2.3 collective-permute-start.2
  197.7 2.5 collective-permute-done.2
  200.2 0.1 add.56
  200.3 0.0 copy-start.8
  200.3 0.0 copy-start.9
  200.3 34.5 %all_to_all.36.parts = f32[8,32,1152]{2,1,0:T(8,128)S(1)} all-to-all(f32[8,32,1152]{2,1,0:T(8,128)S(1)} %bitcast.41), channel_id=1, replica_groups={{0,64,128,192,256,320,384,448},{32,96,160,224,288,352,416,480},{1,65,12..., dimensions={0} | all-to-all | bytes 2359296 | tf_op jit(solution)/shard_map/all_to_all | solution.py:155
  234.9 0.1 shard_map.80
  234.9 20.3 %all_to_all.37 = bf16[8,32,1024]{2,1,0:T(8,128)(2,1)S(1)} all-to-all(bf16[8,32,1024]{2,1,0:T(8,128)(2,1)S(1)} %get-tuple-element.20), channel_id=1, replica_groups={{0,64,128,192,256,320,384,448},{32,96,160,224,288,352,416,480},{1,65,12..., dimensions={0} | all-to-all | bytes 1048576 | tf_op jit(solution)/shard_map/all_to_all | solution.py:155
  255.2 2.5 collective-permute-start.3
  257.7 0.0 copy-done.8
  257.7 0.0 copy-done.9
  257.8 0.8 shard_map.81.second
  258.5 0.7 collective-permute-done.3.gp_g
  259.2 3.7 shard_map.82
  262.9 2.0 copy-done.1
  264.9 7.1 %all-to-all-start.6 = ((bf16[32,512,128]{2,1,0:T(8,128)(2,1)}), bf16[32,512,128]{2,1,0:T(8,128)(2,1)}, u32[]{:S(2)}, u32[]{:S(2)}) async-start(bf16[32,512,128]{2,1,0:T(8,128)(2,1)} %copy-done.1), calls=%async_computation.6 | async-start | bytes 8388608 | tf_op jit(solution)/shard_map/all_to_all | solution.py:255
  272.0 0.2 slice_reduce_fusion
  272.2 0.2 select_reduce_fusion
  272.4 0.6 slice_reduce_fusion.1
  273.1 93.3 %all-to-all-done.6.parts = bf16[32,512,128]{2,1,0:T(8,128)(2,1)} async-done(((bf16[32,512,128]{2,1,0:T(8,128)(2,1)}), bf16[32,512,128]{2,1,0:T(8,128)(2,1)}, u32[]{:S(2)}, u32[]{:S(2)}) %all-to-all-start.6) | async-done | bytes 4194336 | tf_op jit(solution)/shard_map/all_to_all | solution.py:255
  366.3 5.2 %shard_map.83 = f32[512,256]{1,0:T(8,128)} custom-call(s32[32]{0:T(128)S(1)} %broadcast_add_fusion.flags, bf16[32,512,128]{2,1,0:T(8,128)(2,1)} %all-to-all-done.6.parts), custom_call_target="tpu_custom_call" | custom-call | flops 2097152 | bytes 4194304 | tf_op jit(solution)/shard_map/pallas_call | solution.py:258
  (13 shorter events, 0.1 us)
Async XLA Ops:
  7.2 133.1 %copy-start = (f32[8192]{0:T(1024)S(1)}, f32[8192]{0:T(1024)}, u32[]{:S(2)}) copy-start(f32[8192]{0:T(1024)} %param.8) | copy-start | bytes 98308
  7.2 110.9 %all-gather.3.cloned.1.call-start = ((), (), s32[]{:S(2)}) async-start(), calls=%async_computation.7 | async-start | bytes 3244032 | tf_op jit(solution)/shard_map/all_gather | solution.py:160
  10.8 19.7 %all-to-all-start = ((s32[32,8,128]{2,1,0:T(8,128)}), s32[32,8,128]{2,1,0:T(8,128)S(1)}, u32[]{:S(2)}, u32[]{:S(2)}) async-start(s32[32,8,128]{2,1,0:T(8,128)} %broadcast_in_dim.51), calls=%async_computation | async-start | bytes 262144 | tf_op jit(solution)/shard_map/all_to_all | solution.py:165
  32.4 6.3 %copy-start.4 = (f32[512]{0:T(512)S(1)}, f32[512]{0:T(512)}, u32[]{:S(2)}) copy-start(f32[512]{0:T(512)} %param.9) | copy-start | bytes 6148
  32.4 69.8 %all-to-all-start.1 = ((bf16[32,320,128]{2,1,0:T(8,128)(2,1)}), bf16[32,320,128]{2,1,0:T(8,128)(2,1)S(1)}, u32[]{:S(2)}, u32[]{:S(2)}) async-start(bf16[32,320,128]{2,1,0:T(8,128)(2,1)} %broadcast_select_fusion), calls=%async_computation.1 | async-start | bytes 5242880 | tf_op jit(solution)/shard_map/all_to_all | solution.py:176
  36.6 81.5 %copy-start.5 = (s32[1,8]{1,0:T(1,128)S(1)}, s32[1,8]{1,0:T(1,128)}, u32[]{:S(2)}) copy-start(s32[1,8]{1,0:T(1,128)} %param.10) | copy-start | bytes 100
  118.1 1.9 copy-start.2
  120.0 0.9 copy-start.3
  123.2 7.6 %copy-start.6 = (bf16[512,1024]{1,0:T(8,128)(2,1)}, bf16[512,1024]{1,0:T(8,128)(2,1)S(1)}, u32[]{:S(2)}) copy-start(bf16[512,1024]{1,0:T(8,128)(2,1)S(1)} %get-tuple-element.16.tiles) | copy-start | bytes 3145732
  123.2 6.4 %collective-permute-start = (f32[256,1024]{1,0:T(8,128)S(1)}, f32[256,1024]{1,0:T(8,128)S(1)}, u32[]{:S(2)}, u32[]{:S(2)}) collective-permute-start(f32[256,1024]{1,0:T(8,128)S(1)} %get-tuple-element.14), channel_id=1, source_target_pairs={{0,32},{32,0},{64,96},{96,64},{128,160},{160,128},{192,224},{224,1... | collective-permute-start | bytes 3145736 | tf_op jit(solution)/shard_map/ppermute | solution.py:199
  130.8 63.1 %copy-start.7 = (bf16[512,1024]{1,0:T(8,128)(2,1)S(1)}, bf16[512,1024]{1,0:T(8,128)(2,1)}, u32[]{:S(2)}) copy-start(bf16[512,1024]{1,0:T(8,128)(2,1)} %copy-done.6) | copy-start | bytes 3145732
  130.8 38.7 %all-to-all-start.2 = ((f32[8,32,1024]{2,1,0:T(8,128)}), f32[8,32,1024]{2,1,0:T(8,128)S(1)}, u32[]{:S(2)}, u32[]{:S(2)}) async-start(f32[8,32,1024]{2,1,0:T(8,128)} %bitcast.42), calls=%async_computation.2 | async-start | bytes 2097152 | tf_op jit(solution)/shard_map/all_to_all | solution.py:155
  189.8 4.1 %collective-permute-start.1 = (bf16[256,1024]{1,0:T(8,128)(2,1)S(1)}, bf16[256,1024]{1,0:T(8,128)(2,1)S(1)}, u32[]{:S(2)}, u32[]{:S(2)}) collective-permute-start(bf16[256,1024]{1,0:T(8,128)(2,1)S(1)} %bitcast.25), channel_id=1, source_target_pairs={{0,32},{32,0},{64,96},{96,64},{128,160},{160,128},{192,224},{224,1... | collective-permute-start | bytes 1572872 | tf_op jit(solution)/shard_map/ppermute | solution.py:209
  195.4 4.7 %collective-permute-start.2 = (f32[256,1152]{1,0:T(8,128)S(1)}, f32[256,1152]{1,0:T(8,128)S(1)}, u32[]{:S(2)}, u32[]{:S(2)}) collective-permute-start(f32[256,1152]{1,0:T(8,128)S(1)} %get-tuple-element.18), channel_id=1, source_target_pairs={{0,32},{32,0},{64,96},{96,64},{128,160},{160,128},{192,224},{224,1... | collective-permute-start | bytes 3538952 | tf_op jit(solution)/shard_map/ppermute | solution.py:225
  200.3 57.4 %copy-start.8 = (bf16[256,512]{0,1:T(8,128)(2,1)S(1)}, bf16[256,512]{0,1:T(8,128)(2,1)}, u32[]{:S(2)}) copy-start(bf16[256,512]{0,1:T(8,128)(2,1)} %get-tuple-element.31) | copy-start | bytes 786436
  200.3 57.4 %copy-start.9 = (bf16[256,512]{0,1:T(8,128)(2,1)S(1)}, bf16[256,512]{0,1:T(8,128)(2,1)}, u32[]{:S(2)}) copy-start(bf16[256,512]{0,1:T(8,128)(2,1)} %get-tuple-element.32) | copy-start | bytes 786436
  255.2 4.0 %collective-permute-start.3 = (bf16[256,1024]{1,0:T(8,128)(2,1)S(1)}, bf16[256,1024]{1,0:T(8,128)(2,1)S(1)}, u32[]{:S(2)}, u32[]{:S(2)}) collective-permute-start(bf16[256,1024]{1,0:T(8,128)(2,1)S(1)} %bitcast.28), channel_id=1, source_target_pairs={{0,32},{32,0},{64,96},{96,64},{128,160},{160,128},{192,224},{224,1... | collective-permute-start | bytes 1572872 | tf_op jit(solution)/shard_map/ppermute | solution.py:244
  262.9 2.0 copy-start.1
  264.9 101.4 %all-to-all-start.6 = ((bf16[32,512,128]{2,1,0:T(8,128)(2,1)}), bf16[32,512,128]{2,1,0:T(8,128)(2,1)}, u32[]{:S(2)}, u32[]{:S(2)}) async-start(bf16[32,512,128]{2,1,0:T(8,128)(2,1)} %copy-done.1), calls=%async_computation.6 | async-start | bytes 8388608 | tf_op jit(solution)/shard_map/all_to_all | solution.py:255
Sparse Core Ops, SparseCore 0:
  11.2 106.9 all-gather.2

commit v2 on v1

--- a/solution.py
+++ b/solution.py
@@ -15,6 +15,7 @@
 SMEM_SPEC = pl.BlockSpec(memory_space=pltpu.SMEM)
 VMEM_SPEC = pl.BlockSpec(memory_space=pltpu.VMEM)
 ANY_SPEC = pl.BlockSpec(memory_space=pl.ANY)
+HBM_SPEC = pl.BlockSpec(memory_space=pltpu.HBM)
 
 
 def contract(a, b, dim_a, dim_b):
@@ -36,28 +37,28 @@
     )
 
 
-def encode_kernel(slots, ids, give_x, keep_x, head, tail, give, keep, tiles, sems):
-    cut = head.shape[1]
+def prepare_kernel(which, x, bias, x_g, x_k, c_g, c_k, c_t):
+    half = x_g.shape[0]
+    core = which[0]
+    for i, (part, out) in enumerate(((x_g, c_g), (x_k, c_k))):
+        rows = x[:, (1 - core) if i == 0 else core].reshape(part.shape)
+        part[...] = rows
+        centered = rows.astype(F32) - bias[...]
+        out[...] = centered.astype(BF16)
+        c_t[:, i * half : (i + 1) * half] = centered.T.astype(BF16)
+
+
+def encode_kernel(slots, ids, give_x, keep_x, blocks, give, keep, tiles, sems):
     copies = []
     for s in range(slots):
-        owner = ids[s] // 2
-        lane = pl.multiple_of((ids[s] % 2) * BLK, BLK)
-        columns = pl.ds(s * BLK, BLK)
-        one = pltpu.make_async_copy(
-            head.at[owner], tiles.at[pl.ds(0, cut), columns], sems.at[2 * s]
+        copy = pltpu.make_async_copy(
+            blocks.at[ids[s] // 2], tiles.at[:, pl.ds(s * BLK, BLK)], sems.at[s]
         )
-        two = pltpu.make_async_copy(
-            tail.at[owner, :, pl.ds(lane, BLK)],
-            tiles.at[pl.ds(cut, tail.shape[1]), columns],
-            sems.at[2 * s + 1],
-        )
-        one.start()
-        two.start()
-        copies.append((one, two))
+        copy.start()
+        copies.append(copy)
     for s in range(0, slots, 2):
-        for pair in copies[s : s + 2]:
-            for copy in pair:
-                copy.wait()
+        for copy in copies[s : s + 2]:
+            copy.wait()
         columns = slice(s * BLK, (s + 2) * BLK)
         part = tiles[:, columns]
         give[:, columns] = contract(give_x[...], part, 1, 0)
@@ -99,8 +100,9 @@
     loss[...] = total[:, latents:]
 
 
-def contribution_kernel(slots, ids, c_t, gp_g, gp_k, second, send, stage, sems):
+def contribution_kernel(slots, ids, c_t, gp_g, gp_k, second, head, tail, stage, sems):
     half = gp_g.shape[0]
+    cut = head.shape[1]
     copies = []
     for s in range(0, slots, 2):
         columns = slice(s * BLK, (s + 2) * BLK)
@@ -109,31 +111,32 @@
             + contract(c_t[:, half:], gp_k[:, columns], 1, 0)
             + second[:, columns]
         ).astype(BF16)
-        for i in range(2):
-            stage[s + i] = total[:, i * BLK : (i + 1) * BLK]
-            copy = pltpu.make_async_copy(
-                stage.at[s + i], send.at[ids[s + i] // 2], sems.at[s + i]
-            )
+        for i in range(s, s + 2):
+            part = total[:, (i - s) * BLK : (i - s + 1) * BLK]
+            tail[i] = part[cut:]
+            stage[i] = part[:cut]
+            copy = pltpu.make_async_copy(stage.at[i], head.at[ids[i] // 2], sems.at[i])
             copy.start()
             copies.append(copy)
     for copy in copies:
         copy.wait()
 
 
-def collect_kernel(owners, flags, parts, out):
-    out[...] = jnp.zeros_like(out)
-
-    def step(j, carry):
-        flag = flags[j]
-        for b in range(2):
-
-            @pl.when(flag == b)
-            def _():
-                out[:, b * BLK : (b + 1) * BLK] += parts[j].astype(F32)
-
-        return carry
-
-    lax.fori_loop(0, owners, step, 0)
+def combine_kernel(sources, places, head, tail, out, total):
+    y = pl.program_id(0)
+    cut = head.shape[2]
+    total[...] = jnp.zeros_like(total)
+    for x in range(sources):
+        place = places[x, y]
+
+        @pl.when(place >= 0)
+        def _():
+            b = place % 2
+            total[b, :cut] += head[x, 0].astype(F32)
+            total[b, cut:] += tail[x, place // 2].astype(F32)
+
+    for b in range(2):
+        out[0, :, b * BLK : (b + 1) * BLK] = total[b].astype(BF16)
 
 
 def on_device(activations, weight, enc_bias, dec_bias, block_ids, counts):
@@ -149,6 +152,11 @@
     core = lax.axis_index("dp") % 2
     same_core = [[2 * z + c for z in range(chips)] for c in range(2)]
     swap = [(q, q ^ 1) for q in range(groups)]
+    down = math.gcd(owners, 8) if owners > 8 else owners // 2
+    across = owners // down
+    same_x = [[x * down + y for y in range(down)] for x in range(across)]
+    same_y = [[x * down + y for x in range(across)] for y in range(down)]
+    my_x, my_y = myself // down, myself % down
     cut = width * 5 // 8
 
     def across_chips(array):
@@ -157,7 +165,7 @@
     def shape(dims, dtype):
         return jax.ShapeDtypeStruct(dims, dtype)
 
-    tail = lax.all_gather(weight[cut:], "latent", axis=0)
+    column = lax.all_gather(weight, "latent", axis=0, axis_index_groups=same_x)
 
     ids = block_ids[0]
     note = jnp.concatenate([ids, counts])
@@ -165,36 +173,46 @@
     notes = lax.all_to_all(
         jnp.broadcast_to(note, (owners, 8, BLK)), "latent", 0, 0, tiled=True
     )[:, 0, :]
-    all_ids = notes[:, :slots]
-    all_counts = notes[:, slots]
-    all_live = jnp.arange(slots)[None, :] < all_counts[:, None]
-    mine = all_ids // 2 == myself
-    upper = jnp.any(mine & (all_ids % 2 == 1), axis=1)
-    flags = jnp.sum(jnp.where(mine & all_live, all_ids % 2 + 1, 0), axis=1) - 1
-
-    head = jnp.where(upper[:, None, None], weight[None, :cut, BLK:], weight[None, :cut, :BLK])
-    head = lax.all_to_all(head, "latent", 0, 0, tiled=True)
+    row_notes = lax.dynamic_index_in_dim(
+        notes.reshape(across, down, BLK), my_y, 1, keepdims=False
+    )
+    row_ids = row_notes[:, :slots]
+    row_live = jnp.arange(slots)[None, :] < row_notes[:, slots : slots + 1]
+    column_owners = my_x * down + jnp.arange(down)
+    match = row_ids[:, None, :] // 2 == column_owners[None, :, None]
+    upper = jnp.any(match & (row_ids % 2 == 1)[:, None, :], axis=2)
+    code = jnp.arange(slots)[None, :] * 2 + row_ids % 2 + 1
+    places = jnp.sum(jnp.where(match & row_live[:, None, :], code[:, None, :], 0), axis=2) - 1
+
+    blocks = jnp.where(
+        upper[:, :, None, None], column[None, :, :, BLK:], column[None, :, :, :BLK]
+    )
+    blocks = lax.all_to_all(
+        blocks.reshape(owners, width, BLK), "latent", 0, 0, tiled=True, axis_index_groups=same_y
+    )
 
     live = (jnp.arange(slots) < counts[0]).astype(F32)
     live_row = jnp.repeat(live, BLK)[None, :]
     bias_row = jnp.take(enc_bias.reshape(-1, BLK), ids, axis=0).reshape(1, latents)
-    by_chunk = activations.reshape(chips, 2, share, width)
-    x_k = lax.dynamic_index_in_dim(by_chunk, core, 1, keepdims=False).reshape(half, width)
-    x_g = lax.dynamic_index_in_dim(by_chunk, 1 - core, 1, keepdims=False).reshape(half, width)
-    c_k = (x_k.astype(F32) - dec_bias).astype(BF16)
-    c_g = (x_g.astype(F32) - dec_bias).astype(BF16)
-    c_t = jnp.concatenate([c_g, c_k], axis=0).T
+    x_g, x_k, c_g, c_k, c_t = call(
+        prepare_kernel,
+        (shape((half, width), BF16),) * 4 + (shape((width, rows), BF16),),
+        [SMEM_SPEC, VMEM_SPEC, VMEM_SPEC],
+        (VMEM_SPEC,) * 5,
+        flops=rows * width * 4,
+        bytes_accessed=rows * width * 8,
+    )(core[None], activations.reshape(chips, 2, share, width), dec_bias[None, :])
 
     matmul = 2 * half * width * latents
     give, keep, tiles = call(
         functools.partial(encode_kernel, slots),
         (shape((half, latents), F32), shape((half, latents), F32), shape((width, latents), BF16)),
-        [SMEM_SPEC, VMEM_SPEC, VMEM_SPEC, ANY_SPEC, ANY_SPEC],
+        [SMEM_SPEC, VMEM_SPEC, VMEM_SPEC, ANY_SPEC],
         (VMEM_SPEC, VMEM_SPEC, VMEM_SPEC),
         flops=2 * matmul,
         bytes_accessed=4 * half * latents * 4,
-        scratch=[pltpu.SemaphoreType.DMA((2 * slots,))],
-    )(ids, c_g, c_k, head, tail)
+        scratch=[pltpu.SemaphoreType.DMA((slots,))],
+    )(ids, c_g, c_k, blocks)
 
     keep = keep + lax.ppermute(give, "dp", swap)
     parts = across_chips(keep.reshape(chips, share, latents))
@@ -243,29 +261,35 @@
     gp_k = across_chips(spread).reshape(half, latents)
     gp_g = lax.ppermute(gp_k, "dp", swap)
 
-    send = call(
+    head, tail = call(
         functools.partial(contribution_kernel, slots),
-        shape((owners, width, BLK), BF16),
+        (shape((owners, cut, BLK), BF16), shape((slots, width - cut, BLK), BF16)),
         [SMEM_SPEC] + [VMEM_SPEC] * 4,
-        ANY_SPEC,
+        (HBM_SPEC, VMEM_SPEC),
         flops=2 * matmul,
         bytes_accessed=half * latents * 16,
-        scratch=[pltpu.VMEM((slots, width, BLK), BF16), pltpu.SemaphoreType.DMA((slots,))],
+        scratch=[pltpu.VMEM((slots, cut, BLK), BF16), pltpu.SemaphoreType.DMA((slots,))],
     )(ids, c_t, gp_g, gp_k, second)
-    received = lax.all_to_all(send, "latent", 0, 0, tiled=True)
-
-    chunk = min(width, 128)
-    weight_grad = pl.pallas_call(
-        functools.partial(collect_kernel, owners),
-        grid=(width // chunk,),
-        in_specs=[SMEM_SPEC, pl.BlockSpec((owners, chunk, BLK), lambda i: (0, i, 0))],
-        out_specs=pl.BlockSpec((chunk, 2 * BLK), lambda i: (i, 0)),
-        out_shape=shape((width, 2 * BLK), F32),
+    tail = lax.all_gather(tail, "latent", axis=0, axis_index_groups=same_y)
+    head = lax.all_to_all(head, "latent", 0, 0, tiled=True, axis_index_groups=same_y)
+    sums = pl.pallas_call(
+        functools.partial(combine_kernel, across),
+        grid=(down,),
+        in_specs=[
+            SMEM_SPEC,
+            pl.BlockSpec((across, 1, cut, BLK), lambda y: (0, y, 0, 0)),
+            VMEM_SPEC,
+        ],
+        out_specs=pl.BlockSpec((1, width, 2 * BLK), lambda y: (y, 0, 0)),
+        out_shape=shape((down, width, 2 * BLK), BF16),
+        scratch_shapes=[pltpu.VMEM((2, width, BLK), F32)],
         compiler_params=pltpu.CompilerParams(vmem_limit_bytes=VMEM_LIMIT),
         cost_estimate=pl.CostEstimate(
             flops=owners * width * BLK, bytes_accessed=owners * width * BLK * 2, transcendentals=0
         ),
-    )(flags, received)
+    )(places, head.reshape(across, down, cut, BLK), tail)
+    sums = lax.all_to_all(sums, "latent", 0, 0, tiled=True, axis_index_groups=same_x)
+    weight_grad = jnp.sum(sums.astype(F32), axis=0)
     return (weight_grad, row_error)
 
 

time: 380 us -> 371 us (0.976)
  local copies, waits for them, and re-layouts: 14.4 us -> 8.14 us
    all_to_all x2 -> x3, waiting for transfers between devices: 152 us -> 139 us  [the longest x1 50.7 us: on_device(): lax.all_to_all(sums, 'latent', 0, 0, tiled=True, axis_index_groups=same_x)]
    all_gather x1 -> x2, waiting for transfers between devices: 15.9 us -> 25.5 us  [the longest x1 25.5 us: on_device(): column = lax.all_gather(weight, 'latent', axis=0, axis_index_groups=same_x)]
    pallas_call x2 -> x3, Pallas kernels: 8.89 us -> 6.09 us  [the longest x1 3.94 us: on_device(): call(functools.partial(contribution_kernel, slots), (shape((owners, cut,...]
    all_to_all x2 -> x3, starting transfers between devices: 11.3 us -> 12.6 us  [the longest x1 4.99 us: on_device(): lax.all_to_all(blocks.reshape(owners, width, BLK), 'latent', 0, 0, tiled=...]
  transfers between devices with their start and end apart: 9 -> 11, of which waited for: 9 -> 10; matrix products, arithmetic and copies ran while one was open for 3% -> 1% of each run, Pallas kernels for 0% -> 0%
where the time goes in v2:
time: 371 us; the launch traced here: 370 us
  waiting for transfers between devices  210 us (57%)
  blocking collectives  74.8 us (20%)
  starting transfers between devices  44.8 us (12%)
  between operations  15 us (4%)
  Pallas kernels  11.3 us (3%)
  local copies, waits for them, and re-layouts  8.14 us (2%)
  other arithmetic  6.21 us (2%)
    all_to_all x3, blocking collectives, across_chips(): lax.all_to_all(array, 'dp', 0, 0, tiled=True, axis_index_groups=same_core)  74.8 us
    all_to_all x1, waiting for transfers between devices, on_device(): lax.all_to_all(sums, 'latent', 0, 0, tiled=True, axis_index_groups=same_x)  50.7 us
    all_to_all x1, waiting for transfers between devices, on_device(): lax.all_to_all(blocks.reshape(owners, width, BLK), 'latent', 0, 0, tiled=...  44.3 us
    all_to_all x1, waiting for transfers between devices, on_device(): lax.all_to_all(head, 'latent', 0, 0, tiled=True, axis_index_groups=same_y)  43.8 us
    all_to_all x1, waiting for transfers between devices, across_chips(): lax.all_to_all(array, 'dp', 0, 0, tiled=True, axis_index_groups=same_core)  28.5 us
    all_gather x1, waiting for transfers between devices, on_device(): column = lax.all_gather(weight, 'latent', axis=0, axis_index_groups=same_x)  25.5 us
    all_to_all x1, starting transfers between devices, on_device(): lax.all_to_all(jnp.broadcast_to(note, (owners, 8, BLK)), 'latent', 0, 0,...  10.5 us
    ppermute x2, starting transfers between devices, on_device(): keep = keep + lax.ppermute(give, 'dp', swap)  9.39 us
  transfers between devices with their start and end apart: 11, of which 10 were waited for; matrix products, arithmetic and copies ran while one was open for 1% of the time, Pallas kernels for 0%

profile of v2, /device:TPU:1, one launch (start us, length us, event | category | flops | bytes accessed | tf_op | source)
XLA Modules:
  0.0 369.9 jit_solution(6699810154633763803)
XLA Ops:
  7.2 0.0 copy-start
  7.2 0.0 all-gather.5.cloned.1.call-start
  7.2 0.7 all-gather.5.cloned.1.call-update
  8.6 0.7 pad_add_fusion
  9.3 0.7 broadcast_in_dim.75
  10.0 10.5 %all-to-all-start = ((s32[32,8,128]{2,1,0:T(8,128)}), s32[32,8,128]{2,1,0:T(8,128)S(1)}, u32[]{:S(2)}, u32[]{:S(2)}) async-start(s32[32,8,128]{2,1,0:T(8,128)} %broadcast_in_dim.75), calls=%async_computation | async-start | bytes 262144 | tf_op jit(solution)/shard_map/all_to_all | solution.py:173
  20.5 9.1 %all-to-all-done = s32[32,8,128]{2,1,0:T(8,128)S(1)} async-done(((s32[32,8,128]{2,1,0:T(8,128)}), s32[32,8,128]{2,1,0:T(8,128)S(1)}, u32[]{:S(2)}, u32[]{:S(2)}) %all-to-all-start) | async-done | bytes 131104 | tf_op jit(solution)/shard_map/all_to_all | solution.py:173
  29.7 0.2 fusion
  29.9 0.1 broadcast_in_dim.80
  30.0 25.5 %all-gather.5.cloned.1.call-done = bf16[4096,256]{1,0:T(8,128)(2,1)} async-done(((bf16[512,256]{1,0:T(8,128)(2,1)}), bf16[4096,256]{1,0:T(8,128)(2,1)}) %all-gather.5.cloned.1.call-update) | async-done | bytes 2097168 | tf_op jit(solution)/shard_map/all_gather | solution.py:168
  55.5 1.7 fusion.3
  57.2 2.5 bitcast_select_fusion
  59.7 0.0 copy-start.5
  59.7 0.0 copy-start.6
  59.7 5.0 %all-to-all-start.1 = ((bf16[32,512,128]{2,1,0:T(8,128)(2,1)}), bf16[32,512,128]{2,1,0:T(8,128)(2,1)}, u32[]{:S(2)}, u32[]{:S(2)}) async-start(bf16[32,512,128]{2,1,0:T(8,128)(2,1)} %bitcast_select_fusion), calls=%async_computation.1 | async-start | bytes 8388608 | tf_op jit(solution)/shard_map/all_to_all | solution.py:190
  64.7 0.0 copy-done.4
  64.7 0.0 copy-done.5
  64.7 0.2 shard_map.77
  64.9 44.3 %all-to-all-done.1.blocks = bf16[32,512,128]{2,1,0:T(8,128)(2,1)} async-done(((bf16[32,512,128]{2,1,0:T(8,128)(2,1)}), bf16[32,512,128]{2,1,0:T(8,128)(2,1)}, u32[]{:S(2)}, u32[]{:S(2)}) %all-to-all-start.1) | async-done | bytes 4194336 | tf_op jit(solution)/shard_map/all_to_all | solution.py:190
  109.3 0.0 copy-done.6
  109.3 2.8 shard_map.78
  112.1 7.1 %collective-permute-start = (f32[256,1024]{1,0:T(8,128)S(1)}, f32[256,1024]{1,0:T(8,128)S(1)}, u32[]{:S(2)}, u32[]{:S(2)}) collective-permute-start(f32[256,1024]{1,0:T(8,128)S(1)} %get-tuple-element.24), channel_id=1, source_target_pairs={{0,32},{32,0},{64,96},{96,64},{128,160},{160,128},{192,224},{224,1... | collective-permute-start | bytes 3145736 | tf_op jit(solution)/shard_map/ppermute | solution.py:217
  119.2 2.3 collective-permute-done
  121.5 1.2 add.76
  122.6 7.1 %all-to-all-start.2 = ((f32[8,32,1024]{2,1,0:T(8,128)}), f32[8,32,1024]{2,1,0:T(8,128)S(1)}, u32[]{:S(2)}, u32[]{:S(2)}) async-start(f32[8,32,1024]{2,1,0:T(8,128)} %bitcast.47), calls=%async_computation.2 | async-start | bytes 2097152 | tf_op jit(solution)/shard_map/all_to_all | solution.py:163
  129.8 0.0 all-gather.7.cloned.1.call-start
  129.8 0.0 copy-done
  129.8 0.6 gather_fusion
  130.4 0.1 broadcast_select_fusion
  130.5 28.5 %all-to-all-done.2.parts = f32[8,32,1024]{2,1,0:T(8,128)S(1)} async-done(((f32[8,32,1024]{2,1,0:T(8,128)}), f32[8,32,1024]{2,1,0:T(8,128)S(1)}, u32[]{:S(2)}, u32[]{:S(2)}) %all-to-all-start.2) | async-done | bytes 1048608 | tf_op jit(solution)/shard_map/all_to_all | solution.py:163
  159.0 0.1 broadcast_in_dim.88
  159.1 0.1 shard_map.79
  159.1 20.1 %all_to_all.40 = bf16[8,32,1024]{2,1,0:T(8,128)(2,1)S(1)} all-to-all(bf16[8,32,1024]{2,1,0:T(8,128)(2,1)S(1)} %get-tuple-element.25), channel_id=1, replica_groups={{0,64,128,192,256,320,384,448},{32,96,160,224,288,352,416,480},{1,65,12..., dimensions={0} | all-to-all | bytes 1048576 | tf_op jit(solution)/shard_map/all_to_all | solution.py:163
  179.3 2.6 collective-permute-start.1
  181.9 1.5 collective-permute-done.1.act_g
  183.4 1.5 shard_map.80
  184.9 2.3 collective-permute-start.2
  187.2 2.5 collective-permute-done.2
  189.7 0.1 add.79
  189.8 34.4 %all_to_all.41.parts = f32[8,32,1152]{2,1,0:T(8,128)S(1)} all-to-all(f32[8,32,1152]{2,1,0:T(8,128)S(1)} %bitcast.46), channel_id=1, replica_groups={{0,64,128,192,256,320,384,448},{32,96,160,224,288,352,416,480},{1,65,12..., dimensions={0} | all-to-all | bytes 2359296 | tf_op jit(solution)/shard_map/all_to_all | solution.py:163
  224.2 0.1 shard_map.81
  224.3 20.3 %all_to_all.42 = bf16[8,32,1024]{2,1,0:T(8,128)(2,1)S(1)} all-to-all(bf16[8,32,1024]{2,1,0:T(8,128)(2,1)S(1)} %get-tuple-element.32), channel_id=1, replica_groups={{0,64,128,192,256,320,384,448},{32,96,160,224,288,352,416,480},{1,65,12..., dimensions={0} | all-to-all | bytes 1048576 | tf_op jit(solution)/shard_map/all_to_all | solution.py:163
  244.6 2.5 collective-permute-start.3
  247.1 0.8 shard_map.82.second
  247.8 0.7 collective-permute-done.3.gp_g
  248.6 3.9 %shard_map.83 = (bf16[32,320,128]{2,1,0:T(8,128)(2,1)S(1)}, bf16[8,192,128]{2,1,0:T(8,128)(2,1)}) custom-call(s32[8]{0:T(128)S(1)} %bitcast.45, bf16[512,512]{1,0:T(8,128)(2,1)S(1)} %get-tuple-element.20.c_t, bf16[256,1024]{1,0:T(8,128)(2,1)S(1)} %collective-permute-done.3.gp_g, bf16[256,1024]{1,0:T(8,128)(2,1)S(1)} %bitcast.35, ...), custom_call_target="tpu_custom_call" | custom-call | flops 536870912 | bytes 4194304 | tf_op jit(solution)/shard_map/pallas_call | solution.py:264
  252.5 0.0 copy-start.2
  252.5 1.5 copy-done.2
  254.0 0.0 all-gather.7.cloned.1.call-update
  254.1 3.7 all-to-all-start.6
  257.7 0.2 slice_reduce_fusion.1
  257.9 0.1 iota_compare_fusion
  258.0 0.2 select_reduce_fusion
  258.2 43.8 %all-to-all-done.6 = bf16[32,320,128]{2,1,0:T(8,128)(2,1)S(1)} async-done(((bf16[32,320,128]{2,1,0:T(8,128)(2,1)}), bf16[32,320,128]{2,1,0:T(8,128)(2,1)S(1)}, u32[]{:S(2)}, u32[]{:S(2)}) %all-to-all-start.6) | async-done | bytes 2621472 | tf_op jit(solution)/shard_map/all_to_all | solution.py:274
  302.0 0.0 all-gather.7.cloned.1.call-done
  302.0 0.0 copy-start.3
  302.0 1.4 copy-done.3
  303.4 1.9 shard_map.84
  305.4 0.0 copy-start.1
  305.4 1.3 copy-done.1
  306.7 4.0 %all-to-all-start.7 = ((bf16[8,512,256]{2,1,0:T(8,128)(2,1)}), bf16[8,512,256]{2,1,0:T(8,128)(2,1)S(1)}, u32[]{:S(2)}, u32[]{:S(2)}) async-start(bf16[8,512,256]{2,1,0:T(8,128)(2,1)} %copy-done.1), calls=%async_computation.7 | async-start | bytes 4194304 | tf_op jit(solution)/shard_map/all_to_all | solution.py:291
  310.7 0.6 slice_reduce_fusion
  311.3 50.7 %all-to-all-done.7 = bf16[8,512,256]{2,1,0:T(8,128)(2,1)S(1)} async-done(((bf16[8,512,256]{2,1,0:T(8,128)(2,1)}), bf16[8,512,256]{2,1,0:T(8,128)(2,1)S(1)}, u32[]{:S(2)}, u32[]{:S(2)}) %all-to-all-start.7) | async-done | bytes 2097184 | tf_op jit(solution)/shard_map/all_to_all | solution.py:291
  362.0 1.1 convert_reduce_fusion
  (13 shorter events, 0.1 us)
Async XLA Ops:
  7.2 122.7 %copy-start = (f32[8192]{0:T(1024)S(1)}, f32[8192]{0:T(1024)}, u32[]{:S(2)}) copy-start(f32[8192]{0:T(1024)} %param.8) | copy-start | bytes 98308
  7.2 48.3 %all-gather.5.cloned.1.call-start = ((), (), s32[]{:S(2)}) async-start(), calls=%async_computation.8 | async-start | bytes 2359296 | tf_op jit(solution)/shard_map/all_gather | solution.py:168
  10.0 19.7 %all-to-all-start = ((s32[32,8,128]{2,1,0:T(8,128)}), s32[32,8,128]{2,1,0:T(8,128)S(1)}, u32[]{:S(2)}, u32[]{:S(2)}) async-start(s32[32,8,128]{2,1,0:T(8,128)} %broadcast_in_dim.75), calls=%async_computation | async-start | bytes 262144 | tf_op jit(solution)/shard_map/all_to_all | solution.py:173
  59.7 5.0 %copy-start.4 = (bf16[512,512]{1,0:T(8,128)(2,1)S(1)}, bf16[512,512]{1,0:T(8,128)(2,1)}, u32[]{:S(2)}) copy-start(bf16[512,512]{1,0:T(8,128)(2,1)} %param.6) | copy-start | bytes 1572868
  59.7 5.0 %copy-start.5 = (f32[512]{0:T(512)S(1)}, f32[512]{0:T(512)}, u32[]{:S(2)}) copy-start(f32[512]{0:T(512)} %param.9) | copy-start | bytes 6148
  59.7 49.6 %copy-start.6 = (s32[1,8]{1,0:T(1,128)S(1)}, s32[1,8]{1,0:T(1,128)}, u32[]{:S(2)}) copy-start(s32[1,8]{1,0:T(1,128)} %param.10) | copy-start | bytes 100
  59.7 49.6 %all-to-all-start.1 = ((bf16[32,512,128]{2,1,0:T(8,128)(2,1)}), bf16[32,512,128]{2,1,0:T(8,128)(2,1)}, u32[]{:S(2)}, u32[]{:S(2)}) async-start(bf16[32,512,128]{2,1,0:T(8,128)(2,1)} %bitcast_select_fusion), calls=%async_computation.1 | async-start | bytes 8388608 | tf_op jit(solution)/shard_map/all_to_all | solution.py:190
  112.1 9.4 %collective-permute-start = (f32[256,1024]{1,0:T(8,128)S(1)}, f32[256,1024]{1,0:T(8,128)S(1)}, u32[]{:S(2)}, u32[]{:S(2)}) collective-permute-start(f32[256,1024]{1,0:T(8,128)S(1)} %get-tuple-element.24), channel_id=1, source_target_pairs={{0,32},{32,0},{64,96},{96,64},{128,160},{160,128},{192,224},{224,1... | collective-permute-start | bytes 3145736 | tf_op jit(solution)/shard_map/ppermute | solution.py:217
  122.6 36.3 %all-to-all-start.2 = ((f32[8,32,1024]{2,1,0:T(8,128)}), f32[8,32,1024]{2,1,0:T(8,128)S(1)}, u32[]{:S(2)}, u32[]{:S(2)}) async-start(f32[8,32,1024]{2,1,0:T(8,128)} %bitcast.47), calls=%async_computation.2 | async-start | bytes 2097152 | tf_op jit(solution)/shard_map/all_to_all | solution.py:163
  129.8 172.3 %all-gather.7.cloned.1.call-start = ((), (), s32[]{:S(2)}) async-start(), calls=%async_computation.9 | async-start | bytes 1966080 | tf_op jit(solution)/shard_map/all_gather | solution.py:273
  179.3 4.1 %collective-permute-start.1 = (bf16[256,1024]{1,0:T(8,128)(2,1)S(1)}, bf16[256,1024]{1,0:T(8,128)(2,1)S(1)}, u32[]{:S(2)}, u32[]{:S(2)}) collective-permute-start(bf16[256,1024]{1,0:T(8,128)(2,1)S(1)} %bitcast.31), channel_id=1, source_target_pairs={{0,32},{32,0},{64,96},{96,64},{128,160},{160,128},{192,224},{224,1... | collective-permute-start | bytes 1572872 | tf_op jit(solution)/shard_map/ppermute | solution.py:227
  184.9 4.7 %collective-permute-start.2 = (f32[256,1152]{1,0:T(8,128)S(1)}, f32[256,1152]{1,0:T(8,128)S(1)}, u32[]{:S(2)}, u32[]{:S(2)}) collective-permute-start(f32[256,1152]{1,0:T(8,128)S(1)} %get-tuple-element.30), channel_id=1, source_target_pairs={{0,32},{32,0},{64,96},{96,64},{128,160},{160,128},{192,224},{224,1... | collective-permute-start | bytes 3538952 | tf_op jit(solution)/shard_map/ppermute | solution.py:243
  244.6 4.0 %collective-permute-start.3 = (bf16[256,1024]{1,0:T(8,128)(2,1)S(1)}, bf16[256,1024]{1,0:T(8,128)(2,1)S(1)}, u32[]{:S(2)}, u32[]{:S(2)}) collective-permute-start(bf16[256,1024]{1,0:T(8,128)(2,1)S(1)} %bitcast.34), channel_id=1, source_target_pairs={{0,32},{32,0},{64,96},{96,64},{128,160},{160,128},{192,224},{224,1... | collective-permute-start | bytes 1572872 | tf_op jit(solution)/shard_map/ppermute | solution.py:262
  252.5 1.5 copy-start.2
  254.1 48.0 %all-to-all-start.6 = ((bf16[32,320,128]{2,1,0:T(8,128)(2,1)}), bf16[32,320,128]{2,1,0:T(8,128)(2,1)S(1)}, u32[]{:S(2)}, u32[]{:S(2)}) async-start(bf16[32,320,128]{2,1,0:T(8,128)(2,1)} %copy-done.2), calls=%async_computation.6 | async-start | bytes 5242880 | tf_op jit(solution)/shard_map/all_to_all | solution.py:274
  302.0 1.4 copy-start.3
  305.4 1.3 copy-start.1
  306.7 55.3 %all-to-all-start.7 = ((bf16[8,512,256]{2,1,0:T(8,128)(2,1)}), bf16[8,512,256]{2,1,0:T(8,128)(2,1)S(1)}, u32[]{:S(2)}, u32[]{:S(2)}) async-start(bf16[8,512,256]{2,1,0:T(8,128)(2,1)} %copy-done.1), calls=%async_computation.7 | async-start | bytes 4194304 | tf_op jit(solution)/shard_map/all_to_all | solution.py:291
Sparse Core Ops, SparseCore 0:
  10.1 45.3 all-gather.4
  254.2 35.7 all-gather.6

commit v3 on v2

--- a/solution.py
+++ b/solution.py
@@ -15,7 +15,6 @@
 SMEM_SPEC = pl.BlockSpec(memory_space=pltpu.SMEM)
 VMEM_SPEC = pl.BlockSpec(memory_space=pltpu.VMEM)
 ANY_SPEC = pl.BlockSpec(memory_space=pl.ANY)
-HBM_SPEC = pl.BlockSpec(memory_space=pltpu.HBM)
 
 
 def contract(a, b, dim_a, dim_b):
@@ -79,8 +78,11 @@
         loss = jnp.sum(err * err, axis=1, keepdims=True) * loss_scale
         grad = (err * scale).astype(BF16)
         out[...] = grad
-        part[:, :latents] = contract(grad, tiles[...], 1, 0)
-        part[:, latents:] = jnp.broadcast_to(loss, (loss.shape[0], BLK))
+        latent_grad = contract(grad, tiles[...], 1, 0)
+        part[:, :latents] = latent_grad
+        top = jnp.max(jnp.abs(latent_grad), axis=1, keepdims=True)
+        lane = lax.broadcasted_iota(jnp.int32, (loss.shape[0], BLK), 1)
+        part[:, latents:] = jnp.where(lane == 0, loss, top)
 
 
 def second_kernel(out_g, out_k, act_g, act_k, second):
@@ -92,18 +94,44 @@
         )
 
 
+def power_above(x):
+    return jnp.ceil(jnp.log2(jnp.maximum(x, 1e-30)))
+
+
+def pack_kernel(keep, got, out):
+    latents = out.shape[1] - BLK
+    total = keep[...] + got[...]
+    loss, top = total[:, latents : latents + 1], total[:, latents + 1 : latents + 2]
+    top = power_above(top)
+    power = power_above(loss)
+    scaled = loss * jnp.exp2(-power)
+    first = scaled.astype(BF16).astype(F32)
+    rest = (scaled - first) * 256.0
+    lane = lax.broadcasted_iota(jnp.int32, (total.shape[0], BLK), 1)
+    out[:, :latents] = total[:, :latents] * jnp.exp2(14.0 - top)
+    out[:, latents:] = jnp.where(
+        lane == 0, top, jnp.where(lane == 1, power, jnp.where(lane == 2, first, rest))
+    )
+
+
 def gate_kernel(parts, pre, live, spread, loss):
-    latents = pre.shape[1]
-    total = jnp.sum(parts[...], axis=0)
-    grad = (jnp.where(pre[...] > 0, total[:, :latents], 0.0) * live[...]).astype(BF16)
+    chips, _, width = parts.shape
+    latents = width - BLK
+    total = jnp.zeros(pre.shape, F32)
+    error = jnp.zeros(loss.shape, F32)
+    for z in range(chips):
+        extra = parts[z, :, latents:]
+        total += parts[z, :, :latents] * jnp.exp2(extra[:, :1] - 14.0)
+        row = (extra[:, 2:3] + extra[:, 3:4] * (1.0 / 256.0)) * jnp.exp2(extra[:, 1:2])
+        error += jnp.broadcast_to(row, loss.shape)
+    grad = (jnp.where(pre[...] > 0, total, 0.0) * live[...]).astype(BF16)
     spread[...] = jnp.broadcast_to(grad[None], spread.shape)
-    loss[...] = total[:, latents:]
-
-
-def contribution_kernel(slots, ids, c_t, gp_g, gp_k, second, head, tail, stage, sems):
+    loss[...] = error
+
+
+def contribution_kernel(slots, c_t, gp_g, gp_k, second, low, high):
     half = gp_g.shape[0]
-    cut = head.shape[1]
-    copies = []
+    cut = low.shape[1]
     for s in range(0, slots, 2):
         columns = slice(s * BLK, (s + 2) * BLK)
         total = (
@@ -113,27 +141,33 @@
         ).astype(BF16)
         for i in range(s, s + 2):
             part = total[:, (i - s) * BLK : (i - s + 1) * BLK]
-            tail[i] = part[cut:]
-            stage[i] = part[:cut]
-            copy = pltpu.make_async_copy(stage.at[i], head.at[ids[i] // 2], sems.at[i])
-            copy.start()
-            copies.append(copy)
-    for copy in copies:
-        copy.wait()
-
-
-def combine_kernel(sources, places, head, tail, out, total):
+            low[i] = part[:cut]
+            high[i] = part[cut:]
+
+
+def combine_kernel(places, own, after, far_a, far_b, before, out, total):
     y = pl.program_id(0)
-    cut = head.shape[2]
+    few = far_a.shape[0]
     total[...] = jnp.zeros_like(total)
-    for x in range(sources):
+    for x in range(4):
         place = places[x, y]
-
-        @pl.when(place >= 0)
-        def _():
-            b = place % 2
-            total[b, :cut] += head[x, 0].astype(F32)
-            total[b, cut:] += tail[x, place // 2].astype(F32)
+        b = place % 2
+        slot = place // 2
+        if x == 2:
+
+            @pl.when((place >= 0) & (slot < few))
+            def _():
+                total[b] += far_a[slot].astype(F32)
+
+            @pl.when(slot >= few)
+            def _():
+                total[b] += far_b[slot - few].astype(F32)
+        else:
+            source = (own, after, None, before)[x]
+
+            @pl.when(place >= 0)
+            def _():
+                total[b] += source[slot].astype(F32)
 
     for b in range(2):
         out[0, :, b * BLK : (b + 1) * BLK] = total[b].astype(BF16)
@@ -152,12 +186,14 @@
     core = lax.axis_index("dp") % 2
     same_core = [[2 * z + c for z in range(chips)] for c in range(2)]
     swap = [(q, q ^ 1) for q in range(groups)]
-    down = math.gcd(owners, 8) if owners > 8 else owners // 2
-    across = owners // down
+    across = 4
+    down = owners // across
     same_x = [[x * down + y for y in range(down)] for x in range(across)]
     same_y = [[x * down + y for x in range(across)] for y in range(down)]
     my_x, my_y = myself // down, myself % down
-    cut = width * 5 // 8
+    cut = width // 2
+    next_x = [(j, (j + down) % owners) for j in range(owners)]
+    last_x = [(j, (j - down) % owners) for j in range(owners)]
 
     def across_chips(array):
         return lax.all_to_all(array, "dp", 0, 0, tiled=True, axis_index_groups=same_core)
@@ -183,6 +219,7 @@
     upper = jnp.any(match & (row_ids % 2 == 1)[:, None, :], axis=2)
     code = jnp.arange(slots)[None, :] * 2 + row_ids % 2 + 1
     places = jnp.sum(jnp.where(match & row_live[:, None, :], code[:, None, :], 0), axis=2) - 1
+    places = jnp.roll(places, -my_x, axis=0)
 
     blocks = jnp.where(
         upper[:, :, None, None], column[None, :, :, BLK:], column[None, :, :, :BLK]
@@ -240,8 +277,14 @@
         flops=4 * matmul,
         bytes_accessed=half * latents * 14,
     )(act_g, act_k, tiles, x_g, x_k, dec_bias[None, :])
-    keep = keep + lax.ppermute(give, "dp", swap)
-    parts = across_chips(keep.reshape(chips, share, latents + BLK))
+    packed = call(
+        pack_kernel,
+        shape((half, latents + BLK), F32),
+        [VMEM_SPEC] * 2,
+        VMEM_SPEC,
+        bytes_accessed=half * latents * 12,
+    )(keep, lax.ppermute(give, "dp", swap))
+    parts = across_chips(packed.astype(jnp.float16).reshape(chips, share, latents + BLK))
     second = call(
         second_kernel,
         shape((width, latents), F32),
@@ -256,40 +299,45 @@
         [VMEM_SPEC] * 3,
         (VMEM_SPEC, VMEM_SPEC),
         bytes_accessed=half * latents * 6,
-    )(parts, pre, live_row)
+    )(parts.astype(F32), pre, live_row)
     row_error = loss[:, 0]
     gp_k = across_chips(spread).reshape(half, latents)
     gp_g = lax.ppermute(gp_k, "dp", swap)
 
-    head, tail = call(
+    halves = call(
         functools.partial(contribution_kernel, slots),
-        (shape((owners, cut, BLK), BF16), shape((slots, width - cut, BLK), BF16)),
-        [SMEM_SPEC] + [VMEM_SPEC] * 4,
-        (HBM_SPEC, VMEM_SPEC),
+        (shape((slots, cut, BLK), BF16), shape((slots, width - cut, BLK), BF16)),
+        [VMEM_SPEC] * 4,
+        (VMEM_SPEC, VMEM_SPEC),
         flops=2 * matmul,
         bytes_accessed=half * latents * 16,
-        scratch=[pltpu.VMEM((slots, cut, BLK), BF16), pltpu.SemaphoreType.DMA((slots,))],
-    )(ids, c_t, gp_g, gp_k, second)
-    tail = lax.all_gather(tail, "latent", axis=0, axis_index_groups=same_y)
-    head = lax.all_to_all(head, "latent", 0, 0, tiled=True, axis_index_groups=same_y)
-    sums = pl.pallas_call(
-        functools.partial(combine_kernel, across),
-        grid=(down,),
-        in_specs=[
-            SMEM_SPEC,
-            pl.BlockSpec((across, 1, cut, BLK), lambda y: (0, y, 0, 0)),
-            VMEM_SPEC,
-        ],
-        out_specs=pl.BlockSpec((1, width, 2 * BLK), lambda y: (y, 0, 0)),
-        out_shape=shape((down, width, 2 * BLK), BF16),
-        scratch_shapes=[pltpu.VMEM((2, width, BLK), F32)],
-        compiler_params=pltpu.CompilerParams(vmem_limit_bytes=VMEM_LIMIT),
-        cost_estimate=pl.CostEstimate(
-            flops=owners * width * BLK, bytes_accessed=owners * width * BLK * 2, transcendentals=0
-        ),
-    )(places, head.reshape(across, down, cut, BLK), tail)
-    sums = lax.all_to_all(sums, "latent", 0, 0, tiled=True, axis_index_groups=same_x)
-    weight_grad = jnp.sum(sums.astype(F32), axis=0)
+    )(c_t, gp_g, gp_k, second)
+
+    few = slots // 2
+    grads = []
+    for part in halves:
+        before = lax.ppermute(part, "latent", next_x)
+        after = lax.ppermute(part, "latent", last_x)
+        far_a = lax.ppermute(after[:few], "latent", last_x)
+        far_b = lax.ppermute(before[few:], "latent", next_x)
+        features = part.shape[1]
+        sums = pl.pallas_call(
+            combine_kernel,
+            grid=(down,),
+            in_specs=[SMEM_SPEC] + [VMEM_SPEC] * 5,
+            out_specs=pl.BlockSpec((1, features, 2 * BLK), lambda y: (y, 0, 0)),
+            out_shape=shape((down, features, 2 * BLK), BF16),
+            scratch_shapes=[pltpu.VMEM((2, features, BLK), F32)],
+            compiler_params=pltpu.CompilerParams(vmem_limit_bytes=VMEM_LIMIT),
+            cost_estimate=pl.CostEstimate(
+                flops=owners * features * BLK,
+                bytes_accessed=owners * features * BLK * 2,
+                transcendentals=0,
+            ),
+        )(places, part, after, far_a, far_b, before)
+        sums = lax.all_to_all(sums, "latent", 0, 0, tiled=True, axis_index_groups=same_x)
+        grads.append(jnp.sum(sums.astype(F32), axis=0))
+    weight_grad = jnp.concatenate(grads, axis=0)
     return (weight_grad, row_error)
 
 

time: 371 us -> 345 us (0.930)
  waiting for transfers between devices: 210 us -> 167 us
  starting transfers between devices: 44.8 us -> 71.6 us
  blocking collectives: 74.8 us -> 62.2 us
  local copies, waits for them, and re-layouts: 8.14 us -> 4 us
    all_to_all x1 -> x0, waiting for transfers between devices: 43.8 us -> none  [on_device(): lax.all_to_all(head, 'latent', 0, 0, tiled=True, axis_index_groups=same_y)]
    ppermute x0 -> x9, waiting for transfers between devices: none -> 29.8 us  [the longest x2 9.24 us: on_device(): after = lax.ppermute(part, 'latent', last_x)]
    ppermute x0 -> x9, starting transfers between devices: none -> 26.5 us  [the longest x2 8.58 us: on_device(): far_a = lax.ppermute(after[:few], 'latent', last_x)]
    all_to_all x1 -> x2, waiting for transfers between devices: 50.7 us -> 24.4 us  [on_device(): lax.all_to_all(sums, 'latent', 0, 0, tiled=True, axis_index_groups=same_x)]
    all_to_all x3, blocking collectives: 74.8 us -> 62.2 us  [across_chips(): lax.all_to_all(array, 'dp', 0, 0, tiled=True, axis_index_groups=same_core)]
    all_to_all x1 -> x2, starting transfers between devices: 3.99 us -> 10.3 us  [on_device(): lax.all_to_all(sums, 'latent', 0, 0, tiled=True, axis_index_groups=same_x)]
    unnamed x14 -> x8, local copies, waits for them, and re-layouts: 4.24 us -> 0.02 us
    pallas_call x2 -> x4, Pallas kernels: 5.85 us -> 8.39 us  [the longest x2 7.38 us: on_device(): pl.pallas_call(combine_kernel, grid=(down,), in_specs=[SMEM_SPEC] + [VMEM...]
  transfers between devices with their start and end apart: 11 -> 18, of which waited for: 10 -> 15; matrix products, arithmetic and copies ran while one was open for 1% -> 1% of each run, Pallas kernels for 0% -> 1%
where the time goes in v3:
time: 345 us; the launch traced here: 340 us
  waiting for transfers between devices  167 us (48%)
  starting transfers between devices  71.6 us (21%)
  blocking collectives  62.2 us (18%)
  between operations  15.1 us (4%)
  Pallas kernels  14.3 us (4%)
  other arithmetic  6.25 us (2%)
  local copies, waits for them, and re-layouts  4 us (1%)
    all_to_all x3, blocking collectives, across_chips(): lax.all_to_all(array, 'dp', 0, 0, tiled=True, axis_index_groups=same_core)  62.2 us
    all_to_all x1, waiting for transfers between devices, on_device(): lax.all_to_all(blocks.reshape(owners, width, BLK), 'latent', 0, 0, tiled=...  44.3 us
    all_to_all x1, waiting for transfers between devices, across_chips(): lax.all_to_all(array, 'dp', 0, 0, tiled=True, axis_index_groups=same_core)  28.6 us
    all_gather x1, waiting for transfers between devices, on_device(): column = lax.all_gather(weight, 'latent', axis=0, axis_index_groups=same_x)  25.5 us
    all_to_all x2, waiting for transfers between devices, on_device(): lax.all_to_all(sums, 'latent', 0, 0, tiled=True, axis_index_groups=same_x)  24.4 us
    all_to_all x1, starting transfers between devices, on_device(): lax.all_to_all(jnp.broadcast_to(note, (owners, 8, BLK)), 'latent', 0, 0,...  10.5 us
    all_to_all x2, starting transfers between devices, on_device(): lax.all_to_all(sums, 'latent', 0, 0, tiled=True, axis_index_groups=same_x)  10.3 us
    ppermute x2, waiting for transfers between devices, on_device(): after = lax.ppermute(part, 'latent', last_x)  9.24 us
  transfers between devices with their start and end apart: 18, of which 15 were waited for; matrix products, arithmetic and copies ran while one was open for 1% of the time, Pallas kernels for 1%

profile of v3, /device:TPU:1, one launch (start us, length us, event | category | flops | bytes accessed | tf_op | source)
XLA Modules:
  0.0 340.2 jit_solution(3056197693457550264)
XLA Ops:
  7.2 0.7 all-gather.3.cloned.1.call-update
  8.6 0.7 pad_add_fusion.1
  9.3 0.7 broadcast_in_dim.75
  10.0 10.5 %all-to-all-start = ((s32[32,8,128]{2,1,0:T(8,128)}), s32[32,8,128]{2,1,0:T(8,128)S(1)}, u32[]{:S(2)}, u32[]{:S(2)}) async-start(s32[32,8,128]{2,1,0:T(8,128)} %broadcast_in_dim.75), calls=%async_computation | async-start | bytes 262144 | tf_op jit(solution)/shard_map/all_to_all | solution.py:209
  20.5 9.1 %all-to-all-done = s32[32,8,128]{2,1,0:T(8,128)S(1)} async-done(((s32[32,8,128]{2,1,0:T(8,128)}), s32[32,8,128]{2,1,0:T(8,128)S(1)}, u32[]{:S(2)}, u32[]{:S(2)}) %all-to-all-start) | async-done | bytes 131104 | tf_op jit(solution)/shard_map/all_to_all | solution.py:209
  29.7 0.2 fusion
  29.9 0.1 broadcast_in_dim.80
  30.0 25.5 %all-gather.3.cloned.1.call-done = bf16[4096,256]{1,0:T(8,128)(2,1)} async-done(((bf16[512,256]{1,0:T(8,128)(2,1)}), bf16[4096,256]{1,0:T(8,128)(2,1)}) %all-gather.3.cloned.1.call-update) | async-done | bytes 2097168 | tf_op jit(solution)/shard_map/all_gather | solution.py:204
  55.5 1.7 fusion.3
  57.2 2.4 bitcast_select_fusion
  59.7 5.0 %all-to-all-start.1 = ((bf16[32,512,128]{2,1,0:T(8,128)(2,1)}), bf16[32,512,128]{2,1,0:T(8,128)(2,1)}, u32[]{:S(2)}, u32[]{:S(2)}) async-start(bf16[32,512,128]{2,1,0:T(8,128)(2,1)} %bitcast_select_fusion), calls=%async_computation.1 | async-start | bytes 8388608 | tf_op jit(solution)/shard_map/all_to_all | solution.py:227
  64.7 0.2 shard_map.77
  64.9 44.3 %all-to-all-done.1.blocks = bf16[32,512,128]{2,1,0:T(8,128)(2,1)} async-done(((bf16[32,512,128]{2,1,0:T(8,128)(2,1)}), bf16[32,512,128]{2,1,0:T(8,128)(2,1)}, u32[]{:S(2)}, u32[]{:S(2)}) %all-to-all-start.1) | async-done | bytes 4194336 | tf_op jit(solution)/shard_map/all_to_all | solution.py:227
  109.3 2.8 shard_map.78
  112.1 7.1 %collective-permute-start = (f32[256,1024]{1,0:T(8,128)S(1)}, f32[256,1024]{1,0:T(8,128)S(1)}, u32[]{:S(2)}, u32[]{:S(2)}) collective-permute-start(f32[256,1024]{1,0:T(8,128)S(1)} %get-tuple-element.24), channel_id=1, source_target_pairs={{0,32},{32,0},{64,96},{96,64},{128,160},{160,128},{192,224},{224,1... | collective-permute-start | bytes 3145736 | tf_op jit(solution)/shard_map/ppermute | solution.py:254
  119.2 2.3 collective-permute-done
  121.5 1.2 add.85
  122.6 7.1 %all-to-all-start.2 = ((f32[8,32,1024]{2,1,0:T(8,128)}), f32[8,32,1024]{2,1,0:T(8,128)S(1)}, u32[]{:S(2)}, u32[]{:S(2)}) async-start(f32[8,32,1024]{2,1,0:T(8,128)} %bitcast.41), calls=%async_computation.2 | async-start | bytes 2097152 | tf_op jit(solution)/shard_map/all_to_all | solution.py:199
  129.8 0.6 gather_fusion
  130.4 0.1 broadcast_select_fusion
  130.4 28.6 %all-to-all-done.2.parts = f32[8,32,1024]{2,1,0:T(8,128)S(1)} async-done(((f32[8,32,1024]{2,1,0:T(8,128)}), f32[8,32,1024]{2,1,0:T(8,128)S(1)}, u32[]{:S(2)}, u32[]{:S(2)}) %all-to-all-start.2) | async-done | bytes 1048608 | tf_op jit(solution)/shard_map/all_to_all | solution.py:199
  159.0 0.1 broadcast_in_dim.88
  159.1 0.1 shard_map.79
  159.1 20.1 %all_to_all.40 = bf16[8,32,1024]{2,1,0:T(8,128)(2,1)S(1)} all-to-all(bf16[8,32,1024]{2,1,0:T(8,128)(2,1)S(1)} %get-tuple-element.25), channel_id=1, replica_groups={{0,64,128,192,256,320,384,448},{32,96,160,224,288,352,416,480},{1,65,12..., dimensions={0} | all-to-all | bytes 1048576 | tf_op jit(solution)/shard_map/all_to_all | solution.py:199
  179.3 2.6 collective-permute-start.1
  181.9 1.5 collective-permute-done.1.act_g
  183.4 1.6 shard_map.80
  185.0 2.3 collective-permute-start.2
  187.3 2.5 collective-permute-done.2.got
  189.8 0.3 shard_map.81
  190.1 21.8 %all_to_all.41 = f16[8,32,1152]{2,1,0:T(8,128)(2,1)S(1)} all-to-all(f16[8,32,1152]{2,1,0:T(8,128)(2,1)S(1)} %bitcast.42), channel_id=1, replica_groups={{0,64,128,192,256,320,384,448},{32,96,160,224,288,352,416,480},{1,65,12..., dimensions={0} | all-to-all | bytes 1179648 | tf_op jit(solution)/shard_map/all_to_all | solution.py:199
  211.9 0.1 convert_element_type.17.parts
  212.0 0.4 shard_map.82
  212.4 20.3 %all_to_all.42 = bf16[8,32,1024]{2,1,0:T(8,128)(2,1)S(1)} all-to-all(bf16[8,32,1024]{2,1,0:T(8,128)(2,1)S(1)} %get-tuple-element.32), channel_id=1, replica_groups={{0,64,128,192,256,320,384,448},{32,96,160,224,288,352,416,480},{1,65,12..., dimensions={0} | all-to-all | bytes 1048576 | tf_op jit(solution)/shard_map/all_to_all | solution.py:199
  232.6 2.5 collective-permute-start.3
  235.1 0.8 shard_map.83.second
  235.9 0.7 collective-permute-done.3.gp_g
  236.6 0.7 shard_map.84
  237.4 2.8 collective-permute-start.4
  240.2 2.5 collective-permute-start.6
  242.7 0.2 slice_reduce_fusion.1
  242.9 0.1 iota_compare_fusion
  242.9 0.2 select_reduce_fusion
  243.2 9.2 %collective-permute-done.4.after = bf16[8,256,128]{2,1,0:T(8,128)(2,1)S(1)} collective-permute-done((bf16[8,256,128]{2,1,0:T(8,128)(2,1)S(1)}, bf16[8,256,128]{2,1,0:T(8,128)(2,1)S(1)}, u32[]{:S(2)}, u32[]{:S(2)}) %collective-permute-start.4) | collective-permute-done | bytes 524320 | tf_op jit(solution)/shard_map/ppermute | solution.py:320
  252.4 4.0 %collective-permute-start.5 = (bf16[4,256,128]{2,1,0:T(8,128)(2,1)S(1)}, bf16[4,256,128]{2,1,0:T(8,128)(2,1)S(1)}, u32[]{:S(2)}, u32[]{:S(2)}) collective-permute-start(bf16[4,256,128]{2,1,0:T(8,128)(2,1)S(1)} %slice.45), channel_id=1, source_target_pairs={{0,24},{1,25},{2,26},{3,27},{4,28},{5,29},{6,30},{7,31},{8,0},{9,1... | collective-permute-start | bytes 786440 | tf_op jit(solution)/shard_map/ppermute | solution.py:321
  256.5 1.9 collective-permute-start.7
  258.4 2.5 collective-permute-done.5.far_a
  260.9 5.0 %collective-permute-done.7.far_b = bf16[4,256,128]{2,1,0:T(8,128)(2,1)S(1)} collective-permute-done((bf16[4,256,128]{2,1,0:T(8,128)(2,1)S(1)}, bf16[4,256,128]{2,1,0:T(8,128)(2,1)S(1)}, u32[]{:S(2)}, u32[]{:S(2)}) %collective-permute-start.7) | collective-permute-done | bytes 262176 | tf_op jit(solution)/shard_map/ppermute | solution.py:322
  265.9 3.7 %shard_map.85 = bf16[8,256,256]{2,1,0:T(8,128)(2,1)} custom-call(s32[4,8]{1,0:T(4,128)S(1)} %constant_dynamic-slice_fusion.places, bf16[8,256,128]{2,1,0:T(8,128)(2,1)S(1)} %get-tuple-element.35.own, bf16[8,256,128]{2,1,0:T(8,128)(2,1)S(1)} %collective-permute-done.4.after, bf16[4,256,128]{2,1,0:T(8,128)(2,1)S(1)} %collective-permute-done.5.far_a, ...), custom_call_target="tpu_custom_call" | custom-call | flops 1048576 | bytes 2097152 | tf_op jit(solution)/shard_map/pallas_call | solution.py:324
  269.6 4.0 %all-to-all-start.6 = ((bf16[8,256,256]{2,1,0:T(8,128)(2,1)}), bf16[8,256,256]{2,1,0:T(8,128)(2,1)S(1)}, u32[]{:S(2)}, u32[]{:S(2)}) async-start(bf16[8,256,256]{2,1,0:T(8,128)(2,1)} %shard_map.85), calls=%async_computation.6 | async-start | bytes 2097152 | tf_op jit(solution)/shard_map/all_to_all | solution.py:338
  273.6 1.9 collective-permute-start.10
  275.5 4.6 %collective-permute-start.8 = (bf16[8,256,128]{2,1,0:T(8,128)(2,1)S(1)}, bf16[8,256,128]{2,1,0:T(8,128)(2,1)S(1)}, u32[]{:S(2)}, u32[]{:S(2)}) collective-permute-start(bf16[8,256,128]{2,1,0:T(8,128)(2,1)S(1)} %get-tuple-element.36.own), channel_id=1, source_target_pairs={{0,24},{1,25},{2,26},{3,27},{4,28},{5,29},{6,30},{7,31},{8,0},{9,1... | collective-permute-start | bytes 1572872 | tf_op jit(solution)/shard_map/ppermute | solution.py:320
  280.1 7.3 %collective-permute-done.10.before = bf16[8,256,128]{2,1,0:T(8,128)(2,1)S(1)} collective-permute-done((bf16[8,256,128]{2,1,0:T(8,128)(2,1)S(1)}, bf16[8,256,128]{2,1,0:T(8,128)(2,1)S(1)}, u32[]{:S(2)}, u32[]{:S(2)}) %collective-permute-start.10) | collective-permute-done | bytes 524320 | tf_op jit(solution)/shard_map/ppermute | solution.py:319
  287.4 1.9 collective-permute-start.11
  289.4 4.6 %collective-permute-start.9 = (bf16[4,256,128]{2,1,0:T(8,128)(2,1)S(1)}, bf16[4,256,128]{2,1,0:T(8,128)(2,1)S(1)}, u32[]{:S(2)}, u32[]{:S(2)}) collective-permute-start(bf16[4,256,128]{2,1,0:T(8,128)(2,1)S(1)} %slice.47), channel_id=1, source_target_pairs={{0,24},{1,25},{2,26},{3,27},{4,28},{5,29},{6,30},{7,31},{8,0},{9,1... | collective-permute-start | bytes 786440 | tf_op jit(solution)/shard_map/ppermute | solution.py:321
  294.0 1.8 collective-permute-done.11.far_b
  295.8 1.5 collective-permute-done.9.far_a
  297.3 3.7 %shard_map.86 = bf16[8,256,256]{2,1,0:T(8,128)(2,1)} custom-call(s32[4,8]{1,0:T(4,128)S(1)} %constant_dynamic-slice_fusion.places, bf16[8,256,128]{2,1,0:T(8,128)(2,1)S(1)} %get-tuple-element.36.own, bf16[8,256,128]{2,1,0:T(8,128)(2,1)S(1)} %collective-permute-done.8.after, bf16[4,256,128]{2,1,0:T(8,128)(2,1)S(1)} %collective-permute-done.9.far_a, ...), custom_call_target="tpu_custom_call" | custom-call | flops 1048576 | bytes 2097152 | tf_op jit(solution)/shard_map/pallas_call | solution.py:324
  301.0 6.3 %all-to-all-start.7 = ((bf16[8,256,256]{2,1,0:T(8,128)(2,1)}), bf16[8,256,256]{2,1,0:T(8,128)(2,1)S(1)}, u32[]{:S(2)}, u32[]{:S(2)}) async-start(bf16[8,256,256]{2,1,0:T(8,128)(2,1)} %shard_map.86), calls=%async_computation.7 | async-start | bytes 2097152 | tf_op jit(solution)/shard_map/all_to_all | solution.py:338
  307.3 0.6 slice_reduce_fusion
  307.9 0.1 convert_reduce_fusion.1
  308.1 24.3 %all-to-all-done.7 = bf16[8,256,256]{2,1,0:T(8,128)(2,1)S(1)} async-done(((bf16[8,256,256]{2,1,0:T(8,128)(2,1)}), bf16[8,256,256]{2,1,0:T(8,128)(2,1)S(1)}, u32[]{:S(2)}, u32[]{:S(2)}) %all-to-all-start.7) | async-done | bytes 1048608 | tf_op jit(solution)/shard_map/all_to_all | solution.py:338
  332.4 0.1 convert_reduce_fusion
  332.5 0.8 pad_maximum_fusion
  (31 shorter events, 0.3 us)
Async XLA Ops:
  7.2 122.6 %copy-start = (f32[8192]{0:T(1024)S(1)}, f32[8192]{0:T(1024)}, u32[]{:S(2)}) copy-start(f32[8192]{0:T(1024)} %param.8) | copy-start | bytes 98308
  7.2 48.3 %all-gather.3.cloned.1.call-start = ((), (), s32[]{:S(2)}) async-start(), calls=%async_computation.8 | async-start | bytes 2359296 | tf_op jit(solution)/shard_map/all_gather | solution.py:204
  10.0 19.7 %all-to-all-start = ((s32[32,8,128]{2,1,0:T(8,128)}), s32[32,8,128]{2,1,0:T(8,128)S(1)}, u32[]{:S(2)}, u32[]{:S(2)}) async-start(s32[32,8,128]{2,1,0:T(8,128)} %broadcast_in_dim.75), calls=%async_computation | async-start | bytes 262144 | tf_op jit(solution)/shard_map/all_to_all | solution.py:209
  59.6 5.0 %copy-start.1 = (bf16[512,512]{1,0:T(8,128)(2,1)S(1)}, bf16[512,512]{1,0:T(8,128)(2,1)}, u32[]{:S(2)}) copy-start(bf16[512,512]{1,0:T(8,128)(2,1)} %param.6) | copy-start | bytes 1572868
  59.6 5.0 %copy-start.2 = (f32[512]{0:T(512)S(1)}, f32[512]{0:T(512)}, u32[]{:S(2)}) copy-start(f32[512]{0:T(512)} %param.9) | copy-start | bytes 6148
  59.6 49.6 %copy-start.3 = (s32[1,8]{1,0:T(1,128)S(1)}, s32[1,8]{1,0:T(1,128)}, u32[]{:S(2)}) copy-start(s32[1,8]{1,0:T(1,128)} %param.10) | copy-start | bytes 100
  59.7 49.6 %all-to-all-start.1 = ((bf16[32,512,128]{2,1,0:T(8,128)(2,1)}), bf16[32,512,128]{2,1,0:T(8,128)(2,1)}, u32[]{:S(2)}, u32[]{:S(2)}) async-start(bf16[32,512,128]{2,1,0:T(8,128)(2,1)} %bitcast_select_fusion), calls=%async_computation.1 | async-start | bytes 8388608 | tf_op jit(solution)/shard_map/all_to_all | solution.py:227
  112.1 9.4 %collective-permute-start = (f32[256,1024]{1,0:T(8,128)S(1)}, f32[256,1024]{1,0:T(8,128)S(1)}, u32[]{:S(2)}, u32[]{:S(2)}) collective-permute-start(f32[256,1024]{1,0:T(8,128)S(1)} %get-tuple-element.24), channel_id=1, source_target_pairs={{0,32},{32,0},{64,96},{96,64},{128,160},{160,128},{192,224},{224,1... | collective-permute-start | bytes 3145736 | tf_op jit(solution)/shard_map/ppermute | solution.py:254
  122.6 36.3 %all-to-all-start.2 = ((f32[8,32,1024]{2,1,0:T(8,128)}), f32[8,32,1024]{2,1,0:T(8,128)S(1)}, u32[]{:S(2)}, u32[]{:S(2)}) async-start(f32[8,32,1024]{2,1,0:T(8,128)} %bitcast.41), calls=%async_computation.2 | async-start | bytes 2097152 | tf_op jit(solution)/shard_map/all_to_all | solution.py:199
  179.3 4.1 %collective-permute-start.1 = (bf16[256,1024]{1,0:T(8,128)(2,1)S(1)}, bf16[256,1024]{1,0:T(8,128)(2,1)S(1)}, u32[]{:S(2)}, u32[]{:S(2)}) collective-permute-start(bf16[256,1024]{1,0:T(8,128)(2,1)S(1)} %bitcast.28), channel_id=1, source_target_pairs={{0,32},{32,0},{64,96},{96,64},{128,160},{160,128},{192,224},{224,1... | collective-permute-start | bytes 1572872 | tf_op jit(solution)/shard_map/ppermute | solution.py:264
  185.0 4.7 %collective-permute-start.2 = (f32[256,1152]{1,0:T(8,128)S(1)}, f32[256,1152]{1,0:T(8,128)S(1)}, u32[]{:S(2)}, u32[]{:S(2)}) collective-permute-start(f32[256,1152]{1,0:T(8,128)S(1)} %get-tuple-element.30), channel_id=1, source_target_pairs={{0,32},{32,0},{64,96},{96,64},{128,160},{160,128},{192,224},{224,1... | collective-permute-start | bytes 3538952 | tf_op jit(solution)/shard_map/ppermute | solution.py:286
  232.6 4.0 %collective-permute-start.3 = (bf16[256,1024]{1,0:T(8,128)(2,1)S(1)}, bf16[256,1024]{1,0:T(8,128)(2,1)S(1)}, u32[]{:S(2)}, u32[]{:S(2)}) collective-permute-start(bf16[256,1024]{1,0:T(8,128)(2,1)S(1)} %bitcast.31), channel_id=1, source_target_pairs={{0,32},{32,0},{64,96},{96,64},{128,160},{160,128},{192,224},{224,1... | collective-permute-start | bytes 1572872 | tf_op jit(solution)/shard_map/ppermute | solution.py:305
  237.4 15.0 %collective-permute-start.4 = (bf16[8,256,128]{2,1,0:T(8,128)(2,1)S(1)}, bf16[8,256,128]{2,1,0:T(8,128)(2,1)S(1)}, u32[]{:S(2)}, u32[]{:S(2)}) collective-permute-start(bf16[8,256,128]{2,1,0:T(8,128)(2,1)S(1)} %get-tuple-element.35.own), channel_id=1, source_target_pairs={{0,24},{1,25},{2,26},{3,27},{4,28},{5,29},{6,30},{7,31},{8,0},{9,1... | collective-permute-start | bytes 1572872 | tf_op jit(solution)/shard_map/ppermute | solution.py:320
  240.2 16.3 %collective-permute-start.6 = (bf16[8,256,128]{2,1,0:T(8,128)(2,1)S(1)}, bf16[8,256,128]{2,1,0:T(8,128)(2,1)S(1)}, u32[]{:S(2)}, u32[]{:S(2)}) collective-permute-start(bf16[8,256,128]{2,1,0:T(8,128)(2,1)S(1)} %get-tuple-element.35.own), channel_id=1, source_target_pairs={{0,8},{1,9},{2,10},{3,11},{4,12},{5,13},{6,14},{7,15},{8,16},{9,17... | collective-permute-start | bytes 1572872 | tf_op jit(solution)/shard_map/ppermute | solution.py:319
  252.4 8.5 %collective-permute-start.5 = (bf16[4,256,128]{2,1,0:T(8,128)(2,1)S(1)}, bf16[4,256,128]{2,1,0:T(8,128)(2,1)S(1)}, u32[]{:S(2)}, u32[]{:S(2)}) collective-permute-start(bf16[4,256,128]{2,1,0:T(8,128)(2,1)S(1)} %slice.45), channel_id=1, source_target_pairs={{0,24},{1,25},{2,26},{3,27},{4,28},{5,29},{6,30},{7,31},{8,0},{9,1... | collective-permute-start | bytes 786440 | tf_op jit(solution)/shard_map/ppermute | solution.py:321
  256.5 9.4 %collective-permute-start.7 = (bf16[4,256,128]{2,1,0:T(8,128)(2,1)S(1)}, bf16[4,256,128]{2,1,0:T(8,128)(2,1)S(1)}, u32[]{:S(2)}, u32[]{:S(2)}) collective-permute-start(bf16[4,256,128]{2,1,0:T(8,128)(2,1)S(1)} %slice.46), channel_id=1, source_target_pairs={{0,8},{1,9},{2,10},{3,11},{4,12},{5,13},{6,14},{7,15},{8,16},{9,17... | collective-permute-start | bytes 786440 | tf_op jit(solution)/shard_map/ppermute | solution.py:322
  269.6 31.4 %all-to-all-start.6 = ((bf16[8,256,256]{2,1,0:T(8,128)(2,1)}), bf16[8,256,256]{2,1,0:T(8,128)(2,1)S(1)}, u32[]{:S(2)}, u32[]{:S(2)}) async-start(bf16[8,256,256]{2,1,0:T(8,128)(2,1)} %shard_map.85), calls=%async_computation.6 | async-start | bytes 2097152 | tf_op jit(solution)/shard_map/all_to_all | solution.py:338
  273.6 13.8 %collective-permute-start.10 = (bf16[8,256,128]{2,1,0:T(8,128)(2,1)S(1)}, bf16[8,256,128]{2,1,0:T(8,128)(2,1)S(1)}, u32[]{:S(2)}, u32[]{:S(2)}) collective-permute-start(bf16[8,256,128]{2,1,0:T(8,128)(2,1)S(1)} %get-tuple-element.36.own), channel_id=1, source_target_pairs={{0,8},{1,9},{2,10},{3,11},{4,12},{5,13},{6,14},{7,15},{8,16},{9,17... | collective-permute-start | bytes 1572872 | tf_op jit(solution)/shard_map/ppermute | solution.py:319
  275.5 13.9 %collective-permute-start.8 = (bf16[8,256,128]{2,1,0:T(8,128)(2,1)S(1)}, bf16[8,256,128]{2,1,0:T(8,128)(2,1)S(1)}, u32[]{:S(2)}, u32[]{:S(2)}) collective-permute-start(bf16[8,256,128]{2,1,0:T(8,128)(2,1)S(1)} %get-tuple-element.36.own), channel_id=1, source_target_pairs={{0,24},{1,25},{2,26},{3,27},{4,28},{5,29},{6,30},{7,31},{8,0},{9,1... | collective-permute-start | bytes 1572872 | tf_op jit(solution)/shard_map/ppermute | solution.py:320
  287.4 8.3 %collective-permute-start.11 = (bf16[4,256,128]{2,1,0:T(8,128)(2,1)S(1)}, bf16[4,256,128]{2,1,0:T(8,128)(2,1)S(1)}, u32[]{:S(2)}, u32[]{:S(2)}) collective-permute-start(bf16[4,256,128]{2,1,0:T(8,128)(2,1)S(1)} %slice.48), channel_id=1, source_target_pairs={{0,8},{1,9},{2,10},{3,11},{4,12},{5,13},{6,14},{7,15},{8,16},{9,17... | collective-permute-start | bytes 786440 | tf_op jit(solution)/shard_map/ppermute | solution.py:322
  289.4 7.9 %collective-permute-start.9 = (bf16[4,256,128]{2,1,0:T(8,128)(2,1)S(1)}, bf16[4,256,128]{2,1,0:T(8,128)(2,1)S(1)}, u32[]{:S(2)}, u32[]{:S(2)}) collective-permute-start(bf16[4,256,128]{2,1,0:T(8,128)(2,1)S(1)} %slice.47), channel_id=1, source_target_pairs={{0,24},{1,25},{2,26},{3,27},{4,28},{5,29},{6,30},{7,31},{8,0},{9,1... | collective-permute-start | bytes 786440 | tf_op jit(solution)/shard_map/ppermute | solution.py:321
  301.0 31.4 %all-to-all-start.7 = ((bf16[8,256,256]{2,1,0:T(8,128)(2,1)}), bf16[8,256,256]{2,1,0:T(8,128)(2,1)S(1)}, u32[]{:S(2)}, u32[]{:S(2)}) async-start(bf16[8,256,256]{2,1,0:T(8,128)(2,1)} %shard_map.86), calls=%async_computation.7 | async-start | bytes 2097152 | tf_op jit(solution)/shard_map/all_to_all | solution.py:338
Sparse Core Ops, SparseCore 0:
  10.1 45.3 all-gather.2

commit v4 on v3

v4 whole, which is shorter than its diff:
```python
import functools
import math

import jax
import jax.numpy as jnp
from jax import lax
from jax.experimental import pallas as pl
from jax.experimental.pallas import tpu as pltpu
from jax.sharding import PartitionSpec as P

BLK = 128
BF16 = jnp.bfloat16
F32 = jnp.float32
VMEM_LIMIT = 20 * 1024 * 1024
SMEM_SPEC = pl.BlockSpec(memory_space=pltpu.SMEM)
VMEM_SPEC = pl.BlockSpec(memory_space=pltpu.VMEM)
ANY_SPEC = pl.BlockSpec(memory_space=pl.ANY)


def contract(a, b, dim_a, dim_b):
    return lax.dot_general(a, b, (((dim_a,), (dim_b,)), ((), ())), preferred_element_type=F32)


def call(kernel, out_shape, in_specs, out_specs, flops=0, bytes_accessed=0, scratch=(), **more):
    return pl.pallas_call(
        kernel,
        out_shape=out_shape,
        in_specs=in_specs,
        out_specs=out_specs,
        scratch_shapes=list(scratch),
        compiler_params=pltpu.CompilerParams(vmem_limit_bytes=VMEM_LIMIT),
        cost_estimate=pl.CostEstimate(
            flops=flops, bytes_accessed=bytes_accessed, transcendentals=0
        ),
        **more,
    )


def prepare_kernel(which, x, bias, x_g, x_k, c_g, c_k, c_t):
    half = x_g.shape[0]
    core = which[0]
    for i, (part, out) in enumerate(((x_g, c_g), (x_k, c_k))):
        rows = x[:, (1 - core) if i == 0 else core].reshape(part.shape)
        part[...] = rows
        centered = rows.astype(F32) - bias[...]
        out[...] = centered.astype(BF16)
        c_t[:, i * half : (i + 1) * half] = centered.T.astype(BF16)


def encode_kernel(slots, ids, rows, blocks, out, tiles, raw, sems):
    side = BLK // 2
    middle = slots * side
    copies = []
    for s in range(slots):
        copy = pltpu.make_async_copy(blocks.at[ids[s] // 2], raw.at[s], sems.at[s])
        copy.start()
        copies.append(copy)
    for s in range(0, slots, 2):
        copies[s].wait()
        copies[s + 1].wait()
        one, two = raw[s], raw[s + 1]
        start = s * side
        tiles[:, start : start + BLK] = jnp.concatenate([one[:, :side], two[:, :side]], axis=1)
        tiles[:, middle + start : middle + start + BLK] = jnp.concatenate(
            [one[:, side:], two[:, side:]], axis=1
        )
    for start in range(0, 2 * middle, 2 * BLK):
        columns = slice(start, start + 2 * BLK)
        out[:, columns] = contract(rows[...], tiles[:, columns], 1, 0)


def encode_rest_kernel(rows, tiles, got, out):
    for start in range(0, out.shape[1], 2 * BLK):
        columns = slice(start, start + 2 * BLK)
        out[:, columns] = contract(rows[...], tiles[:, columns], 1, 0) + got[:, columns]


def activate_kernel(parts, bias, live, pre, spread):
    total = jnp.sum(parts[...], axis=0) + bias[...]
    pre[...] = total
    act = (jnp.maximum(total, 0.0) * live[...]).astype(BF16)
    spread[...] = jnp.broadcast_to(act[None], spread.shape)


def error_kernel(scale, loss_scale, act, tiles, x, bias, part, out):
    latents = tiles.shape[1]
    err = contract(act[...], tiles[...], 1, 1) + bias[...] - x[...].astype(F32)
    loss = jnp.sum(err * err, axis=1, keepdims=True) * loss_scale
    grad = (err * scale).astype(BF16)
    out[...] = grad
    latent_grad = contract(grad, tiles[...], 1, 0)
    part[:, :latents] = latent_grad
    top = jnp.max(jnp.abs(latent_grad), axis=1, keepdims=True)
    lane = lax.broadcasted_iota(jnp.int32, (loss.shape[0], BLK), 1)
    part[:, latents:] = jnp.where(lane == 0, loss, top)


def second_kernel(out_g, out_k, act_g, act_k, first_half, second_half):
    middle = first_half.shape[1]
    for i, second in enumerate((first_half, second_half)):
        for start in range(0, middle, 2 * BLK):
            columns = slice(i * middle + start, i * middle + start + 2 * BLK)
            second[:, start : start + 2 * BLK] = contract(
                out_k[...], act_k[:, columns], 0, 0
            ) + contract(out_g[...], act_g[:, columns], 0, 0)


def power_above(x):
    return jnp.ceil(jnp.log2(jnp.maximum(x, 1e-30)))


def pack_kernel(keep, got, out):
    middle = out.shape[1] - BLK
    extra = keep[:, 2 * middle :] + got[:, 2 * middle :]
    loss, top = extra[:, :1], power_above(extra[:, 1:2])
    power = power_above(loss)
    scaled = loss * jnp.exp2(-power)
    first = scaled.astype(BF16).astype(F32)
    rest = (scaled - first) * 256.0
    lane = lax.broadcasted_iota(jnp.int32, extra.shape, 1)
    out[:, :middle] = (keep[:, :middle] + got[:, :middle]) * jnp.exp2(14.0 - top)
    out[:, middle:] = jnp.where(
        lane == 0, top, jnp.where(lane == 1, power, jnp.where(lane == 2, first, rest))
    )


def pack_rest_kernel(keep, got, earlier, out):
    middle = out.shape[1]
    extra = keep[:, 2 * middle :] + got[:, 2 * middle :]
    top = power_above(extra[:, 1:2])
    out[...] = (keep[:, middle : 2 * middle] + got[:, middle : 2 * middle]) * jnp.exp2(14.0 - top)


def gate_kernel(start, parts, extras, pre, live, spread, loss):
    chips, _, middle = spread.shape
    shape = (pre.shape[0], middle)
    total = jnp.zeros(shape, F32)
    error = jnp.zeros(loss.shape, F32)
    for z in range(chips):
        extra = extras[z, :, middle:]
        total += parts[z, :, :middle] * jnp.exp2(extra[:, :1] - 14.0)
        row = (extra[:, 2:3] + extra[:, 3:4] * (1.0 / 256.0)) * jnp.exp2(extra[:, 1:2])
        error += jnp.broadcast_to(row, loss.shape)
    columns = slice(start, start + middle)
    grad = (jnp.where(pre[:, columns] > 0, total, 0.0) * live[:, columns]).astype(BF16)
    spread[...] = jnp.broadcast_to(grad[None], spread.shape)
    loss[...] = error


def contribution_kernel(c_t, gp_g, gp_k, second, out):
    half = gp_g.shape[0]
    for i in range(0, out.shape[0], 2):
        columns = slice(i * BLK, (i + 2) * BLK)
        total = (
            contract(c_t[:, :half], gp_g[:, columns], 1, 0)
            + contract(c_t[:, half:], gp_k[:, columns], 1, 0)
            + second[:, columns]
        ).astype(BF16)
        out[i] = total[:, :BLK]
        out[i + 1] = total[:, BLK:]


def combine_kernel(places, own, after, far_a, far_b, before, out, total):
    y = pl.program_id(0)
    few = far_a.shape[0]
    side = BLK // 2
    found = jnp.maximum(
        jnp.maximum(places[0, y], places[1, y]), jnp.maximum(places[2, y], places[3, y])
    )

    @pl.when(found < 0)
    def _():
        out[...] = jnp.zeros_like(out)

    @pl.when(found >= 0)
    def _():
        total[...] = jnp.zeros_like(total)
        lower = lax.broadcasted_iota(jnp.int32, total.shape, 1) < side

        def add(source, pair, b, odd):
            value = source[pair].astype(F32)

            @pl.when(b == odd)
            def _():
                total[...] += jnp.where(lower == (b == 0), value, 0.0)

            @pl.when(b != odd)
            def _():
                total[...] += jnp.where(lower == (b == 0), pltpu.roll(value, side, 1), 0.0)

        for x in range(4):
            place = places[x, y]
            b, slot = place % 2, place // 2
            pair, odd = slot // 2, slot % 2
            if x == 2:

                @pl.when((place >= 0) & (pair < few))
                def _():
                    add(far_a, pair, b, odd)

                @pl.when((place >= 0) & (pair >= few))
                def _():
                    add(far_b, pair - few, b, odd)
            else:
                source = (own, after, None, before)[x]

                @pl.when(place >= 0)
                def _():
                    add(source, pair, b, odd)

        out[0] = total[...].astype(BF16)


def finish_kernel(first, second, out):
    side = BLK // 2
    total = jnp.sum(second[...].astype(F32), axis=0)
    for b in range(2):
        columns = slice(b * side, (b + 1) * side)
        out[:, b * BLK : (b + 1) * BLK] = jnp.concatenate(
            [first[:, columns], total[:, columns]], axis=1
        )


def on_device(activations, weight, enc_bias, dec_bias, block_ids, counts):
    rows, width = activations.shape
    owners = lax.axis_size("latent")
    groups = lax.axis_size("dp")
    share = rows // groups
    chips = groups // 2
    half = rows // 2
    slots = block_ids.shape[1]
    latents = slots * BLK
    myself = lax.axis_index("latent")
    core = lax.axis_index("dp") % 2
    same_core = [[2 * z + c for z in range(chips)] for c in range(2)]
    swap = [(q, q ^ 1) for q in range(groups)]
    across = 4
    down = owners // across
    same_x = [[x * down + y for y in range(down)] for x in range(across)]
    same_y = [[x * down + y for x in range(across)] for y in range(down)]
    my_x, my_y = myself // down, myself % down
    next_x = [(j, (j + down) % owners) for j in range(owners)]
    last_x = [(j, (j - down) % owners) for j in range(owners)]

    def across_chips(array):
        return lax.all_to_all(array, "dp", 0, 0, tiled=True, axis_index_groups=same_core)

    def shape(dims, dtype):
        return jax.ShapeDtypeStruct(dims, dtype)

    column = lax.all_gather(weight, "latent", axis=0, axis_index_groups=same_x)

    ids = block_ids[0]
    note = jnp.concatenate([ids, counts])
    note = jnp.pad(note, (0, BLK - slots - 1))
    notes = lax.all_to_all(
        jnp.broadcast_to(note, (owners, 8, BLK)), "latent", 0, 0, tiled=True
    )[:, 0, :]
    row_notes = lax.dynamic_index_in_dim(
        notes.reshape(across, down, BLK), my_y, 1, keepdims=False
    )
    row_ids = row_notes[:, :slots]
    row_live = jnp.arange(slots)[None, :] < row_notes[:, slots : slots + 1]
    column_owners = my_x * down + jnp.arange(down)
    match = row_ids[:, None, :] // 2 == column_owners[None, :, None]
    upper = jnp.any(match & (row_ids % 2 == 1)[:, None, :], axis=2)
    code = jnp.arange(slots)[None, :] * 2 + row_ids % 2 + 1
    places = jnp.sum(jnp.where(match & row_live[:, None, :], code[:, None, :], 0), axis=2) - 1
    places = jnp.roll(places, -my_x, axis=0)

    blocks = jnp.where(
        upper[:, :, None, None], column[None, :, :, BLK:], column[None, :, :, :BLK]
    )
    blocks = lax.all_to_all(
        blocks.reshape(owners, width, BLK), "latent", 0, 0, tiled=True, axis_index_groups=same_y
    )

    live = (jnp.arange(slots) < counts[0]).astype(F32)
    live_row = jnp.tile(jnp.repeat(live, BLK // 2), 2)[None, :]
    bias_row = jnp.take(enc_bias.reshape(-1, BLK), ids, axis=0)
    bias_row = bias_row.reshape(slots, 2, BLK // 2).transpose(1, 0, 2).reshape(1, latents)
    x_g, x_k, c_g, c_k, c_t = call(
        prepare_kernel,
        (shape((half, width), BF16),) * 4 + (shape((width, rows), BF16),),
        [SMEM_SPEC, VMEM_SPEC, VMEM_SPEC],
        (VMEM_SPEC,) * 5,
        flops=rows * width * 4,
        bytes_accessed=rows * width * 8,
    )(core[None], activations.reshape(chips, 2, share, width), dec_bias[None, :])

    matmul = 2 * half * width * latents
    middle = latents // 2
    give, tiles = call(
        functools.partial(encode_kernel, slots),
        (shape((half, latents), F32), shape((width, latents), BF16)),
        [SMEM_SPEC, VMEM_SPEC, ANY_SPEC],
        (VMEM_SPEC, VMEM_SPEC),
        flops=matmul,
        bytes_accessed=4 * half * latents * 3,
        scratch=[pltpu.VMEM((slots, width, BLK), BF16), pltpu.SemaphoreType.DMA((slots,))],
    )(ids, c_g, blocks)
    keep = call(
        encode_rest_kernel,
        shape((half, latents), F32),
        [VMEM_SPEC] * 3,
        VMEM_SPEC,
        flops=matmul,
        bytes_accessed=4 * half * latents * 3,
    )(c_k, tiles, lax.ppermute(give, "dp", swap))
    parts = across_chips(keep.reshape(chips, share, latents))
    pre, spread = call(
        activate_kernel,
        (shape((share, latents), F32), shape((chips, share, latents), BF16)),
        [VMEM_SPEC] * 3,
        (VMEM_SPEC, VMEM_SPEC),
        bytes_accessed=half * latents * 6,
    )(parts, bias_row, live_row)
    act_k = across_chips(spread).reshape(half, latents)
    act_g = lax.ppermute(act_k, "dp", swap)

    scale = 2.0 / math.sqrt(rows * owners)
    give, keep = (
        call(
            functools.partial(error_kernel, scale, 1.0 / (width * groups)),
            (shape((half, latents + BLK), F32), shape((half, width), BF16)),
            [VMEM_SPEC] * 4,
            (VMEM_SPEC,) * 2,
            flops=2 * matmul,
            bytes_accessed=half * latents * 7,
        )(act, tiles, x, dec_bias[None, :])
        for act, x in ((act_g, x_g), (act_k, x_k))
    )
    (give, out_g), (keep, out_k) = give, keep
    got = lax.ppermute(give, "dp", swap)
    second = call(
        second_kernel,
        (shape((width, middle), F32),) * 2,
        [VMEM_SPEC] * 4,
        (VMEM_SPEC,) * 2,
        flops=2 * matmul,
        bytes_accessed=half * latents * 16,
    )(out_g, out_k, act_g, act_k)

    parts = []
    extras = None
    for i in range(2):
        if i == 0:
            packed = call(
                pack_kernel,
                shape((half, middle + BLK), F32),
                [VMEM_SPEC] * 2,
                VMEM_SPEC,
                bytes_accessed=half * latents * 6,
            )(keep, got)
        else:
            packed = call(
                pack_rest_kernel,
                shape((half, middle), F32),
                [VMEM_SPEC] * 2 + [ANY_SPEC],
                VMEM_SPEC,
                bytes_accessed=half * latents * 6,
            )(keep, got, gp_k)
        sums = across_chips(packed.astype(jnp.float16).reshape(chips, share, -1)).astype(F32)
        extras = sums if extras is None else extras
        spread, loss = call(
            functools.partial(gate_kernel, i * middle),
            (shape((chips, share, middle), BF16), shape((share, BLK), F32)),
            [VMEM_SPEC] * 4,
            (VMEM_SPEC, VMEM_SPEC),
            bytes_accessed=half * latents * 3,
        )(sums, extras, pre, live_row)
        if i == 0:
            row_error = loss[:, 0]
        gp_k = across_chips(spread).reshape(half, middle)
        gp_g = lax.ppermute(gp_k, "dp", swap)
        parts.append(
            call(
                contribution_kernel,
                shape((slots // 2, width, BLK), BF16),
                [VMEM_SPEC] * 4,
                VMEM_SPEC,
                flops=matmul,
                bytes_accessed=half * latents * 8,
            )(c_t, gp_g, gp_k, second[i])
        )

    few = slots // 4
    grads = []
    for part in parts:
        before = lax.ppermute(part, "latent", next_x)
        after = lax.ppermute(part, "latent", last_x)
        far_a = lax.ppermute(after[:few], "latent", last_x)
        far_b = lax.ppermute(before[few:], "latent", next_x)
        sums = pl.pallas_call(
            combine_kernel,
            grid=(down,),
            in_specs=[SMEM_SPEC] + [VMEM_SPEC] * 5,
            out_specs=pl.BlockSpec((1, width, BLK), lambda y: (y, 0, 0)),
            out_shape=shape((down, width, BLK), BF16),
            scratch_shapes=[pltpu.VMEM((width, BLK), F32)],
            compiler_params=pltpu.CompilerParams(vmem_limit_bytes=VMEM_LIMIT),
            cost_estimate=pl.CostEstimate(
                flops=owners * width * BLK // 2,
                bytes_accessed=owners * width * BLK,
                transcendentals=0,
            ),
        )(places, part, after, far_a, far_b, before)
        grads.append(lax.all_to_all(sums, "latent", 0, 0, tiled=True, axis_index_groups=same_x))
    weight_grad = call(
        finish_kernel,
        shape((width, 2 * BLK), F32),
        [VMEM_SPEC] * 2,
        VMEM_SPEC,
        bytes_accessed=width * BLK * 8 * 4,
    )(jnp.sum(grads[0].astype(F32), axis=0), grads[1])
    return (weight_grad, row_error)


def solution(mesh):
    placed = (P("latent", "dp"), P("dp", "latent"), P(), P("dp"), P("latent", None), P("latent"))
    return jax.shard_map(
        on_device,
        mesh=mesh,
        in_specs=placed,
        out_specs=(P("dp", "latent"), P(("latent", "dp"))),
        check_vma=False,
    )
```

time: 345 us -> 352 us (1.020)
  blocking collectives: 62.2 us -> 50.9 us
  starting transfers between devices: 71.6 us -> 81.6 us
  local copies, waits for them, and re-layouts: 4 us -> 9.75 us
  Pallas kernels: 14.3 us -> 18.2 us
    all_to_all x3, blocking collectives: 62.2 us -> 50.9 us  [across_chips(): lax.all_to_all(array, 'dp', 0, 0, tiled=True, axis_index_groups=same_core)]
    all_to_all x1 -> x3, starting transfers between devices: 7.11 us -> 14.6 us  [across_chips(): lax.all_to_all(array, 'dp', 0, 0, tiled=True, axis_index_groups=same_core)]
    ppermute x2, waiting for transfers between devices: 7.33 us -> 0.01 us  [on_device(): before = lax.ppermute(part, 'latent', next_x)]
    unnamed x8 -> x34, local copies, waits for them, and re-layouts: 0.02 us -> 5.53 us
    ppermute x1, starting transfers between devices: 2.28 us -> 7.11 us  [on_device(): lax.ppermute(give, 'dp', swap)]
    ppermute x1, starting transfers between devices: 7.11 us -> 2.28 us  [on_device(): got = lax.ppermute(give, 'dp', swap)]
    ppermute x1 -> x2, starting transfers between devices: 2.48 us -> 6.79 us  [on_device(): gp_g = lax.ppermute(gp_k, 'dp', swap)]
    pallas_call x4 -> x9, Pallas kernels: 2.16 us -> 5.94 us  [the longest x1 1.45 us: on_device(): call(encode_rest_kernel, shape((half, latents), F32), [VMEM_SPEC] * 3, VM...]
  transfers between devices with their start and end apart: 18 -> 21, of which waited for: 15 -> 16; matrix products, arithmetic and copies ran while one was open for 1% -> 2% of each run, Pallas kernels for 1% -> 3%
where the time goes in v4:
time: 352 us; the launch traced here: 351 us
  waiting for transfers between devices  169 us (48%)
  starting transfers between devices  81.6 us (23%)
  blocking collectives  50.9 us (14%)
  Pallas kernels  18.2 us (5%)
  between operations  15.2 us (4%)
  local copies, waits for them, and re-layouts  9.75 us (3%)
  other arithmetic  5.86 us (2%)
    all_to_all x3, blocking collectives, across_chips(): lax.all_to_all(array, 'dp', 0, 0, tiled=True, axis_index_groups=same_core)  50.9 us
    all_to_all x1, waiting for transfers between devices, on_device(): lax.all_to_all(blocks.reshape(owners, width, BLK), 'latent', 0, 0, tiled=...  43.6 us
    all_to_all x3, waiting for transfers between devices, across_chips(): lax.all_to_all(array, 'dp', 0, 0, tiled=True, axis_index_groups=same_core)  32.3 us
    all_to_all x2, waiting for transfers between devices, on_device(): lax.all_to_all(sums, 'latent', 0, 0, tiled=True, axis_index_groups=same_x)  26.8 us
    all_gather x1, waiting for transfers between devices, on_device(): column = lax.all_gather(weight, 'latent', axis=0, axis_index_groups=same_x)  25.5 us
    all_to_all x3, starting transfers between devices, across_chips(): lax.all_to_all(array, 'dp', 0, 0, tiled=True, axis_index_groups=same_core)  14.6 us
    all_to_all x2, starting transfers between devices, on_device(): lax.all_to_all(sums, 'latent', 0, 0, tiled=True, axis_index_groups=same_x)  10.9 us
    all_to_all x1, starting transfers between devices, on_device(): lax.all_to_all(jnp.broadcast_to(note, (owners, 8, BLK)), 'latent', 0, 0,...  10.5 us
  transfers between devices with their start and end apart: 21, of which 16 were waited for; matrix products, arithmetic and copies ran while one was open for 2% of the time, Pallas kernels for 3%

profile of v4, /device:TPU:1, one launch (start us, length us, event | category | flops | bytes accessed | tf_op | source)
XLA Modules:
  0.0 350.6 jit_solution(2052185301428001819)
XLA Ops:
  7.2 0.7 all-gather.3.cloned.1.call-update
  8.6 0.7 pad_add_fusion.1
  9.3 0.7 broadcast_in_dim.76
  10.0 10.5 %all-to-all-start = ((s32[32,8,128]{2,1,0:T(8,128)}), s32[32,8,128]{2,1,0:T(8,128)S(1)}, u32[]{:S(2)}, u32[]{:S(2)}) async-start(s32[32,8,128]{2,1,0:T(8,128)} %broadcast_in_dim.76), calls=%async_computation | async-start | bytes 262144 | tf_op jit(solution)/shard_map/all_to_all | solution.py:256
  20.5 9.1 %all-to-all-done = s32[32,8,128]{2,1,0:T(8,128)S(1)} async-done(((s32[32,8,128]{2,1,0:T(8,128)}), s32[32,8,128]{2,1,0:T(8,128)S(1)}, u32[]{:S(2)}, u32[]{:S(2)}) %all-to-all-start) | async-done | bytes 131104 | tf_op jit(solution)/shard_map/all_to_all | solution.py:256
  30.0 25.5 %all-gather.3.cloned.1.call-done = bf16[4096,256]{1,0:T(8,128)(2,1)} async-done(((bf16[512,256]{1,0:T(8,128)(2,1)}), bf16[4096,256]{1,0:T(8,128)(2,1)}) %all-gather.3.cloned.1.call-update) | async-done | bytes 2097168 | tf_op jit(solution)/shard_map/all_gather | solution.py:251
  55.5 1.7 fusion.4
  57.2 2.5 bitcast_select_fusion
  59.7 5.0 %all-to-all-start.1 = ((bf16[32,512,128]{2,1,0:T(8,128)(2,1)}), bf16[32,512,128]{2,1,0:T(8,128)(2,1)}, u32[]{:S(2)}, u32[]{:S(2)}) async-start(bf16[32,512,128]{2,1,0:T(8,128)(2,1)} %bitcast_select_fusion), calls=%async_computation.1 | async-start | bytes 8388608 | tf_op jit(solution)/shard_map/all_to_all | solution.py:274
  65.0 0.7 copy-done.8
  65.7 43.6 %all-to-all-done.1.blocks = bf16[32,512,128]{2,1,0:T(8,128)(2,1)} async-done(((bf16[32,512,128]{2,1,0:T(8,128)(2,1)}), bf16[32,512,128]{2,1,0:T(8,128)(2,1)}, u32[]{:S(2)}, u32[]{:S(2)}) %all-to-all-start.1) | async-done | bytes 4194336 | tf_op jit(solution)/shard_map/all_to_all | solution.py:274
  109.3 2.6 shard_map.78
  111.9 7.1 %collective-permute-start = (f32[256,1024]{1,0:T(8,128)S(1)}, f32[256,1024]{1,0:T(8,128)S(1)}, u32[]{:S(2)}, u32[]{:S(2)}) collective-permute-start(f32[256,1024]{1,0:T(8,128)S(1)} %get-tuple-element.24), channel_id=1, source_target_pairs={{0,32},{32,0},{64,96},{96,64},{128,160},{160,128},{192,224},{224,1... | collective-permute-start | bytes 3145736 | tf_op jit(solution)/shard_map/ppermute | solution.py:309
  119.0 2.3 collective-permute-done.got
  121.3 1.4 shard_map.79
  122.7 7.1 %all-to-all-start.2 = ((f32[8,32,1024]{2,1,0:T(8,128)}), f32[8,32,1024]{2,1,0:T(8,128)S(1)}, u32[]{:S(2)}, u32[]{:S(2)}) async-start(f32[8,32,1024]{2,1,0:T(8,128)} %bitcast.9), calls=%async_computation.2 | async-start | bytes 2097152 | tf_op jit(solution)/shard_map/all_to_all | solution.py:246
  130.0 0.6 gather_fusion
  130.8 28.2 %all-to-all-done.2.parts = f32[8,32,1024]{2,1,0:T(8,128)S(1)} async-done(((f32[8,32,1024]{2,1,0:T(8,128)}), f32[8,32,1024]{2,1,0:T(8,128)S(1)}, u32[]{:S(2)}, u32[]{:S(2)}) %all-to-all-start.2) | async-done | bytes 1048608 | tf_op jit(solution)/shard_map/all_to_all | solution.py:246
  159.2 20.1 %all_to_all.50 = bf16[8,32,1024]{2,1,0:T(8,128)(2,1)S(1)} all-to-all(bf16[8,32,1024]{2,1,0:T(8,128)(2,1)S(1)} %get-tuple-element.25), channel_id=1, replica_groups={{0,64,128,192,256,320,384,448},{32,96,160,224,288,352,416,480},{1,65,12..., dimensions={0} | all-to-all | bytes 1048576 | tf_op jit(solution)/shard_map/all_to_all | solution.py:246
  179.3 2.6 collective-permute-start.1
  181.9 1.5 collective-permute-done.1.act.act_g
  183.4 1.1 copy-done.11
  184.6 0.9 shard_map.82
  185.5 2.3 collective-permute-start.2
  187.8 0.9 copy-done.9
  188.8 0.9 shard_map.81
  189.7 0.5 collective-permute-done.2.got
  190.6 16.1 %all_to_all.51 = f16[8,32,640]{2,1,0:T(8,128)(2,1)S(1)} all-to-all(f16[8,32,640]{2,1,0:T(8,128)(2,1)S(1)} %bitcast.52), channel_id=1, replica_groups={{0,64,128,192,256,320,384,448},{32,96,160,224,288,352,416,480},{1,65,12..., dimensions={0} | all-to-all | bytes 655360 | tf_op jit(solution)/shard_map/all_to_all | solution.py:246
  207.1 14.6 %all_to_all.52 = bf16[8,32,512]{2,1,0:T(8,128)(2,1)S(1)} all-to-all(bf16[8,32,512]{2,1,0:T(8,128)(2,1)S(1)} %get-tuple-element.31), channel_id=1, replica_groups={{0,64,128,192,256,320,384,448},{32,96,160,224,288,352,416,480},{1,65,12..., dimensions={0} | all-to-all | bytes 524288 | tf_op jit(solution)/shard_map/all_to_all | solution.py:246
  221.8 2.6 collective-permute-start.3
  224.5 0.8 convert_element_type.22
  225.3 4.1 %all-to-all-start.7 = ((f16[8,32,512]{2,1,0:T(8,128)(2,1)}), f16[8,32,512]{2,1,0:T(8,128)(2,1)}, u32[]{:S(2)}, u32[]{:S(2)}) async-start(f16[8,32,512]{2,1,0:T(8,128)(2,1)} %bitcast.53), calls=%async_computation.7 | async-start | bytes 524288 | tf_op jit(solution)/shard_map/all_to_all | solution.py:246
  229.4 0.9 copy-done.15
  230.3 0.8 shard_map.85
  231.1 0.4 shard_map.86.own
  231.6 0.5 copy-done.1
  232.1 2.8 collective-permute-start.4
  234.9 2.5 collective-permute-start.6
  237.7 4.1 %all-to-all-done.7 = f16[8,32,512]{2,1,0:T(8,128)(2,1)} async-done(((f16[8,32,512]{2,1,0:T(8,128)(2,1)}), f16[8,32,512]{2,1,0:T(8,128)(2,1)}, u32[]{:S(2)}, u32[]{:S(2)}) %all-to-all-start.7) | async-done | bytes 262176 | tf_op jit(solution)/shard_map/all_to_all | solution.py:246
  241.7 1.0 convert_element_type.23.parts
  242.7 1.0 shard_map.89
  243.8 3.4 all-to-all-start.8
  247.6 4.0 %collective-permute-start.5 = (bf16[2,512,128]{2,1,0:T(8,128)(2,1)S(1)}, bf16[2,512,128]{2,1,0:T(8,128)(2,1)S(1)}, u32[]{:S(2)}, u32[]{:S(2)}) collective-permute-start(bf16[2,512,128]{2,1,0:T(8,128)(2,1)S(1)} %slice.45), channel_id=1, source_target_pairs={{0,24},{1,25},{2,26},{3,27},{4,28},{5,29},{6,30},{7,31},{8,0},{9,1... | collective-permute-start | bytes 786440 | tf_op jit(solution)/shard_map/ppermute | solution.py:392
  251.6 1.9 collective-permute-start.7
  253.6 2.9 collective-permute-done.5.far_a
  256.5 4.9 %collective-permute-done.7.far_b = bf16[2,512,128]{2,1,0:T(8,128)(2,1)S(1)} collective-permute-done((bf16[2,512,128]{2,1,0:T(8,128)(2,1)S(1)}, bf16[2,512,128]{2,1,0:T(8,128)(2,1)S(1)}, u32[]{:S(2)}, u32[]{:S(2)}) %collective-permute-start.7) | collective-permute-done | bytes 262176 | tf_op jit(solution)/shard_map/ppermute | solution.py:393
  261.4 3.7 %shard_map.87 = bf16[8,512,128]{2,1,0:T(8,128)(2,1)} custom-call(s32[4,8]{1,0:T(4,128)S(1)} %constant_dynamic-slice_fusion.places, bf16[4,512,128]{2,1,0:T(8,128)(2,1)S(1)} %shard_map.86.own, bf16[4,512,128]{2,1,0:T(8,128)(2,1)S(1)} %collective-permute-done.4.after, bf16[2,512,128]{2,1,0:T(8,128)(2,1)S(1)} %collective-permute-done.5.far_a, ...), custom_call_target="tpu_custom_call" | custom-call | flops 1048576 | bytes 2097152 | tf_op jit(solution)/shard_map/pallas_call | solution.py:394
  265.2 4.0 %all-to-all-start.6 = ((bf16[8,512,128]{2,1,0:T(8,128)(2,1)}), bf16[8,512,128]{2,1,0:T(8,128)(2,1)S(1)}, u32[]{:S(2)}, u32[]{:S(2)}) async-start(bf16[8,512,128]{2,1,0:T(8,128)(2,1)} %shard_map.87), calls=%async_computation.6 | async-start | bytes 2097152 | tf_op jit(solution)/shard_map/all_to_all | solution.py:408
  269.2 4.2 %collective-permute-start.8 = (bf16[256,512]{1,0:T(8,128)(2,1)S(1)}, bf16[256,512]{1,0:T(8,128)(2,1)S(1)}, u32[]{:S(2)}, u32[]{:S(2)}) collective-permute-start(bf16[256,512]{1,0:T(8,128)(2,1)S(1)} %bitcast.37), channel_id=1, source_target_pairs={{0,32},{32,0},{64,96},{96,64},{128,160},{160,128},{192,224},{224,1... | collective-permute-start | bytes 786440 | tf_op jit(solution)/shard_map/ppermute | solution.py:375
  273.3 1.1 collective-permute-done.8.gp_g
  274.5 1.2 copy-done.2
  275.7 0.4 shard_map.90.own
  276.2 1.9 collective-permute-start.9
  278.1 3.4 collective-permute-start.11
  281.5 9.7 %collective-permute-done.9.after = bf16[4,512,128]{2,1,0:T(8,128)(2,1)S(1)} collective-permute-done((bf16[4,512,128]{2,1,0:T(8,128)(2,1)S(1)}, bf16[4,512,128]{2,1,0:T(8,128)(2,1)S(1)}, u32[]{:S(2)}, u32[]{:S(2)}) %collective-permute-start.9) | collective-permute-done | bytes 524320 | tf_op jit(solution)/shard_map/ppermute | solution.py:391
  291.2 3.4 collective-permute-start.10
  294.7 1.9 collective-permute-start.12
  296.6 3.1 collective-permute-done.10.far_a
  299.7 4.7 %collective-permute-done.12.far_b = bf16[2,512,128]{2,1,0:T(8,128)(2,1)S(1)} collective-permute-done((bf16[2,512,128]{2,1,0:T(8,128)(2,1)S(1)}, bf16[2,512,128]{2,1,0:T(8,128)(2,1)S(1)}, u32[]{:S(2)}, u32[]{:S(2)}) %collective-permute-start.12) | collective-permute-done | bytes 262176 | tf_op jit(solution)/shard_map/ppermute | solution.py:393
  304.4 3.7 %shard_map.91 = bf16[8,512,128]{2,1,0:T(8,128)(2,1)} custom-call(s32[4,8]{1,0:T(4,128)S(1)} %constant_dynamic-slice_fusion.places, bf16[4,512,128]{2,1,0:T(8,128)(2,1)S(1)} %shard_map.90.own, bf16[4,512,128]{2,1,0:T(8,128)(2,1)S(1)} %collective-permute-done.9.after, bf16[2,512,128]{2,1,0:T(8,128)(2,1)S(1)} %collective-permute-done.10.far_a, ...), custom_call_target="tpu_custom_call" | custom-call | flops 1048576 | bytes 2097152 | tf_op jit(solution)/shard_map/pallas_call | solution.py:394
  308.2 6.9 %all-to-all-start.9 = ((bf16[8,512,128]{2,1,0:T(8,128)(2,1)}), bf16[8,512,128]{2,1,0:T(8,128)(2,1)S(1)}, u32[]{:S(2)}, u32[]{:S(2)}) async-start(bf16[8,512,128]{2,1,0:T(8,128)(2,1)} %shard_map.91), calls=%async_computation.9 | async-start | bytes 2097152 | tf_op jit(solution)/shard_map/all_to_all | solution.py:408
  315.1 0.6 slice_reduce_fusion
  315.8 26.8 %all-to-all-done.9.second = bf16[8,512,128]{2,1,0:T(8,128)(2,1)S(1)} async-done(((bf16[8,512,128]{2,1,0:T(8,128)(2,1)}), bf16[8,512,128]{2,1,0:T(8,128)(2,1)S(1)}, u32[]{:S(2)}, u32[]{:S(2)}) %all-to-all-start.9) | async-done | bytes 1048608 | tf_op jit(solution)/shard_map/all_to_all | solution.py:408
  342.7 1.1 shard_map.92
  (71 shorter events, 2.8 us)
Async XLA Ops:
  7.2 122.9 %copy-start = (f32[8192]{0:T(1024)S(1)}, f32[8192]{0:T(1024)}, u32[]{:S(2)}) copy-start(f32[8192]{0:T(1024)} %param.8) | copy-start | bytes 98308
  7.2 48.3 %all-gather.3.cloned.1.call-start = ((), (), s32[]{:S(2)}) async-start(), calls=%async_computation.10 | async-start | bytes 2359296 | tf_op jit(solution)/shard_map/all_gather | solution.py:251
  10.0 19.7 %all-to-all-start = ((s32[32,8,128]{2,1,0:T(8,128)}), s32[32,8,128]{2,1,0:T(8,128)S(1)}, u32[]{:S(2)}, u32[]{:S(2)}) async-start(s32[32,8,128]{2,1,0:T(8,128)} %broadcast_in_dim.76), calls=%async_computation | async-start | bytes 262144 | tf_op jit(solution)/shard_map/all_to_all | solution.py:256
  59.7 5.0 %copy-start.3 = (bf16[512,512]{1,0:T(8,128)(2,1)S(1)}, bf16[512,512]{1,0:T(8,128)(2,1)}, u32[]{:S(2)}) copy-start(bf16[512,512]{1,0:T(8,128)(2,1)} %param.6) | copy-start | bytes 1572868
  59.7 5.0 %copy-start.4 = (f32[512]{0:T(512)S(1)}, f32[512]{0:T(512)}, u32[]{:S(2)}) copy-start(f32[512]{0:T(512)} %param.9) | copy-start | bytes 6148
  59.7 49.6 %copy-start.5 = (s32[1,8]{1,0:T(1,128)S(1)}, s32[1,8]{1,0:T(1,128)}, u32[]{:S(2)}) copy-start(s32[1,8]{1,0:T(1,128)} %param.10) | copy-start | bytes 100
  59.7 49.6 %all-to-all-start.1 = ((bf16[32,512,128]{2,1,0:T(8,128)(2,1)}), bf16[32,512,128]{2,1,0:T(8,128)(2,1)}, u32[]{:S(2)}, u32[]{:S(2)}) async-start(bf16[32,512,128]{2,1,0:T(8,128)(2,1)} %bitcast_select_fusion), calls=%async_computation.1 | async-start | bytes 8388608 | tf_op jit(solution)/shard_map/all_to_all | solution.py:274
  65.0 0.7 copy-start.8
  65.7 46.2 %copy-start.10 = (bf16[256,512]{1,0:T(8,128)(2,1)}, bf16[256,512]{1,0:T(8,128)(2,1)S(1)}, u32[]{:S(2)}) copy-start(bf16[256,512]{1,0:T(8,128)(2,1)S(1)} %get-tuple-element.28.x) | copy-start | bytes 786436
  111.9 9.4 %collective-permute-start = (f32[256,1024]{1,0:T(8,128)S(1)}, f32[256,1024]{1,0:T(8,128)S(1)}, u32[]{:S(2)}, u32[]{:S(2)}) collective-permute-start(f32[256,1024]{1,0:T(8,128)S(1)} %get-tuple-element.24), channel_id=1, source_target_pairs={{0,32},{32,0},{64,96},{96,64},{128,160},{160,128},{192,224},{224,1... | collective-permute-start | bytes 3145736 | tf_op jit(solution)/shard_map/ppermute | solution.py:309
  122.7 36.3 %all-to-all-start.2 = ((f32[8,32,1024]{2,1,0:T(8,128)}), f32[8,32,1024]{2,1,0:T(8,128)S(1)}, u32[]{:S(2)}, u32[]{:S(2)}) async-start(f32[8,32,1024]{2,1,0:T(8,128)} %bitcast.9), calls=%async_computation.2 | async-start | bytes 2097152 | tf_op jit(solution)/shard_map/all_to_all | solution.py:246
  179.3 4.1 %collective-permute-start.1 = (bf16[256,1024]{1,0:T(8,128)(2,1)S(1)}, bf16[256,1024]{1,0:T(8,128)(2,1)S(1)}, u32[]{:S(2)}, u32[]{:S(2)}) collective-permute-start(bf16[256,1024]{1,0:T(8,128)(2,1)S(1)} %bitcast.40), channel_id=1, source_target_pairs={{0,32},{32,0},{64,96},{96,64},{128,160},{160,128},{192,224},{224,1... | collective-permute-start | bytes 1572872 | tf_op jit(solution)/shard_map/ppermute | solution.py:319
  183.4 6.8 %copy-start.6 = (bf16[256,1024]{1,0:T(8,128)(2,1)}, bf16[256,1024]{1,0:T(8,128)(2,1)S(1)}, u32[]{:S(2)}) copy-start(bf16[256,1024]{1,0:T(8,128)(2,1)S(1)} %collective-permute-done.1.act.act_g) | copy-start | bytes 1572868
  183.4 1.1 copy-start.11
  185.5 5.0 %copy-start.12 = (bf16[256,512]{1,0:T(8,128)(2,1)}, bf16[256,512]{1,0:T(8,128)(2,1)S(1)}, u32[]{:S(2)}) copy-start(bf16[256,512]{1,0:T(8,128)(2,1)S(1)} %get-tuple-element.32.out_g) | copy-start | bytes 786436
  185.5 4.7 %collective-permute-start.2 = (f32[256,1152]{1,0:T(8,128)S(1)}, f32[256,1152]{1,0:T(8,128)S(1)}, u32[]{:S(2)}, u32[]{:S(2)}) collective-permute-start(f32[256,1152]{1,0:T(8,128)S(1)} %get-tuple-element.29), channel_id=1, source_target_pairs={{0,32},{32,0},{64,96},{96,64},{128,160},{160,128},{192,224},{224,1... | collective-permute-start | bytes 3538952 | tf_op jit(solution)/shard_map/ppermute | solution.py:334
  187.8 1.0 copy-start.9
  189.7 17.0 %copy-start.14 = (bf16[256,512]{1,0:T(8,128)(2,1)}, bf16[256,512]{1,0:T(8,128)(2,1)S(1)}, u32[]{:S(2)}) copy-start(bf16[256,512]{1,0:T(8,128)(2,1)S(1)} %get-tuple-element.33.out_k) | copy-start | bytes 786436
  221.8 7.6 %copy-start.7 = (bf16[256,1024]{1,0:T(8,128)(2,1)S(1)}, bf16[256,1024]{1,0:T(8,128)(2,1)}, u32[]{:S(2)}) copy-start(bf16[256,1024]{1,0:T(8,128)(2,1)} %copy-done.6) | copy-start | bytes 1572868
  221.8 7.6 %copy-start.13 = (bf16[256,512]{1,0:T(8,128)(2,1)S(1)}, bf16[256,512]{1,0:T(8,128)(2,1)}, u32[]{:S(2)}) copy-start(bf16[256,512]{1,0:T(8,128)(2,1)} %copy-done.12) | copy-start | bytes 786436
  221.8 9.3 %collective-permute-start.3 = (bf16[256,512]{1,0:T(8,128)(2,1)S(1)}, bf16[256,512]{1,0:T(8,128)(2,1)S(1)}, u32[]{:S(2)}, u32[]{:S(2)}) collective-permute-start(bf16[256,512]{1,0:T(8,128)(2,1)S(1)} %bitcast.34), channel_id=1, source_target_pairs={{0,32},{32,0},{64,96},{96,64},{128,160},{160,128},{192,224},{224,1... | collective-permute-start | bytes 786440 | tf_op jit(solution)/shard_map/ppermute | solution.py:375
  225.3 16.4 %all-to-all-start.7 = ((f16[8,32,512]{2,1,0:T(8,128)(2,1)}), f16[8,32,512]{2,1,0:T(8,128)(2,1)}, u32[]{:S(2)}, u32[]{:S(2)}) async-start(f16[8,32,512]{2,1,0:T(8,128)(2,1)} %bitcast.53), calls=%async_computation.7 | async-start | bytes 524288 | tf_op jit(solution)/shard_map/all_to_all | solution.py:246
  229.4 1.0 copy-start.15
  231.1 1.0 copy-start.1
  232.1 15.4 %collective-permute-start.4 = (bf16[4,512,128]{2,1,0:T(8,128)(2,1)S(1)}, bf16[4,512,128]{2,1,0:T(8,128)(2,1)S(1)}, u32[]{:S(2)}, u32[]{:S(2)}) collective-permute-start(bf16[4,512,128]{2,1,0:T(8,128)(2,1)S(1)} %shard_map.86.own), channel_id=1, source_target_pairs={{0,24},{1,25},{2,26},{3,27},{4,28},{5,29},{6,30},{7,31},{8,0},{9,1... | collective-permute-start | bytes 1572872 | tf_op jit(solution)/shard_map/ppermute | solution.py:391
  234.9 16.7 %collective-permute-start.6 = (bf16[4,512,128]{2,1,0:T(8,128)(2,1)S(1)}, bf16[4,512,128]{2,1,0:T(8,128)(2,1)S(1)}, u32[]{:S(2)}, u32[]{:S(2)}) collective-permute-start(bf16[4,512,128]{2,1,0:T(8,128)(2,1)S(1)} %shard_map.86.own), channel_id=1, source_target_pairs={{0,8},{1,9},{2,10},{3,11},{4,12},{5,13},{6,14},{7,15},{8,16},{9,17... | collective-permute-start | bytes 1572872 | tf_op jit(solution)/shard_map/ppermute | solution.py:390
  243.8 21.4 %all-to-all-start.8 = ((bf16[8,32,512]{2,1,0:T(8,128)(2,1)}), bf16[8,32,512]{2,1,0:T(8,128)(2,1)S(1)}, u32[]{:S(2)}, u32[]{:S(2)}) async-start(bf16[8,32,512]{2,1,0:T(8,128)(2,1)} %get-tuple-element.35), calls=%async_computation.8 | async-start | bytes 524288 | tf_op jit(solution)/shard_map/all_to_all | solution.py:246
  247.6 8.9 %collective-permute-start.5 = (bf16[2,512,128]{2,1,0:T(8,128)(2,1)S(1)}, bf16[2,512,128]{2,1,0:T(8,128)(2,1)S(1)}, u32[]{:S(2)}, u32[]{:S(2)}) collective-permute-start(bf16[2,512,128]{2,1,0:T(8,128)(2,1)S(1)} %slice.45), channel_id=1, source_target_pairs={{0,24},{1,25},{2,26},{3,27},{4,28},{5,29},{6,30},{7,31},{8,0},{9,1... | collective-permute-start | bytes 786440 | tf_op jit(solution)/shard_map/ppermute | solution.py:392
  251.6 9.8 %collective-permute-start.7 = (bf16[2,512,128]{2,1,0:T(8,128)(2,1)S(1)}, bf16[2,512,128]{2,1,0:T(8,128)(2,1)S(1)}, u32[]{:S(2)}, u32[]{:S(2)}) collective-permute-start(bf16[2,512,128]{2,1,0:T(8,128)(2,1)S(1)} %slice.46), channel_id=1, source_target_pairs={{0,8},{1,9},{2,10},{3,11},{4,12},{5,13},{6,14},{7,15},{8,16},{9,17... | collective-permute-start | bytes 786440 | tf_op jit(solution)/shard_map/ppermute | solution.py:393
  265.2 43.0 %all-to-all-start.6 = ((bf16[8,512,128]{2,1,0:T(8,128)(2,1)}), bf16[8,512,128]{2,1,0:T(8,128)(2,1)S(1)}, u32[]{:S(2)}, u32[]{:S(2)}) async-start(bf16[8,512,128]{2,1,0:T(8,128)(2,1)} %shard_map.87), calls=%async_computation.6 | async-start | bytes 2097152 | tf_op jit(solution)/shard_map/all_to_all | solution.py:408
  269.2 5.3 %collective-permute-start.8 = (bf16[256,512]{1,0:T(8,128)(2,1)S(1)}, bf16[256,512]{1,0:T(8,128)(2,1)S(1)}, u32[]{:S(2)}, u32[]{:S(2)}) collective-permute-start(bf16[256,512]{1,0:T(8,128)(2,1)S(1)} %bitcast.37), channel_id=1, source_target_pairs={{0,32},{32,0},{64,96},{96,64},{128,160},{160,128},{192,224},{224,1... | collective-permute-start | bytes 786440 | tf_op jit(solution)/shard_map/ppermute | solution.py:375
  274.5 1.2 copy-start.2
  276.2 15.0 %collective-permute-start.9 = (bf16[4,512,128]{2,1,0:T(8,128)(2,1)S(1)}, bf16[4,512,128]{2,1,0:T(8,128)(2,1)S(1)}, u32[]{:S(2)}, u32[]{:S(2)}) collective-permute-start(bf16[4,512,128]{2,1,0:T(8,128)(2,1)S(1)} %shard_map.90.own), channel_id=1, source_target_pairs={{0,24},{1,25},{2,26},{3,27},{4,28},{5,29},{6,30},{7,31},{8,0},{9,1... | collective-permute-start | bytes 1572872 | tf_op jit(solution)/shard_map/ppermute | solution.py:391
  278.1 16.6 %collective-permute-start.11 = (bf16[4,512,128]{2,1,0:T(8,128)(2,1)S(1)}, bf16[4,512,128]{2,1,0:T(8,128)(2,1)S(1)}, u32[]{:S(2)}, u32[]{:S(2)}) collective-permute-start(bf16[4,512,128]{2,1,0:T(8,128)(2,1)S(1)} %shard_map.90.own), channel_id=1, source_target_pairs={{0,8},{1,9},{2,10},{3,11},{4,12},{5,13},{6,14},{7,15},{8,16},{9,17... | collective-permute-start | bytes 1572872 | tf_op jit(solution)/shard_map/ppermute | solution.py:390
  291.2 8.5 %collective-permute-start.10 = (bf16[2,512,128]{2,1,0:T(8,128)(2,1)S(1)}, bf16[2,512,128]{2,1,0:T(8,128)(2,1)S(1)}, u32[]{:S(2)}, u32[]{:S(2)}) collective-permute-start(bf16[2,512,128]{2,1,0:T(8,128)(2,1)S(1)} %slice.47), channel_id=1, source_target_pairs={{0,24},{1,25},{2,26},{3,27},{4,28},{5,29},{6,30},{7,31},{8,0},{9,1... | collective-permute-start | bytes 786440 | tf_op jit(solution)/shard_map/ppermute | solution.py:392
  294.7 9.7 %collective-permute-start.12 = (bf16[2,512,128]{2,1,0:T(8,128)(2,1)S(1)}, bf16[2,512,128]{2,1,0:T(8,128)(2,1)S(1)}, u32[]{:S(2)}, u32[]{:S(2)}) collective-permute-start(bf16[2,512,128]{2,1,0:T(8,128)(2,1)S(1)} %slice.48), channel_id=1, source_target_pairs={{0,8},{1,9},{2,10},{3,11},{4,12},{5,13},{6,14},{7,15},{8,16},{9,17... | collective-permute-start | bytes 786440 | tf_op jit(solution)/shard_map/ppermute | solution.py:393
  308.2 34.5 %all-to-all-start.9 = ((bf16[8,512,128]{2,1,0:T(8,128)(2,1)}), bf16[8,512,128]{2,1,0:T(8,128)(2,1)S(1)}, u32[]{:S(2)}, u32[]{:S(2)}) async-start(bf16[8,512,128]{2,1,0:T(8,128)(2,1)} %shard_map.91), calls=%async_computation.9 | async-start | bytes 2097152 | tf_op jit(solution)/shard_map/all_to_all | solution.py:408
Sparse Core Ops, SparseCore 0:
  10.1 45.3 all-gather.2

commit v5 on v3

--- a/solution.py
+++ b/solution.py
@@ -11,7 +11,7 @@
 BLK = 128
 BF16 = jnp.bfloat16
 F32 = jnp.float32
-VMEM_LIMIT = 40 * 1024 * 1024
+VMEM_LIMIT = 20 * 1024 * 1024
 SMEM_SPEC = pl.BlockSpec(memory_space=pltpu.SMEM)
 VMEM_SPEC = pl.BlockSpec(memory_space=pltpu.VMEM)
 ANY_SPEC = pl.BlockSpec(memory_space=pl.ANY)
@@ -47,7 +47,7 @@
         c_t[:, i * half : (i + 1) * half] = centered.T.astype(BF16)
 
 
-def encode_kernel(slots, ids, give_x, keep_x, blocks, give, keep, tiles, sems):
+def fetch_kernel(slots, ids, blocks, tiles, sems):
     copies = []
     for s in range(slots):
         copy = pltpu.make_async_copy(
@@ -55,13 +55,20 @@
         )
         copy.start()
         copies.append(copy)
-    for s in range(0, slots, 2):
-        for copy in copies[s : s + 2]:
-            copy.wait()
-        columns = slice(s * BLK, (s + 2) * BLK)
-        part = tiles[:, columns]
-        give[:, columns] = contract(give_x[...], part, 1, 0)
-        keep[:, columns] = contract(keep_x[...], part, 1, 0)
+    for copy in copies:
+        copy.wait()
+
+
+def encode_kernel(rows, tiles, out):
+    for start in range(0, out.shape[1], 2 * BLK):
+        columns = slice(start, start + 2 * BLK)
+        out[:, columns] = contract(rows[...], tiles[:, columns], 1, 0)
+
+
+def encode_rest_kernel(rows, tiles, part, out):
+    for start in range(0, out.shape[1], 2 * BLK):
+        columns = slice(start, start + 2 * BLK)
+        out[:, columns] = contract(rows[...], tiles[:, columns], 1, 0) + part[:, columns]
 
 
 def activate_kernel(parts, bias, live, pre, spread):
@@ -71,18 +78,31 @@
     spread[...] = jnp.broadcast_to(act[None], spread.shape)
 
 
-def error_kernel(scale, loss_scale, act_g, act_k, tiles, x_g, x_k, bias, give, keep, out_g, out_k):
+def power_above(x):
+    return jnp.ceil(jnp.log2(jnp.maximum(x, 1e-30)))
+
+
+def error_kernel(scale, loss_scale, act, tiles, tiles_o, x, x_o, bias, bias_o, out, grad_out, grad_out_o):
     latents = tiles.shape[1]
-    for act, x, part, out in ((act_g, x_g, give, out_g), (act_k, x_k, keep, out_k)):
-        err = contract(act[...], tiles[...], 1, 1) + bias[...] - x[...].astype(F32)
-        loss = jnp.sum(err * err, axis=1, keepdims=True) * loss_scale
+    loss = 0.0
+    grads = []
+    for w, rows, b, g in ((tiles, x, bias, grad_out), (tiles_o, x_o, bias_o, grad_out_o)):
+        err = contract(act[...], w[...], 1, 1) + b[...] - rows[...].astype(F32)
+        loss += jnp.sum(err * err, axis=1, keepdims=True) * loss_scale
         grad = (err * scale).astype(BF16)
-        out[...] = grad
-        latent_grad = contract(grad, tiles[...], 1, 0)
-        part[:, :latents] = latent_grad
-        top = jnp.max(jnp.abs(latent_grad), axis=1, keepdims=True)
-        lane = lax.broadcasted_iota(jnp.int32, (loss.shape[0], BLK), 1)
-        part[:, latents:] = jnp.where(lane == 0, loss, top)
+        g[...] = grad
+        grads.append(grad)
+    total = contract(grads[0], tiles[...], 1, 0) + contract(grads[1], tiles_o[...], 1, 0)
+    top = power_above(jnp.max(jnp.abs(total), axis=1, keepdims=True))
+    power = power_above(loss)
+    scaled = loss * jnp.exp2(-power)
+    first = scaled.astype(BF16).astype(F32)
+    rest = (scaled - first) * 256.0
+    lane = lax.broadcasted_iota(jnp.int32, (total.shape[0], BLK), 1)
+    out[:, :latents] = total * jnp.exp2(14.0 - top)
+    out[:, latents:] = jnp.where(
+        lane == 0, top, jnp.where(lane == 1, power, jnp.where(lane == 2, first, rest))
+    )
 
 
 def second_kernel(out_g, out_k, act_g, act_k, second):
@@ -92,26 +112,6 @@
         second[:, columns] = contract(out_k[...], act_k[:, columns], 0, 0) + contract(
             out_g[...], act_g[:, columns], 0, 0
         )
-
-
-def power_above(x):
-    return jnp.ceil(jnp.log2(jnp.maximum(x, 1e-30)))
-
-
-def pack_kernel(keep, got, out):
-    latents = out.shape[1] - BLK
-    total = keep[...] + got[...]
-    loss, top = total[:, latents : latents + 1], total[:, latents + 1 : latents + 2]
-    top = power_above(top)
-    power = power_above(loss)
-    scaled = loss * jnp.exp2(-power)
-    first = scaled.astype(BF16).astype(F32)
-    rest = (scaled - first) * 256.0
-    lane = lax.broadcasted_iota(jnp.int32, (total.shape[0], BLK), 1)
-    out[:, :latents] = total[:, :latents] * jnp.exp2(14.0 - top)
-    out[:, latents:] = jnp.where(
-        lane == 0, top, jnp.where(lane == 1, power, jnp.where(lane == 2, first, rest))
-    )
 
 
 def gate_kernel(parts, pre, live, spread, loss):
@@ -145,32 +145,27 @@
             high[i] = part[cut:]
 
 
-def combine_kernel(places, own, after, far_a, far_b, before, out, total):
+def combine_kernel(places, own, after, far_a, far_b, before, out):
     y = pl.program_id(0)
     few = far_a.shape[0]
-    total[...] = jnp.zeros_like(total)
-    for x in range(4):
-        place = places[x, y]
-        b = place % 2
-        slot = place // 2
-        if x == 2:
-
-            @pl.when((place >= 0) & (slot < few))
-            def _():
-                total[b] += far_a[slot].astype(F32)
-
-            @pl.when(slot >= few)
-            def _():
-                total[b] += far_b[slot - few].astype(F32)
-        else:
-            source = (own, after, None, before)[x]
-
-            @pl.when(place >= 0)
-            def _():
-                total[b] += source[slot].astype(F32)
-
-    for b in range(2):
-        out[0, :, b * BLK : (b + 1) * BLK] = total[b].astype(BF16)
+    features = own.shape[1]
+    chunk = min(features, 64)
+    place = [places[x, y] for x in range(4)]
+    slot = [jnp.maximum(p, 0) // 2 for p in place]
+    for start in range(0, features, chunk):
+        rows = slice(start, start + chunk)
+        far = jnp.where(
+            slot[2] < few,
+            far_a[jnp.minimum(slot[2], few - 1), rows],
+            far_b[jnp.maximum(slot[2] - few, 0), rows],
+        )
+        values = (own[slot[0], rows], after[slot[1], rows], far, before[slot[3], rows])
+        values = [value.astype(F32) for value in values]
+        for b in range(2):
+            total = 0.0
+            for p, value in zip(place, values):
+                total += jnp.where((p >= 0) & (p % 2 == b), value, 0.0)
+            out[0, rows, b * BLK : (b + 1) * BLK] = total.astype(BF16)
 
 
 def on_device(activations, weight, enc_bias, dec_bias, block_ids, counts):
@@ -241,17 +236,32 @@
     )(core[None], activations.reshape(chips, 2, share, width), dec_bias[None, :])
 
     matmul = 2 * half * width * latents
-    give, keep, tiles = call(
-        functools.partial(encode_kernel, slots),
-        (shape((half, latents), F32), shape((half, latents), F32), shape((width, latents), BF16)),
-        [SMEM_SPEC, VMEM_SPEC, VMEM_SPEC, ANY_SPEC],
-        (VMEM_SPEC, VMEM_SPEC, VMEM_SPEC),
-        flops=2 * matmul,
-        bytes_accessed=4 * half * latents * 4,
+    x_o, c_o, bias_o = (lax.ppermute(a, "dp", swap) for a in (x_g, c_g, dec_bias[None, :]))
+    tiles = call(
+        functools.partial(fetch_kernel, slots),
+        shape((width, latents), BF16),
+        [SMEM_SPEC, ANY_SPEC],
+        VMEM_SPEC,
+        bytes_accessed=2 * width * latents * 2,
         scratch=[pltpu.SemaphoreType.DMA((slots,))],
-    )(ids, c_g, c_k, blocks)
-
-    keep = keep + lax.ppermute(give, "dp", swap)
+    )(ids, blocks)
+    tiles_o = lax.ppermute(tiles, "dp", swap)
+    part = call(
+        encode_kernel,
+        shape((half, latents), F32),
+        [VMEM_SPEC] * 2,
+        VMEM_SPEC,
+        flops=matmul,
+        bytes_accessed=4 * half * latents * 2,
+    )(c_k, tiles)
+    keep = call(
+        encode_rest_kernel,
+        shape((half, latents), F32),
+        [VMEM_SPEC] * 3,
+        VMEM_SPEC,
+        flops=matmul,
+        bytes_accessed=4 * half * latents * 3,
+    )(c_o, tiles_o, part)
     parts = across_chips(keep.reshape(chips, share, latents))
     pre, spread = call(
         activate_kernel,
@@ -261,30 +271,23 @@
         bytes_accessed=half * latents * 6,
     )(parts, bias_row, live_row)
     act_k = across_chips(spread).reshape(half, latents)
-    act_g = lax.ppermute(act_k, "dp", swap)
 
     scale = 2.0 / math.sqrt(rows * owners)
-    give, keep, out_g, out_k = call(
+    packed, out_k, out_o = call(
         functools.partial(error_kernel, scale, 1.0 / (width * groups)),
         (
-            shape((half, latents + BLK), F32),
             shape((half, latents + BLK), F32),
             shape((half, width), BF16),
             shape((half, width), BF16),
         ),
-        [VMEM_SPEC] * 6,
-        (VMEM_SPEC,) * 4,
+        [VMEM_SPEC] * 7,
+        (VMEM_SPEC,) * 3,
         flops=4 * matmul,
         bytes_accessed=half * latents * 14,
-    )(act_g, act_k, tiles, x_g, x_k, dec_bias[None, :])
-    packed = call(
-        pack_kernel,
-        shape((half, latents + BLK), F32),
-        [VMEM_SPEC] * 2,
-        VMEM_SPEC,
-        bytes_accessed=half * latents * 12,
-    )(keep, lax.ppermute(give, "dp", swap))
+    )(act_k, tiles, tiles_o, x_k, x_o, dec_bias[None, :], bias_o)
     parts = across_chips(packed.astype(jnp.float16).reshape(chips, share, latents + BLK))
+    act_g = lax.ppermute(act_k, "dp", swap)
+    out_g = lax.ppermute(out_o, "dp", swap)
     second = call(
         second_kernel,
         shape((width, latents), F32),
@@ -327,7 +330,6 @@
             in_specs=[SMEM_SPEC] + [VMEM_SPEC] * 5,
             out_specs=pl.BlockSpec((1, features, 2 * BLK), lambda y: (y, 0, 0)),
             out_shape=shape((down, features, 2 * BLK), BF16),
-            scratch_shapes=[pltpu.VMEM((2, features, BLK), F32)],
             compiler_params=pltpu.CompilerParams(vmem_limit_bytes=VMEM_LIMIT),
             cost_estimate=pl.CostEstimate(
                 flops=owners * features * BLK,

time: 345 us -> 343 us (level)
  waiting for transfers between devices: 167 us -> 145 us
  starting transfers between devices: 71.6 us -> 83.9 us
  blocking collectives: 62.2 us -> 69.1 us
  local copies, waits for them, and re-layouts: 4 us -> 8.12 us
    all_to_all x0 -> x1, blocking collectives: none -> 48 us  [on_device(): lax.all_to_all(blocks.reshape(owners, width, BLK), 'latent', 0, 0, tiled=...]
    all_to_all x1 -> x0, waiting for transfers between devices: 44.3 us -> none  [on_device(): lax.all_to_all(blocks.reshape(owners, width, BLK), 'latent', 0, 0, tiled=...]
    all_to_all x3 -> x1, blocking collectives: 62.2 us -> 21.1 us  [across_chips(): lax.all_to_all(array, 'dp', 0, 0, tiled=True, axis_index_groups=same_core)]
    all_to_all x1 -> x3, waiting for transfers between devices: 28.6 us -> 54.3 us  [across_chips(): lax.all_to_all(array, 'dp', 0, 0, tiled=True, axis_index_groups=same_core)]
    all_to_all x1 -> x3, starting transfers between devices: 7.11 us -> 14.1 us  [across_chips(): lax.all_to_all(array, 'dp', 0, 0, tiled=True, axis_index_groups=same_core)]
    ppermute x2 -> x5, starting transfers between devices: 9.39 us -> 15.6 us  [the longest x1 7.41 us: on_device(): tiles_o = lax.ppermute(tiles, 'dp', swap)]
    all_to_all x1 -> x0, starting transfers between devices: 4.99 us -> none  [on_device(): lax.all_to_all(blocks.reshape(owners, width, BLK), 'latent', 0, 0, tiled=...]
    unnamed x8 -> x26, local copies, waits for them, and re-layouts: 0.02 us -> 4.13 us
  transfers between devices with their start and end apart: 18 -> 22, of which waited for: 15 -> 15; matrix products, arithmetic and copies ran while one was open for 1% -> 1% of each run, Pallas kernels for 1% -> 2%
where the time goes in v5:
time: 343 us; the launch traced here: 340 us
  waiting for transfers between devices  145 us (42%)
  starting transfers between devices  83.9 us (24%)
  blocking collectives  69.1 us (20%)
  between operations  15.2 us (4%)
  Pallas kernels  15 us (4%)
  local copies, waits for them, and re-layouts  8.12 us (2%)
    all_to_all x3, waiting for transfers between devices, across_chips(): lax.all_to_all(array, 'dp', 0, 0, tiled=True, axis_index_groups=same_core)  54.3 us
    all_to_all x1, blocking collectives, on_device(): lax.all_to_all(blocks.reshape(owners, width, BLK), 'latent', 0, 0, tiled=...  48 us
    all_gather x1, waiting for transfers between devices, on_device(): column = lax.all_gather(weight, 'latent', axis=0, axis_index_groups=same_x)  25.5 us
    all_to_all x2, waiting for transfers between devices, on_device(): lax.all_to_all(sums, 'latent', 0, 0, tiled=True, axis_index_groups=same_x)  24.4 us
    all_to_all x1, blocking collectives, across_chips(): lax.all_to_all(array, 'dp', 0, 0, tiled=True, axis_index_groups=same_core)  21.1 us
    all_to_all x3, starting transfers between devices, across_chips(): lax.all_to_all(array, 'dp', 0, 0, tiled=True, axis_index_groups=same_core)  14.1 us
    all_to_all x1, starting transfers between devices, on_device(): lax.all_to_all(jnp.broadcast_to(note, (owners, 8, BLK)), 'latent', 0, 0,...  10.5 us
    all_to_all x2, starting transfers between devices, on_device(): lax.all_to_all(sums, 'latent', 0, 0, tiled=True, axis_index_groups=same_x)  10.1 us
  transfers between devices with their start and end apart: 22, of which 15 were waited for; matrix products, arithmetic and copies ran while one was open for 1% of the time, Pallas kernels for 2%

profile of v5, /device:TPU:1, one launch (start us, length us, event | category | flops | bytes accessed | tf_op | source)
XLA Modules:
  0.0 339.6 jit_solution(5967437419680402060)
XLA Ops:
  7.2 0.7 all-gather.3.cloned.1.call-update
  8.6 0.7 pad_add_fusion.1
  9.3 0.7 broadcast_in_dim.76
  10.0 10.5 %all-to-all-start = ((s32[32,8,128]{2,1,0:T(8,128)}), s32[32,8,128]{2,1,0:T(8,128)S(1)}, u32[]{:S(2)}, u32[]{:S(2)}) async-start(s32[32,8,128]{2,1,0:T(8,128)} %broadcast_in_dim.76), calls=%async_computation | async-start | bytes 262144 | tf_op jit(solution)/shard_map/all_to_all | solution.py:204
  20.5 9.1 %all-to-all-done = s32[32,8,128]{2,1,0:T(8,128)S(1)} async-done(((s32[32,8,128]{2,1,0:T(8,128)}), s32[32,8,128]{2,1,0:T(8,128)S(1)}, u32[]{:S(2)}, u32[]{:S(2)}) %all-to-all-start) | async-done | bytes 131104 | tf_op jit(solution)/shard_map/all_to_all | solution.py:204
  29.7 0.2 fusion
  30.0 25.5 %all-gather.3.cloned.1.call-done = bf16[4096,256]{1,0:T(8,128)(2,1)} async-done(((bf16[512,256]{1,0:T(8,128)(2,1)}), bf16[4096,256]{1,0:T(8,128)(2,1)}) %all-gather.3.cloned.1.call-update) | async-done | bytes 2097168 | tf_op jit(solution)/shard_map/all_gather | solution.py:199
  55.5 1.7 fusion.3
  57.2 0.5 bitcast_select_fusion
  57.7 48.0 %all_to_all.40.blocks = bf16[32,512,128]{2,1,0:T(8,128)(2,1)S(1)} all-to-all(bf16[32,512,128]{2,1,0:T(8,128)(2,1)S(1)} %bitcast_select_fusion), channel_id=1, replica_groups={{0,8,16,24},{1,9,17,25},{2,10,18,26},{3,11,19,27},{4,12,20,28},{5,13,21..., dimensions={0} | all-to-all | bytes 8388608 | tf_op jit(solution)/shard_map/all_to_all | solution.py:222
  105.7 0.9 shard_map.78.tiles
  106.7 7.4 %collective-permute-start.1 = (bf16[512,1024]{1,0:T(8,128)(2,1)S(1)}, bf16[512,1024]{1,0:T(8,128)(2,1)S(1)}, u32[]{:S(2)}, u32[]{:S(2)}) collective-permute-start(bf16[512,1024]{1,0:T(8,128)(2,1)S(1)} %shard_map.78.tiles), channel_id=1, source_target_pairs={{0,32},{32,0},{64,96},{96,64},{128,160},{160,128},{192,224},{224,1... | collective-permute-start | bytes 3145736 | tf_op jit(solution)/shard_map/ppermute | solution.py:248
  114.1 0.2 shard_map.77
  114.4 0.7 copy-done.7
  115.1 1.9 collective-permute-start
  117.0 0.4 shard_map.79.part
  117.4 1.1 collective-permute-done.rows
  118.5 1.4 shard_map.80
  119.9 7.1 %all-to-all-start.2 = ((f32[8,32,1024]{2,1,0:T(8,128)}), f32[8,32,1024]{2,1,0:T(8,128)S(1)}, u32[]{:S(2)}, u32[]{:S(2)}) async-start(f32[8,32,1024]{2,1,0:T(8,128)} %bitcast.9), calls=%async_computation.2 | async-start | bytes 2097152 | tf_op jit(solution)/shard_map/all_to_all | solution.py:194
  127.0 0.6 gather_fusion
  127.7 28.6 %all-to-all-done.2.parts = f32[8,32,1024]{2,1,0:T(8,128)S(1)} async-done(((f32[8,32,1024]{2,1,0:T(8,128)}), f32[8,32,1024]{2,1,0:T(8,128)S(1)}, u32[]{:S(2)}, u32[]{:S(2)}) %all-to-all-start.2) | async-done | bytes 1048608 | tf_op jit(solution)/shard_map/all_to_all | solution.py:194
  156.5 0.8 copy-done.4
  157.2 3.5 %all-to-all-start.3 = ((bf16[8,32,1024]{2,1,0:T(8,128)(2,1)}), bf16[8,32,1024]{2,1,0:T(8,128)(2,1)S(1)}, u32[]{:S(2)}, u32[]{:S(2)}) async-start(bf16[8,32,1024]{2,1,0:T(8,128)(2,1)} %copy-done.4), calls=%async_computation.3 | async-start | bytes 1048576 | tf_op jit(solution)/shard_map/all_to_all | solution.py:194
  160.7 2.4 collective-permute-start.2
  163.1 1.9 collective-permute-start.3
  165.1 1.1 collective-permute-done.3.bias_o
  166.2 0.7 copy-done.11
  166.9 11.7 %all-to-all-done.3 = bf16[8,32,1024]{2,1,0:T(8,128)(2,1)S(1)} async-done(((bf16[8,32,1024]{2,1,0:T(8,128)(2,1)}), bf16[8,32,1024]{2,1,0:T(8,128)(2,1)S(1)}, u32[]{:S(2)}, u32[]{:S(2)}) %all-to-all-start.3) | async-done | bytes 524320 | tf_op jit(solution)/shard_map/all_to_all | solution.py:194
  178.6 0.9 copy-done.8
  179.6 0.9 copy-done.12
  180.5 1.6 shard_map.82
  182.2 21.1 %all_to_all.41 = f16[8,32,1152]{2,1,0:T(8,128)(2,1)S(1)} all-to-all(f16[8,32,1152]{2,1,0:T(8,128)(2,1)S(1)} %bitcast.42), channel_id=1, replica_groups={{0,64,128,192,256,320,384,448},{32,96,160,224,288,352,416,480},{1,65,12..., dimensions={0} | all-to-all | bytes 1179648 | tf_op jit(solution)/shard_map/all_to_all | solution.py:194
  203.4 1.1 shard_map.83
  204.5 3.5 %all-to-all-start.5 = ((bf16[8,32,1024]{2,1,0:T(8,128)(2,1)}), bf16[8,32,1024]{2,1,0:T(8,128)(2,1)S(1)}, u32[]{:S(2)}, u32[]{:S(2)}) async-start(bf16[8,32,1024]{2,1,0:T(8,128)(2,1)} %get-tuple-element.24), calls=%async_computation.5 | async-start | bytes 1048576 | tf_op jit(solution)/shard_map/all_to_all | solution.py:194
  208.0 3.2 collective-permute-start.6
  211.2 14.0 %all-to-all-done.5 = bf16[8,32,1024]{2,1,0:T(8,128)(2,1)S(1)} async-done(((bf16[8,32,1024]{2,1,0:T(8,128)(2,1)}), bf16[8,32,1024]{2,1,0:T(8,128)(2,1)S(1)}, u32[]{:S(2)}, u32[]{:S(2)}) %all-to-all-start.5) | async-done | bytes 524320 | tf_op jit(solution)/shard_map/all_to_all | solution.py:194
  225.3 3.0 collective-permute-start.4
  228.3 1.9 collective-permute-start.5
  230.2 1.7 collective-permute-done.5.out_g
  231.9 0.8 shard_map.84.second
  232.7 0.7 shard_map.85
  233.4 2.2 collective-permute-start.9
  235.6 4.3 %collective-permute-start.7 = (bf16[8,256,128]{2,1,0:T(8,128)(2,1)S(1)}, bf16[8,256,128]{2,1,0:T(8,128)(2,1)S(1)}, u32[]{:S(2)}, u32[]{:S(2)}) collective-permute-start(bf16[8,256,128]{2,1,0:T(8,128)(2,1)S(1)} %get-tuple-element.27.own), channel_id=1, source_target_pairs={{0,24},{1,25},{2,26},{3,27},{4,28},{5,29},{6,30},{7,31},{8,0},{9,1... | collective-permute-start | bytes 1572872 | tf_op jit(solution)/shard_map/ppermute | solution.py:323
  240.0 0.2 slice_reduce_fusion.1
  240.2 0.2 select_reduce_fusion
  240.4 9.5 %collective-permute-done.9.before = bf16[8,256,128]{2,1,0:T(8,128)(2,1)S(1)} collective-permute-done((bf16[8,256,128]{2,1,0:T(8,128)(2,1)S(1)}, bf16[8,256,128]{2,1,0:T(8,128)(2,1)S(1)}, u32[]{:S(2)}, u32[]{:S(2)}) %collective-permute-start.9) | collective-permute-done | bytes 524320 | tf_op jit(solution)/shard_map/ppermute | solution.py:322
  249.9 1.9 collective-permute-start.10
  251.9 4.6 %collective-permute-start.8 = (bf16[4,256,128]{2,1,0:T(8,128)(2,1)S(1)}, bf16[4,256,128]{2,1,0:T(8,128)(2,1)S(1)}, u32[]{:S(2)}, u32[]{:S(2)}) collective-permute-start(bf16[4,256,128]{2,1,0:T(8,128)(2,1)S(1)} %slice.45), channel_id=1, source_target_pairs={{0,24},{1,25},{2,26},{3,27},{4,28},{5,29},{6,30},{7,31},{8,0},{9,1... | collective-permute-start | bytes 786440 | tf_op jit(solution)/shard_map/ppermute | solution.py:324
  256.5 3.4 collective-permute-done.10.far_b
  259.9 0.9 collective-permute-done.8.far_a
  260.8 3.8 %shard_map.86 = bf16[8,256,256]{2,1,0:T(8,128)(2,1)} custom-call(s32[4,8]{1,0:T(4,128)S(1)} %constant_dynamic-slice_fusion.places, bf16[8,256,128]{2,1,0:T(8,128)(2,1)S(1)} %get-tuple-element.27.own, bf16[8,256,128]{2,1,0:T(8,128)(2,1)S(1)} %collective-permute-done.7.after, bf16[4,256,128]{2,1,0:T(8,128)(2,1)S(1)} %collective-permute-done.8.far_a, ...), custom_call_target="tpu_custom_call" | custom-call | flops 1048576 | bytes 2097152 | tf_op jit(solution)/shard_map/pallas_call | solution.py:327
  264.7 4.0 %all-to-all-start.6 = ((bf16[8,256,256]{2,1,0:T(8,128)(2,1)}), bf16[8,256,256]{2,1,0:T(8,128)(2,1)S(1)}, u32[]{:S(2)}, u32[]{:S(2)}) async-start(bf16[8,256,256]{2,1,0:T(8,128)(2,1)} %shard_map.86), calls=%async_computation.6 | async-start | bytes 2097152 | tf_op jit(solution)/shard_map/all_to_all | solution.py:340
  268.7 5.3 %collective-permute-start.11 = (bf16[8,256,128]{2,1,0:T(8,128)(2,1)S(1)}, bf16[8,256,128]{2,1,0:T(8,128)(2,1)S(1)}, u32[]{:S(2)}, u32[]{:S(2)}) collective-permute-start(bf16[8,256,128]{2,1,0:T(8,128)(2,1)S(1)} %get-tuple-element.28.own), channel_id=1, source_target_pairs={{0,24},{1,25},{2,26},{3,27},{4,28},{5,29},{6,30},{7,31},{8,0},{9,1... | collective-permute-start | bytes 1572872 | tf_op jit(solution)/shard_map/ppermute | solution.py:323
  274.0 1.9 collective-permute-start.13
  275.9 6.8 %collective-permute-done.11.after = bf16[8,256,128]{2,1,0:T(8,128)(2,1)S(1)} collective-permute-done((bf16[8,256,128]{2,1,0:T(8,128)(2,1)S(1)}, bf16[8,256,128]{2,1,0:T(8,128)(2,1)S(1)}, u32[]{:S(2)}, u32[]{:S(2)}) %collective-permute-start.11) | collective-permute-done | bytes 524320 | tf_op jit(solution)/shard_map/ppermute | solution.py:323
  282.8 5.3 %collective-permute-start.12 = (bf16[4,256,128]{2,1,0:T(8,128)(2,1)S(1)}, bf16[4,256,128]{2,1,0:T(8,128)(2,1)S(1)}, u32[]{:S(2)}, u32[]{:S(2)}) collective-permute-start(bf16[4,256,128]{2,1,0:T(8,128)(2,1)S(1)} %slice.47), channel_id=1, source_target_pairs={{0,24},{1,25},{2,26},{3,27},{4,28},{5,29},{6,30},{7,31},{8,0},{9,1... | collective-permute-start | bytes 786440 | tf_op jit(solution)/shard_map/ppermute | solution.py:324
  288.2 1.9 collective-permute-start.14
  290.1 1.3 collective-permute-done.12.far_a
  291.4 5.4 %collective-permute-done.14.far_b = bf16[4,256,128]{2,1,0:T(8,128)(2,1)S(1)} collective-permute-done((bf16[4,256,128]{2,1,0:T(8,128)(2,1)S(1)}, bf16[4,256,128]{2,1,0:T(8,128)(2,1)S(1)}, u32[]{:S(2)}, u32[]{:S(2)}) %collective-permute-start.14) | collective-permute-done | bytes 262176 | tf_op jit(solution)/shard_map/ppermute | solution.py:325
  296.8 3.8 %shard_map.87 = bf16[8,256,256]{2,1,0:T(8,128)(2,1)} custom-call(s32[4,8]{1,0:T(4,128)S(1)} %constant_dynamic-slice_fusion.places, bf16[8,256,128]{2,1,0:T(8,128)(2,1)S(1)} %get-tuple-element.28.own, bf16[8,256,128]{2,1,0:T(8,128)(2,1)S(1)} %collective-permute-done.11.after, bf16[4,256,128]{2,1,0:T(8,128)(2,1)S(1)} %collective-permute-done.12.far_a, ...), custom_call_target="tpu_custom_call" | custom-call | flops 1048576 | bytes 2097152 | tf_op jit(solution)/shard_map/pallas_call | solution.py:327
  300.6 6.1 %all-to-all-start.7 = ((bf16[8,256,256]{2,1,0:T(8,128)(2,1)}), bf16[8,256,256]{2,1,0:T(8,128)(2,1)S(1)}, u32[]{:S(2)}, u32[]{:S(2)}) async-start(bf16[8,256,256]{2,1,0:T(8,128)(2,1)} %shard_map.87), calls=%async_computation.7 | async-start | bytes 2097152 | tf_op jit(solution)/shard_map/all_to_all | solution.py:340
  306.7 0.6 slice_reduce_fusion
  307.5 24.3 %all-to-all-done.7 = bf16[8,256,256]{2,1,0:T(8,128)(2,1)S(1)} async-done(((bf16[8,256,256]{2,1,0:T(8,128)(2,1)}), bf16[8,256,256]{2,1,0:T(8,128)(2,1)S(1)}, u32[]{:S(2)}, u32[]{:S(2)}) %all-to-all-start.7) | async-done | bytes 1048608 | tf_op jit(solution)/shard_map/all_to_all | solution.py:340
  332.0 0.8 pad_maximum_fusion
  (56 shorter events, 1.1 us)
Async XLA Ops:
  7.2 119.9 %copy-start = (f32[8192]{0:T(1024)S(1)}, f32[8192]{0:T(1024)}, u32[]{:S(2)}) copy-start(f32[8192]{0:T(1024)} %param.8) | copy-start | bytes 98308
  7.2 48.3 %all-gather.3.cloned.1.call-start = ((), (), s32[]{:S(2)}) async-start(), calls=%async_computation.8 | async-start | bytes 2359296 | tf_op jit(solution)/shard_map/all_gather | solution.py:199
  10.0 19.7 %all-to-all-start = ((s32[32,8,128]{2,1,0:T(8,128)}), s32[32,8,128]{2,1,0:T(8,128)S(1)}, u32[]{:S(2)}, u32[]{:S(2)}) async-start(s32[32,8,128]{2,1,0:T(8,128)} %broadcast_in_dim.76), calls=%async_computation | async-start | bytes 262144 | tf_op jit(solution)/shard_map/all_to_all | solution.py:204
  57.7 48.0 %copy-start.6 = (s32[1,8]{1,0:T(1,128)S(1)}, s32[1,8]{1,0:T(1,128)}, u32[]{:S(2)}) copy-start(s32[1,8]{1,0:T(1,128)} %param.10) | copy-start | bytes 100
  105.7 8.4 %copy-start.3 = (bf16[512,512]{1,0:T(8,128)(2,1)S(1)}, bf16[512,512]{1,0:T(8,128)(2,1)}, u32[]{:S(2)}) copy-start(bf16[512,512]{1,0:T(8,128)(2,1)} %param.6) | copy-start | bytes 1572868
  105.7 8.4 %copy-start.5 = (f32[512]{0:T(512)S(1)}, f32[512]{0:T(512)}, u32[]{:S(2)}) copy-start(f32[512]{0:T(512)} %param.9) | copy-start | bytes 6148
  106.7 11.8 %collective-permute-start.1 = (bf16[512,1024]{1,0:T(8,128)(2,1)S(1)}, bf16[512,1024]{1,0:T(8,128)(2,1)S(1)}, u32[]{:S(2)}, u32[]{:S(2)}) collective-permute-start(bf16[512,1024]{1,0:T(8,128)(2,1)S(1)} %shard_map.78.tiles), channel_id=1, source_target_pairs={{0,32},{32,0},{64,96},{96,64},{128,160},{160,128},{192,224},{224,1... | collective-permute-start | bytes 3145736 | tf_op jit(solution)/shard_map/ppermute | solution.py:248
  114.4 0.7 copy-start.7
  115.1 1.9 copy-start.9
  115.1 4.8 %copy-start.1 = (bf16[512,512]{1,0:T(8,128)(2,1)}, bf16[512,512]{1,0:T(8,128)(2,1)S(1)}, u32[]{:S(2)}) copy-start(bf16[512,512]{1,0:T(8,128)(2,1)S(1)} %get-tuple-element.16.c_t) | copy-start | bytes 1572868
  115.1 3.4 %collective-permute-start = (bf16[256,512]{1,0:T(8,128)(2,1)S(1)}, bf16[256,512]{1,0:T(8,128)(2,1)S(1)}, u32[]{:S(2)}, u32[]{:S(2)}) collective-permute-start(bf16[256,512]{1,0:T(8,128)(2,1)S(1)} %get-tuple-element.17), channel_id=1, source_target_pairs={{0,32},{32,0},{64,96},{96,64},{128,160},{160,128},{192,224},{224,1... | collective-permute-start | bytes 786440 | tf_op jit(solution)/shard_map/ppermute | solution.py:239
  119.9 36.4 %all-to-all-start.2 = ((f32[8,32,1024]{2,1,0:T(8,128)}), f32[8,32,1024]{2,1,0:T(8,128)S(1)}, u32[]{:S(2)}, u32[]{:S(2)}) async-start(f32[8,32,1024]{2,1,0:T(8,128)} %bitcast.9), calls=%async_computation.2 | async-start | bytes 2097152 | tf_op jit(solution)/shard_map/all_to_all | solution.py:194
  156.4 0.8 copy-start.4
  157.2 21.4 %all-to-all-start.3 = ((bf16[8,32,1024]{2,1,0:T(8,128)(2,1)}), bf16[8,32,1024]{2,1,0:T(8,128)(2,1)S(1)}, u32[]{:S(2)}, u32[]{:S(2)}) async-start(bf16[8,32,1024]{2,1,0:T(8,128)(2,1)} %copy-done.4), calls=%async_computation.3 | async-start | bytes 1048576 | tf_op jit(solution)/shard_map/all_to_all | solution.py:194
  160.7 5.5 %collective-permute-start.2 = (bf16[256,512]{1,0:T(8,128)(2,1)}, bf16[256,512]{1,0:T(8,128)(2,1)S(1)}, u32[]{:S(2)}, u32[]{:S(2)}) collective-permute-start(bf16[256,512]{1,0:T(8,128)(2,1)} %copy-done.9), channel_id=1, source_target_pairs={{0,32},{32,0},{64,96},{96,64},{128,160},{160,128},{192,224},{224,1... | collective-permute-start | bytes 786440 | tf_op jit(solution)/shard_map/ppermute | solution.py:239
  163.1 3.1 collective-permute-start.3
  166.2 0.7 copy-start.11
  178.6 1.0 copy-start.8
  179.6 0.9 copy-start.12
  182.1 21.3 %copy-start.10 = (bf16[256,512]{1,0:T(8,128)(2,1)}, bf16[256,512]{1,0:T(8,128)(2,1)S(1)}, u32[]{:S(2)}) copy-start(bf16[256,512]{1,0:T(8,128)(2,1)S(1)} %get-tuple-element.25) | copy-start | bytes 786436
  204.5 20.8 %all-to-all-start.5 = ((bf16[8,32,1024]{2,1,0:T(8,128)(2,1)}), bf16[8,32,1024]{2,1,0:T(8,128)(2,1)S(1)}, u32[]{:S(2)}, u32[]{:S(2)}) async-start(bf16[8,32,1024]{2,1,0:T(8,128)(2,1)} %get-tuple-element.24), calls=%async_computation.5 | async-start | bytes 1048576 | tf_op jit(solution)/shard_map/all_to_all | solution.py:194
  208.0 24.7 %copy-start.2 = (bf16[512,512]{1,0:T(8,128)(2,1)S(1)}, bf16[512,512]{1,0:T(8,128)(2,1)}, u32[]{:S(2)}) copy-start(bf16[512,512]{1,0:T(8,128)(2,1)} %copy-done.1) | copy-start | bytes 1572868
  208.0 23.9 %collective-permute-start.6 = (bf16[256,1024]{1,0:T(8,128)(2,1)S(1)}, bf16[256,1024]{1,0:T(8,128)(2,1)S(1)}, u32[]{:S(2)}, u32[]{:S(2)}) collective-permute-start(bf16[256,1024]{1,0:T(8,128)(2,1)S(1)} %bitcast.29), channel_id=1, source_target_pairs={{0,32},{32,0},{64,96},{96,64},{128,160},{160,128},{192,224},{224,1... | collective-permute-start | bytes 1572872 | tf_op jit(solution)/shard_map/ppermute | solution.py:289
  225.3 7.4 %collective-permute-start.4 = (bf16[256,1024]{1,0:T(8,128)(2,1)S(1)}, bf16[256,1024]{1,0:T(8,128)(2,1)S(1)}, u32[]{:S(2)}, u32[]{:S(2)}) collective-permute-start(bf16[256,1024]{1,0:T(8,128)(2,1)S(1)} %bitcast.31), channel_id=1, source_target_pairs={{0,32},{32,0},{64,96},{96,64},{128,160},{160,128},{192,224},{224,1... | collective-permute-start | bytes 1572872 | tf_op jit(solution)/shard_map/ppermute | solution.py:308
  228.3 3.6 %collective-permute-start.5 = (bf16[256,512]{1,0:T(8,128)(2,1)}, bf16[256,512]{1,0:T(8,128)(2,1)S(1)}, u32[]{:S(2)}, u32[]{:S(2)}) collective-permute-start(bf16[256,512]{1,0:T(8,128)(2,1)} %copy-done.10), channel_id=1, source_target_pairs={{0,32},{32,0},{64,96},{96,64},{128,160},{160,128},{192,224},{224,1... | collective-permute-start | bytes 786440 | tf_op jit(solution)/shard_map/ppermute | solution.py:290
  233.4 16.5 %collective-permute-start.9 = (bf16[8,256,128]{2,1,0:T(8,128)(2,1)S(1)}, bf16[8,256,128]{2,1,0:T(8,128)(2,1)S(1)}, u32[]{:S(2)}, u32[]{:S(2)}) collective-permute-start(bf16[8,256,128]{2,1,0:T(8,128)(2,1)S(1)} %get-tuple-element.27.own), channel_id=1, source_target_pairs={{0,8},{1,9},{2,10},{3,11},{4,12},{5,13},{6,14},{7,15},{8,16},{9,17... | collective-permute-start | bytes 1572872 | tf_op jit(solution)/shard_map/ppermute | solution.py:322
  235.6 16.3 %collective-permute-start.7 = (bf16[8,256,128]{2,1,0:T(8,128)(2,1)S(1)}, bf16[8,256,128]{2,1,0:T(8,128)(2,1)S(1)}, u32[]{:S(2)}, u32[]{:S(2)}) collective-permute-start(bf16[8,256,128]{2,1,0:T(8,128)(2,1)S(1)} %get-tuple-element.27.own), channel_id=1, source_target_pairs={{0,24},{1,25},{2,26},{3,27},{4,28},{5,29},{6,30},{7,31},{8,0},{9,1... | collective-permute-start | bytes 1572872 | tf_op jit(solution)/shard_map/ppermute | solution.py:323
  249.9 10.0 %collective-permute-start.10 = (bf16[4,256,128]{2,1,0:T(8,128)(2,1)S(1)}, bf16[4,256,128]{2,1,0:T(8,128)(2,1)S(1)}, u32[]{:S(2)}, u32[]{:S(2)}) collective-permute-start(bf16[4,256,128]{2,1,0:T(8,128)(2,1)S(1)} %slice.46), channel_id=1, source_target_pairs={{0,8},{1,9},{2,10},{3,11},{4,12},{5,13},{6,14},{7,15},{8,16},{9,17... | collective-permute-start | bytes 786440 | tf_op jit(solution)/shard_map/ppermute | solution.py:325
  251.9 8.9 %collective-permute-start.8 = (bf16[4,256,128]{2,1,0:T(8,128)(2,1)S(1)}, bf16[4,256,128]{2,1,0:T(8,128)(2,1)S(1)}, u32[]{:S(2)}, u32[]{:S(2)}) collective-permute-start(bf16[4,256,128]{2,1,0:T(8,128)(2,1)S(1)} %slice.45), channel_id=1, source_target_pairs={{0,24},{1,25},{2,26},{3,27},{4,28},{5,29},{6,30},{7,31},{8,0},{9,1... | collective-permute-start | bytes 786440 | tf_op jit(solution)/shard_map/ppermute | solution.py:324
  264.7 35.9 %all-to-all-start.6 = ((bf16[8,256,256]{2,1,0:T(8,128)(2,1)}), bf16[8,256,256]{2,1,0:T(8,128)(2,1)S(1)}, u32[]{:S(2)}, u32[]{:S(2)}) async-start(bf16[8,256,256]{2,1,0:T(8,128)(2,1)} %shard_map.86), calls=%async_computation.6 | async-start | bytes 2097152 | tf_op jit(solution)/shard_map/all_to_all | solution.py:340
  268.7 14.1 %collective-permute-start.11 = (bf16[8,256,128]{2,1,0:T(8,128)(2,1)S(1)}, bf16[8,256,128]{2,1,0:T(8,128)(2,1)S(1)}, u32[]{:S(2)}, u32[]{:S(2)}) collective-permute-start(bf16[8,256,128]{2,1,0:T(8,128)(2,1)S(1)} %get-tuple-element.28.own), channel_id=1, source_target_pairs={{0,24},{1,25},{2,26},{3,27},{4,28},{5,29},{6,30},{7,31},{8,0},{9,1... | collective-permute-start | bytes 1572872 | tf_op jit(solution)/shard_map/ppermute | solution.py:323
  274.0 14.1 %collective-permute-start.13 = (bf16[8,256,128]{2,1,0:T(8,128)(2,1)S(1)}, bf16[8,256,128]{2,1,0:T(8,128)(2,1)S(1)}, u32[]{:S(2)}, u32[]{:S(2)}) collective-permute-start(bf16[8,256,128]{2,1,0:T(8,128)(2,1)S(1)} %get-tuple-element.28.own), channel_id=1, source_target_pairs={{0,8},{1,9},{2,10},{3,11},{4,12},{5,13},{6,14},{7,15},{8,16},{9,17... | collective-permute-start | bytes 1572872 | tf_op jit(solution)/shard_map/ppermute | solution.py:322
  282.8 8.6 %collective-permute-start.12 = (bf16[4,256,128]{2,1,0:T(8,128)(2,1)S(1)}, bf16[4,256,128]{2,1,0:T(8,128)(2,1)S(1)}, u32[]{:S(2)}, u32[]{:S(2)}) collective-permute-start(bf16[4,256,128]{2,1,0:T(8,128)(2,1)S(1)} %slice.47), channel_id=1, source_target_pairs={{0,24},{1,25},{2,26},{3,27},{4,28},{5,29},{6,30},{7,31},{8,0},{9,1... | collective-permute-start | bytes 786440 | tf_op jit(solution)/shard_map/ppermute | solution.py:324
  288.2 8.6 %collective-permute-start.14 = (bf16[4,256,128]{2,1,0:T(8,128)(2,1)S(1)}, bf16[4,256,128]{2,1,0:T(8,128)(2,1)S(1)}, u32[]{:S(2)}, u32[]{:S(2)}) collective-permute-start(bf16[4,256,128]{2,1,0:T(8,128)(2,1)S(1)} %slice.48), channel_id=1, source_target_pairs={{0,8},{1,9},{2,10},{3,11},{4,12},{5,13},{6,14},{7,15},{8,16},{9,17... | collective-permute-start | bytes 786440 | tf_op jit(solution)/shard_map/ppermute | solution.py:325
  300.6 31.2 %all-to-all-start.7 = ((bf16[8,256,256]{2,1,0:T(8,128)(2,1)}), bf16[8,256,256]{2,1,0:T(8,128)(2,1)S(1)}, u32[]{:S(2)}, u32[]{:S(2)}) async-start(bf16[8,256,256]{2,1,0:T(8,128)(2,1)} %shard_map.87), calls=%async_computation.7 | async-start | bytes 2097152 | tf_op jit(solution)/shard_map/all_to_all | solution.py:340
Sparse Core Ops, SparseCore 0:
  10.1 45.3 all-gather.2

commit v6 on v5

--- a/solution.py
+++ b/solution.py
@@ -82,12 +82,21 @@
     return jnp.ceil(jnp.log2(jnp.maximum(x, 1e-30)))
 
 
-def error_kernel(scale, loss_scale, act, tiles, tiles_o, x, x_o, bias, bias_o, out, grad_out, grad_out_o):
+def error_kernel(
+    scale, loss_scale, act, tiles, tiles_o, x, x_o, bias, bias_o, out, grad_out, grad_out_o, held, sems
+):
     latents = tiles.shape[1]
     loss = 0.0
     grads = []
-    for w, rows, b, g in ((tiles, x, bias, grad_out), (tiles_o, x_o, bias_o, grad_out_o)):
-        err = contract(act[...], w[...], 1, 1) + b[...] - rows[...].astype(F32)
+    copies = []
+    for i, rows in enumerate((x, x_o)):
+        copy = pltpu.make_async_copy(rows, held.at[i], sems.at[i])
+        copy.start()
+        copies.append(copy)
+    for i, (w, b, g) in enumerate(((tiles, bias, grad_out), (tiles_o, bias_o, grad_out_o))):
+        err = contract(act[...], w[...], 1, 1) + b[...]
+        copies[i].wait()
+        err = err - held[i].astype(F32)
         loss += jnp.sum(err * err, axis=1, keepdims=True) * loss_scale
         grad = (err * scale).astype(BF16)
         g[...] = grad
@@ -114,7 +123,7 @@
         )
 
 
-def gate_kernel(parts, pre, live, spread, loss):
+def gate_kernel(parts, pre, live, second, spread, loss):
     chips, _, width = parts.shape
     latents = width - BLK
     total = jnp.zeros(pre.shape, F32)
@@ -146,26 +155,30 @@
 
 
 def combine_kernel(places, own, after, far_a, far_b, before, out):
-    y = pl.program_id(0)
     few = far_a.shape[0]
     features = own.shape[1]
     chunk = min(features, 64)
-    place = [places[x, y] for x in range(4)]
-    slot = [jnp.maximum(p, 0) // 2 for p in place]
-    for start in range(0, features, chunk):
-        rows = slice(start, start + chunk)
-        far = jnp.where(
-            slot[2] < few,
-            far_a[jnp.minimum(slot[2], few - 1), rows],
-            far_b[jnp.maximum(slot[2] - few, 0), rows],
-        )
-        values = (own[slot[0], rows], after[slot[1], rows], far, before[slot[3], rows])
-        values = [value.astype(F32) for value in values]
-        for b in range(2):
-            total = 0.0
-            for p, value in zip(place, values):
-                total += jnp.where((p >= 0) & (p % 2 == b), value, 0.0)
-            out[0, rows, b * BLK : (b + 1) * BLK] = total.astype(BF16)
+
+    def one_owner(y, carry):
+        place = [places[x, y] for x in range(4)]
+        slot = [jnp.maximum(p, 0) // 2 for p in place]
+        for start in range(0, features, chunk):
+            rows = slice(start, start + chunk)
+            far = jnp.where(
+                slot[2] < few,
+                far_a[jnp.minimum(slot[2], few - 1), rows],
+                far_b[jnp.maximum(slot[2] - few, 0), rows],
+            )
+            values = (own[slot[0], rows], after[slot[1], rows], far, before[slot[3], rows])
+            values = [value.astype(F32) for value in values]
+            for b in range(2):
+                total = 0.0
+                for p, value in zip(place, values):
+                    total += jnp.where((p >= 0) & (p % 2 == b), value, 0.0)
+                out[y, rows, b * BLK : (b + 1) * BLK] = total.astype(BF16)
+        return carry
+
+    lax.fori_loop(0, out.shape[0], one_owner, 0)
 
 
 def on_device(activations, weight, enc_bias, dec_bias, block_ids, counts):
@@ -216,16 +229,6 @@
     places = jnp.sum(jnp.where(match & row_live[:, None, :], code[:, None, :], 0), axis=2) - 1
     places = jnp.roll(places, -my_x, axis=0)
 
-    blocks = jnp.where(
-        upper[:, :, None, None], column[None, :, :, BLK:], column[None, :, :, :BLK]
-    )
-    blocks = lax.all_to_all(
-        blocks.reshape(owners, width, BLK), "latent", 0, 0, tiled=True, axis_index_groups=same_y
-    )
-
-    live = (jnp.arange(slots) < counts[0]).astype(F32)
-    live_row = jnp.repeat(live, BLK)[None, :]
-    bias_row = jnp.take(enc_bias.reshape(-1, BLK), ids, axis=0).reshape(1, latents)
     x_g, x_k, c_g, c_k, c_t = call(
         prepare_kernel,
         (shape((half, width), BF16),) * 4 + (shape((width, rows), BF16),),
@@ -234,9 +237,20 @@
         flops=rows * width * 4,
         bytes_accessed=rows * width * 8,
     )(core[None], activations.reshape(chips, 2, share, width), dec_bias[None, :])
-
+    x_o, c_o, bias_o = (lax.ppermute(a, "dp", swap) for a in (x_g, c_g, dec_bias[None, :]))
+    upper, x_o, c_o, bias_o = lax.optimization_barrier((upper, x_o, c_o, bias_o))
+
+    blocks = jnp.where(
+        upper[:, :, None, None], column[None, :, :, BLK:], column[None, :, :, :BLK]
+    )
+    blocks = lax.all_to_all(
+        blocks.reshape(owners, width, BLK), "latent", 0, 0, tiled=True, axis_index_groups=same_y
+    )
+
+    live = (jnp.arange(slots) < counts[0]).astype(F32)
+    live_row = jnp.repeat(live, BLK)[None, :]
+    bias_row = jnp.take(enc_bias.reshape(-1, BLK), ids, axis=0).reshape(1, latents)
     matmul = 2 * half * width * latents
-    x_o, c_o, bias_o = (lax.ppermute(a, "dp", swap) for a in (x_g, c_g, dec_bias[None, :]))
     tiles = call(
         functools.partial(fetch_kernel, slots),
         shape((width, latents), BF16),
@@ -280,10 +294,11 @@
             shape((half, width), BF16),
             shape((half, width), BF16),
         ),
-        [VMEM_SPEC] * 7,
+        [VMEM_SPEC] * 3 + [ANY_SPEC] * 2 + [VMEM_SPEC] * 2,
         (VMEM_SPEC,) * 3,
         flops=4 * matmul,
         bytes_accessed=half * latents * 14,
+        scratch=[pltpu.VMEM((2, half, width), BF16), pltpu.SemaphoreType.DMA((2,))],
     )(act_k, tiles, tiles_o, x_k, x_o, dec_bias[None, :], bias_o)
     parts = across_chips(packed.astype(jnp.float16).reshape(chips, share, latents + BLK))
     act_g = lax.ppermute(act_k, "dp", swap)
@@ -299,10 +314,10 @@
     spread, loss = call(
         gate_kernel,
         (shape((chips, share, latents), BF16), shape((share, BLK), F32)),
-        [VMEM_SPEC] * 3,
+        [VMEM_SPEC] * 3 + [ANY_SPEC],
         (VMEM_SPEC, VMEM_SPEC),
         bytes_accessed=half * latents * 6,
-    )(parts.astype(F32), pre, live_row)
+    )(parts.astype(F32), pre, live_row, second)
     row_error = loss[:, 0]
     gp_k = across_chips(spread).reshape(half, latents)
     gp_g = lax.ppermute(gp_k, "dp", swap)
@@ -324,18 +339,13 @@
         far_a = lax.ppermute(after[:few], "latent", last_x)
         far_b = lax.ppermute(before[few:], "latent", next_x)
         features = part.shape[1]
-        sums = pl.pallas_call(
+        sums = call(
             combine_kernel,
-            grid=(down,),
-            in_specs=[SMEM_SPEC] + [VMEM_SPEC] * 5,
-            out_specs=pl.BlockSpec((1, features, 2 * BLK), lambda y: (y, 0, 0)),
-            out_shape=shape((down, features, 2 * BLK), BF16),
-            compiler_params=pltpu.CompilerParams(vmem_limit_bytes=VMEM_LIMIT),
-            cost_estimate=pl.CostEstimate(
-                flops=owners * features * BLK,
-                bytes_accessed=owners * features * BLK * 2,
-                transcendentals=0,
-            ),
+            shape((down, features, 2 * BLK), BF16),
+            [SMEM_SPEC] + [VMEM_SPEC] * 5,
+            VMEM_SPEC,
+            flops=owners * features * BLK,
+            bytes_accessed=owners * features * BLK * 2,
         )(places, part, after, far_a, far_b, before)
         sums = lax.all_to_all(sums, "latent", 0, 0, tiled=True, axis_index_groups=same_x)
         grads.append(jnp.sum(sums.astype(F32), axis=0))

time: 343 us -> 337 us (0.983)
  blocking collectives: 69.1 us -> 88.4 us
  waiting for transfers between devices: 145 us -> 127 us
  starting transfers between devices: 83.9 us -> 75.8 us
    all_to_all x1 -> x2, blocking collectives: 21.1 us -> 40.4 us  [across_chips(): lax.all_to_all(array, 'dp', 0, 0, tiled=True, axis_index_groups=same_core)]
    all_to_all x3 -> x2, waiting for transfers between devices: 54.3 us -> 41.1 us  [across_chips(): lax.all_to_all(array, 'dp', 0, 0, tiled=True, axis_index_groups=same_core)]
    ppermute x2, waiting for transfers between devices: 6.83 us -> 16.8 us  [on_device(): after = lax.ppermute(part, 'latent', last_x)]
    ppermute x2, waiting for transfers between devices: 9.48 us -> 0.01 us  [on_device(): before = lax.ppermute(part, 'latent', next_x)]
    all_to_all x1, waiting for transfers between devices: 9.1 us -> 0.01 us  [on_device(): lax.all_to_all(jnp.broadcast_to(note, (owners, 8, BLK)), 'latent', 0, 0,...]
    ppermute x2, starting transfers between devices: 9.62 us -> 4.69 us  [on_device(): after = lax.ppermute(part, 'latent', last_x)]
    all_to_all x3 -> x2, starting transfers between devices: 14.1 us -> 11.5 us  [across_chips(): lax.all_to_all(array, 'dp', 0, 0, tiled=True, axis_index_groups=same_core)]
  transfers between devices with their start and end apart: 22 -> 21, of which waited for: 15 -> 15; matrix products, arithmetic and copies ran while one was open for 1% -> 1% of each run, Pallas kernels for 2% -> 1%
where the time goes in v6:
time: 337 us; the launch traced here: 333 us
  waiting for transfers between devices  127 us (38%)
  blocking collectives  88.4 us (26%)
  starting transfers between devices  75.8 us (22%)
  between operations  15.2 us (5%)
  Pallas kernels  13.1 us (4%)
  local copies, waits for them, and re-layouts  9.2 us (3%)
  other arithmetic  5.1 us (2%)
    all_to_all x1, blocking collectives, on_device(): lax.all_to_all(blocks.reshape(owners, width, BLK), 'latent', 0, 0, tiled=...  48 us
    all_to_all x2, waiting for transfers between devices, across_chips(): lax.all_to_all(array, 'dp', 0, 0, tiled=True, axis_index_groups=same_core)  41.1 us
    all_to_all x2, blocking collectives, across_chips(): lax.all_to_all(array, 'dp', 0, 0, tiled=True, axis_index_groups=same_core)  40.4 us
    all_to_all x2, waiting for transfers between devices, on_device(): lax.all_to_all(sums, 'latent', 0, 0, tiled=True, axis_index_groups=same_x)  24.6 us
    all_gather x1, waiting for transfers between devices, on_device(): column = lax.all_gather(weight, 'latent', axis=0, axis_index_groups=same_x)  24 us
    ppermute x2, waiting for transfers between devices, on_device(): after = lax.ppermute(part, 'latent', last_x)  16.8 us
    all_to_all x2, starting transfers between devices, across_chips(): lax.all_to_all(array, 'dp', 0, 0, tiled=True, axis_index_groups=same_core)  11.5 us
    all_to_all x1, starting transfers between devices, on_device(): lax.all_to_all(jnp.broadcast_to(note, (owners, 8, BLK)), 'latent', 0, 0,...  10.5 us
  transfers between devices with their start and end apart: 21, of which 15 were waited for; matrix products, arithmetic and copies ran while one was open for 1% of the time, Pallas kernels for 1%

profile of v6, /device:TPU:1, one launch (start us, length us, event | category | flops | bytes accessed | tf_op | source)
XLA Modules:
  0.0 333.3 jit_solution(9091139082156053561)
XLA Ops:
  7.2 0.7 all-gather.3.cloned.1.call-update
  8.6 0.7 pad_add_fusion.1
  9.3 0.7 broadcast_in_dim.76
  9.9 10.5 %all-to-all-start = ((s32[32,8,128]{2,1,0:T(8,128)}), s32[32,8,128]{2,1,0:T(8,128)S(1)}, u32[]{:S(2)}, u32[]{:S(2)}) async-start(s32[32,8,128]{2,1,0:T(8,128)} %broadcast_in_dim.76), calls=%async_computation | async-start | bytes 262144 | tf_op jit(solution)/shard_map/all_to_all | solution.py:217
  20.5 2.9 collective-permute-start.2
  23.4 1.0 copy-done.3
  24.4 0.7 copy-done.6
  25.1 0.2 shard_map.77
  25.3 0.7 copy-done.9
  26.0 1.9 collective-permute-start
  27.9 2.4 collective-permute-start.1
  30.7 0.8 collective-permute-done.1.rows
  31.6 24.0 %all-gather.3.cloned.1.call-done = bf16[4096,256]{1,0:T(8,128)(2,1)} async-done(((bf16[512,256]{1,0:T(8,128)(2,1)}), bf16[4096,256]{1,0:T(8,128)(2,1)}) %all-gather.3.cloned.1.call-update) | async-done | bytes 2097168 | tf_op jit(solution)/shard_map/all_gather | solution.py:212
  55.5 1.7 fusion.3
  57.2 0.6 bitcast_select_fusion
  57.8 48.0 %all_to_all.40.blocks = bf16[32,512,128]{2,1,0:T(8,128)(2,1)S(1)} all-to-all(bf16[32,512,128]{2,1,0:T(8,128)(2,1)S(1)} %bitcast_select_fusion), channel_id=1, replica_groups={{0,8,16,24},{1,9,17,25},{2,10,18,26},{3,11,19,27},{4,12,20,28},{5,13,21..., dimensions={0} | all-to-all | bytes 8388608 | tf_op jit(solution)/shard_map/all_to_all | solution.py:246
  105.8 0.9 shard_map.78.tiles
  106.8 7.4 %collective-permute-start.3 = (bf16[512,1024]{1,0:T(8,128)(2,1)S(1)}, bf16[512,1024]{1,0:T(8,128)(2,1)S(1)}, u32[]{:S(2)}, u32[]{:S(2)}) collective-permute-start(bf16[512,1024]{1,0:T(8,128)(2,1)S(1)} %shard_map.78.tiles), channel_id=1, source_target_pairs={{0,32},{32,0},{64,96},{96,64},{128,160},{160,128},{192,224},{224,1... | collective-permute-start | bytes 3145736 | tf_op jit(solution)/shard_map/ppermute | solution.py:262
  114.2 0.4 shard_map.79.part
  114.6 1.8 collective-permute-done.3.tiles.tiles_o
  116.5 1.4 shard_map.80
  117.9 7.3 %all-to-all-start.2 = ((f32[8,32,1024]{2,1,0:T(8,128)}), f32[8,32,1024]{2,1,0:T(8,128)S(1)}, u32[]{:S(2)}, u32[]{:S(2)}) async-start(f32[8,32,1024]{2,1,0:T(8,128)} %bitcast.9), calls=%async_computation.2 | async-start | bytes 2097152 | tf_op jit(solution)/shard_map/all_to_all | solution.py:207
  125.2 0.6 gather_fusion
  125.8 28.6 %all-to-all-done.2.parts = f32[8,32,1024]{2,1,0:T(8,128)S(1)} async-done(((f32[8,32,1024]{2,1,0:T(8,128)}), f32[8,32,1024]{2,1,0:T(8,128)S(1)}, u32[]{:S(2)}, u32[]{:S(2)}) %all-to-all-start.2) | async-done | bytes 1048608 | tf_op jit(solution)/shard_map/all_to_all | solution.py:207
  154.5 20.3 %all_to_all.41 = bf16[8,32,1024]{2,1,0:T(8,128)(2,1)S(1)} all-to-all(bf16[8,32,1024]{2,1,0:T(8,128)(2,1)S(1)} %get-tuple-element.26), channel_id=1, replica_groups={{0,64,128,192,256,320,384,448},{32,96,160,224,288,352,416,480},{1,65,12..., dimensions={0} | all-to-all | bytes 1048576 | tf_op jit(solution)/shard_map/all_to_all | solution.py:207
  174.8 0.9 copy-done.10
  175.8 0.9 copy-done.12
  176.7 1.9 shard_map.82
  178.6 0.9 convert_element_type.16
  179.5 4.2 %all-to-all-start.4 = ((f16[8,32,1152]{2,1,0:T(8,128)(2,1)}), f16[8,32,1152]{2,1,0:T(8,128)(2,1)}, u32[]{:S(2)}, u32[]{:S(2)}) async-start(f16[8,32,1152]{2,1,0:T(8,128)(2,1)} %bitcast.17), calls=%async_computation.4 | async-start | bytes 1179648 | tf_op jit(solution)/shard_map/all_to_all | solution.py:207
  183.7 2.6 collective-permute-start.5
  186.3 1.9 collective-permute-start.4
  188.3 1.5 collective-permute-done.4.out_g
  189.8 0.8 shard_map.83.second
  190.5 12.5 %all-to-all-done.4 = f16[8,32,1152]{2,1,0:T(8,128)(2,1)} async-done(((f16[8,32,1152]{2,1,0:T(8,128)(2,1)}), f16[8,32,1152]{2,1,0:T(8,128)(2,1)}, u32[]{:S(2)}, u32[]{:S(2)}) %all-to-all-start.4) | async-done | bytes 589856 | tf_op jit(solution)/shard_map/all_to_all | solution.py:207
  203.0 1.1 convert_element_type.17.parts
  204.2 0.9 copy-done.5
  205.1 0.4 shard_map.84
  205.5 20.1 %all_to_all.42 = bf16[8,32,1024]{2,1,0:T(8,128)(2,1)S(1)} all-to-all(bf16[8,32,1024]{2,1,0:T(8,128)(2,1)S(1)} %get-tuple-element.34), channel_id=1, replica_groups={{0,64,128,192,256,320,384,448},{32,96,160,224,288,352,416,480},{1,65,12..., dimensions={0} | all-to-all | bytes 1048576 | tf_op jit(solution)/shard_map/all_to_all | solution.py:207
  225.6 2.6 collective-permute-start.6
  228.2 1.5 collective-permute-done.6.gp_g
  229.8 1.5 shard_map.85
  231.3 2.8 collective-permute-start.11
  234.0 2.5 collective-permute-start.13
  237.0 9.4 %collective-permute-done.11.after = bf16[8,256,128]{2,1,0:T(8,128)(2,1)S(1)} collective-permute-done((bf16[8,256,128]{2,1,0:T(8,128)(2,1)}, bf16[8,256,128]{2,1,0:T(8,128)(2,1)S(1)}, u32[]{:S(2)}, u32[]{:S(2)}) %collective-permute-start.11) | collective-permute-done | bytes 524320 | tf_op jit(solution)/shard_map/ppermute | solution.py:338
  246.5 4.0 %collective-permute-start.12 = (bf16[4,256,128]{2,1,0:T(8,128)(2,1)S(1)}, bf16[4,256,128]{2,1,0:T(8,128)(2,1)S(1)}, u32[]{:S(2)}, u32[]{:S(2)}) collective-permute-start(bf16[4,256,128]{2,1,0:T(8,128)(2,1)S(1)} %slice.47), channel_id=1, source_target_pairs={{0,24},{1,25},{2,26},{3,27},{4,28},{5,29},{6,30},{7,31},{8,0},{9,1... | collective-permute-start | bytes 786440 | tf_op jit(solution)/shard_map/ppermute | solution.py:339
  250.6 1.9 collective-permute-start.14
  252.5 2.5 collective-permute-done.12.far_a
  255.0 5.0 %collective-permute-done.14.far_b = bf16[4,256,128]{2,1,0:T(8,128)(2,1)S(1)} collective-permute-done((bf16[4,256,128]{2,1,0:T(8,128)(2,1)S(1)}, bf16[4,256,128]{2,1,0:T(8,128)(2,1)S(1)}, u32[]{:S(2)}, u32[]{:S(2)}) %collective-permute-start.14) | collective-permute-done | bytes 262176 | tf_op jit(solution)/shard_map/ppermute | solution.py:340
  260.0 3.0 shard_map.87
  263.0 4.0 %all-to-all-start.7 = ((bf16[8,256,256]{2,1,0:T(8,128)(2,1)}), bf16[8,256,256]{2,1,0:T(8,128)(2,1)S(1)}, u32[]{:S(2)}, u32[]{:S(2)}) async-start(bf16[8,256,256]{2,1,0:T(8,128)(2,1)} %shard_map.87), calls=%async_computation.7 | async-start | bytes 2097152 | tf_op jit(solution)/shard_map/all_to_all | solution.py:350
  267.0 1.9 collective-permute-start.7
  268.9 3.4 %collective-permute-start.9 = (bf16[8,256,128]{2,1,0:T(8,128)(2,1)S(1)}, bf16[8,256,128]{2,1,0:T(8,128)(2,1)S(1)}, u32[]{:S(2)}, u32[]{:S(2)}) collective-permute-start(bf16[8,256,128]{2,1,0:T(8,128)(2,1)S(1)} %get-tuple-element.35.own), channel_id=1, source_target_pairs={{0,8},{1,9},{2,10},{3,11},{4,12},{5,13},{6,14},{7,15},{8,16},{9,17... | collective-permute-start | bytes 1572872 | tf_op jit(solution)/shard_map/ppermute | solution.py:337
  272.3 7.3 %collective-permute-done.7.after = bf16[8,256,128]{2,1,0:T(8,128)(2,1)S(1)} collective-permute-done((bf16[8,256,128]{2,1,0:T(8,128)(2,1)S(1)}, bf16[8,256,128]{2,1,0:T(8,128)(2,1)S(1)}, u32[]{:S(2)}, u32[]{:S(2)}) %collective-permute-start.7) | collective-permute-done | bytes 524320 | tf_op jit(solution)/shard_map/ppermute | solution.py:338
  279.6 3.4 %collective-permute-start.8 = (bf16[4,256,128]{2,1,0:T(8,128)(2,1)S(1)}, bf16[4,256,128]{2,1,0:T(8,128)(2,1)S(1)}, u32[]{:S(2)}, u32[]{:S(2)}) collective-permute-start(bf16[4,256,128]{2,1,0:T(8,128)(2,1)S(1)} %slice.45), channel_id=1, source_target_pairs={{0,24},{1,25},{2,26},{3,27},{4,28},{5,29},{6,30},{7,31},{8,0},{9,1... | collective-permute-start | bytes 786440 | tf_op jit(solution)/shard_map/ppermute | solution.py:339
  283.1 1.9 collective-permute-start.10
  285.0 2.0 collective-permute-done.8.far_a
  287.0 4.4 %collective-permute-done.10.far_b = bf16[4,256,128]{2,1,0:T(8,128)(2,1)S(1)} collective-permute-done((bf16[4,256,128]{2,1,0:T(8,128)(2,1)S(1)}, bf16[4,256,128]{2,1,0:T(8,128)(2,1)S(1)}, u32[]{:S(2)}, u32[]{:S(2)}) %collective-permute-start.10) | collective-permute-done | bytes 262176 | tf_op jit(solution)/shard_map/ppermute | solution.py:340
  291.4 2.5 shard_map.86
  293.9 0.3 all-to-all-done.7
  294.2 6.2 %all-to-all-start.6 = ((bf16[8,256,256]{2,1,0:T(8,128)(2,1)}), bf16[8,256,256]{2,1,0:T(8,128)(2,1)S(1)}, u32[]{:S(2)}, u32[]{:S(2)}) async-start(bf16[8,256,256]{2,1,0:T(8,128)(2,1)} %shard_map.86), calls=%async_computation.6 | async-start | bytes 2097152 | tf_op jit(solution)/shard_map/all_to_all | solution.py:350
  300.4 0.6 slice_reduce_fusion
  301.1 24.4 %all-to-all-done.6 = bf16[8,256,256]{2,1,0:T(8,128)(2,1)S(1)} async-done(((bf16[8,256,256]{2,1,0:T(8,128)(2,1)}), bf16[8,256,256]{2,1,0:T(8,128)(2,1)S(1)}, u32[]{:S(2)}, u32[]{:S(2)}) %all-to-all-start.6) | async-done | bytes 1048608 | tf_op jit(solution)/shard_map/all_to_all | solution.py:350
  325.6 0.8 pad_maximum_fusion
  (55 shorter events, 1.5 us)
Async XLA Ops:
  7.2 118.0 %copy-start = (f32[8192]{0:T(1024)S(1)}, f32[8192]{0:T(1024)}, u32[]{:S(2)}) copy-start(f32[8192]{0:T(1024)} %param.8) | copy-start | bytes 98308
  7.2 48.3 %all-gather.3.cloned.1.call-start = ((), (), s32[]{:S(2)}) async-start(), calls=%async_computation.8 | async-start | bytes 2359296 | tf_op jit(solution)/shard_map/all_gather | solution.py:212
  9.9 20.4 %all-to-all-start = ((s32[32,8,128]{2,1,0:T(8,128)}), s32[32,8,128]{2,1,0:T(8,128)S(1)}, u32[]{:S(2)}, u32[]{:S(2)}) async-start(s32[32,8,128]{2,1,0:T(8,128)} %broadcast_in_dim.76), calls=%async_computation | async-start | bytes 262144 | tf_op jit(solution)/shard_map/all_to_all | solution.py:217
  20.5 10.2 %collective-permute-start.2 = (f32[1,512]{1,0:T(1,128)}, f32[1,512]{1,0:T(1,128)S(1)}, u32[]{:S(2)}, u32[]{:S(2)}) collective-permute-start(f32[1,512]{1,0:T(1,128)} %bitcast.37), channel_id=1, source_target_pairs={{0,32},{32,0},{64,96},{96,64},{128,160},{160,128},{192,224},{224,1... | collective-permute-start | bytes 6152 | tf_op jit(solution)/shard_map/ppermute | solution.py:240
  23.3 1.0 copy-start.3
  24.4 0.7 copy-start.6
  25.3 0.7 copy-start.9
  26.0 4.7 %collective-permute-start = (bf16[256,512]{1,0:T(8,128)(2,1)S(1)}, bf16[256,512]{1,0:T(8,128)(2,1)S(1)}, u32[]{:S(2)}, u32[]{:S(2)}) collective-permute-start(bf16[256,512]{1,0:T(8,128)(2,1)S(1)} %get-tuple-element.21), channel_id=1, source_target_pairs={{0,32},{32,0},{64,96},{96,64},{128,160},{160,128},{192,224},{224,1... | collective-permute-start | bytes 786440 | tf_op jit(solution)/shard_map/ppermute | solution.py:240
  27.9 3.6 %collective-permute-start.1 = (bf16[256,512]{1,0:T(8,128)(2,1)S(1)}, bf16[256,512]{1,0:T(8,128)(2,1)S(1)}, u32[]{:S(2)}, u32[]{:S(2)}) collective-permute-start(bf16[256,512]{1,0:T(8,128)(2,1)S(1)} %get-tuple-element.22), channel_id=1, source_target_pairs={{0,32},{32,0},{64,96},{96,64},{128,160},{160,128},{192,224},{224,1... | collective-permute-start | bytes 786440 | tf_op jit(solution)/shard_map/ppermute | solution.py:240
  30.7 26.5 %copy-start.11 = (bf16[256,512]{1,0:T(8,128)(2,1)}, bf16[256,512]{1,0:T(8,128)(2,1)S(1)}, u32[]{:S(2)}) copy-start(bf16[256,512]{1,0:T(8,128)(2,1)S(1)} %collective-permute-done.x_o) | copy-start | bytes 786436
  57.8 48.0 %copy-start.8 = (s32[1,8]{1,0:T(1,128)S(1)}, s32[1,8]{1,0:T(1,128)}, u32[]{:S(2)}) copy-start(s32[1,8]{1,0:T(1,128)} %param.10) | copy-start | bytes 100
  106.8 9.7 %collective-permute-start.3 = (bf16[512,1024]{1,0:T(8,128)(2,1)S(1)}, bf16[512,1024]{1,0:T(8,128)(2,1)S(1)}, u32[]{:S(2)}, u32[]{:S(2)}) collective-permute-start(bf16[512,1024]{1,0:T(8,128)(2,1)S(1)} %shard_map.78.tiles), channel_id=1, source_target_pairs={{0,32},{32,0},{64,96},{96,64},{128,160},{160,128},{192,224},{224,1... | collective-permute-start | bytes 3145736 | tf_op jit(solution)/shard_map/ppermute | solution.py:262
  116.5 1.4 copy-start.1
  117.9 56.9 %copy-start.7 = (f32[512]{0:T(512)S(1)}, f32[512]{0:T(512)}, u32[]{:S(2)}) copy-start(f32[512]{0:T(512)} %param.9) | copy-start | bytes 6148
  117.9 36.5 %all-to-all-start.2 = ((f32[8,32,1024]{2,1,0:T(8,128)}), f32[8,32,1024]{2,1,0:T(8,128)S(1)}, u32[]{:S(2)}, u32[]{:S(2)}) async-start(f32[8,32,1024]{2,1,0:T(8,128)} %bitcast.9), calls=%async_computation.2 | async-start | bytes 2097152 | tf_op jit(solution)/shard_map/all_to_all | solution.py:207
  154.4 20.4 %copy-start.2 = (bf16[512,1024]{1,0:T(8,128)(2,1)S(1)}, bf16[512,1024]{1,0:T(8,128)(2,1)}, u32[]{:S(2)}) copy-start(bf16[512,1024]{1,0:T(8,128)(2,1)} %copy-done.1) | copy-start | bytes 3145732
  154.5 24.1 %copy-start.4 = (f32[32,1024]{1,0:T(8,128)}, f32[32,1024]{1,0:T(8,128)S(1)}, u32[]{:S(2)}) copy-start(f32[32,1024]{1,0:T(8,128)S(1)} %get-tuple-element.31.pre) | copy-start | bytes 393220
  174.8 1.0 copy-start.10
  175.8 0.9 copy-start.12
  179.5 23.6 %all-to-all-start.4 = ((f16[8,32,1152]{2,1,0:T(8,128)(2,1)}), f16[8,32,1152]{2,1,0:T(8,128)(2,1)}, u32[]{:S(2)}, u32[]{:S(2)}) async-start(f16[8,32,1152]{2,1,0:T(8,128)(2,1)} %bitcast.17), calls=%async_computation.4 | async-start | bytes 1179648 | tf_op jit(solution)/shard_map/all_to_all | solution.py:207
  183.7 6.1 %collective-permute-start.5 = (bf16[256,1024]{1,0:T(8,128)(2,1)S(1)}, bf16[256,1024]{1,0:T(8,128)(2,1)S(1)}, u32[]{:S(2)}, u32[]{:S(2)}) collective-permute-start(bf16[256,1024]{1,0:T(8,128)(2,1)S(1)} %bitcast.29), channel_id=1, source_target_pairs={{0,32},{32,0},{64,96},{96,64},{128,160},{160,128},{192,224},{224,1... | collective-permute-start | bytes 1572872 | tf_op jit(solution)/shard_map/ppermute | solution.py:304
  186.3 3.4 %collective-permute-start.4 = (bf16[256,512]{1,0:T(8,128)(2,1)S(1)}, bf16[256,512]{1,0:T(8,128)(2,1)S(1)}, u32[]{:S(2)}, u32[]{:S(2)}) collective-permute-start(bf16[256,512]{1,0:T(8,128)(2,1)S(1)} %get-tuple-element.32), channel_id=1, source_target_pairs={{0,32},{32,0},{64,96},{96,64},{128,160},{160,128},{192,224},{224,1... | collective-permute-start | bytes 786440 | tf_op jit(solution)/shard_map/ppermute | solution.py:305
  204.2 0.9 copy-start.5
  225.6 4.1 %collective-permute-start.6 = (bf16[256,1024]{1,0:T(8,128)(2,1)S(1)}, bf16[256,1024]{1,0:T(8,128)(2,1)S(1)}, u32[]{:S(2)}, u32[]{:S(2)}) collective-permute-start(bf16[256,1024]{1,0:T(8,128)(2,1)S(1)} %bitcast.31), channel_id=1, source_target_pairs={{0,32},{32,0},{64,96},{96,64},{128,160},{160,128},{192,224},{224,1... | collective-permute-start | bytes 1572872 | tf_op jit(solution)/shard_map/ppermute | solution.py:323
  231.3 15.2 %collective-permute-start.11 = (bf16[8,256,128]{2,1,0:T(8,128)(2,1)}, bf16[8,256,128]{2,1,0:T(8,128)(2,1)S(1)}, u32[]{:S(2)}, u32[]{:S(2)}) collective-permute-start(bf16[8,256,128]{2,1,0:T(8,128)(2,1)} %get-tuple-element.36.own), channel_id=1, source_target_pairs={{0,24},{1,25},{2,26},{3,27},{4,28},{5,29},{6,30},{7,31},{8,0},{9,1... | collective-permute-start | bytes 1572872 | tf_op jit(solution)/shard_map/ppermute | solution.py:338
  234.0 16.5 %collective-permute-start.13 = (bf16[8,256,128]{2,1,0:T(8,128)(2,1)}, bf16[8,256,128]{2,1,0:T(8,128)(2,1)S(1)}, u32[]{:S(2)}, u32[]{:S(2)}) collective-permute-start(bf16[8,256,128]{2,1,0:T(8,128)(2,1)} %get-tuple-element.36.own), channel_id=1, source_target_pairs={{0,8},{1,9},{2,10},{3,11},{4,12},{5,13},{6,14},{7,15},{8,16},{9,17... | collective-permute-start | bytes 1572872 | tf_op jit(solution)/shard_map/ppermute | solution.py:337
  246.5 8.5 %collective-permute-start.12 = (bf16[4,256,128]{2,1,0:T(8,128)(2,1)S(1)}, bf16[4,256,128]{2,1,0:T(8,128)(2,1)S(1)}, u32[]{:S(2)}, u32[]{:S(2)}) collective-permute-start(bf16[4,256,128]{2,1,0:T(8,128)(2,1)S(1)} %slice.47), channel_id=1, source_target_pairs={{0,24},{1,25},{2,26},{3,27},{4,28},{5,29},{6,30},{7,31},{8,0},{9,1... | collective-permute-start | bytes 786440 | tf_op jit(solution)/shard_map/ppermute | solution.py:339
  250.6 9.4 %collective-permute-start.14 = (bf16[4,256,128]{2,1,0:T(8,128)(2,1)S(1)}, bf16[4,256,128]{2,1,0:T(8,128)(2,1)S(1)}, u32[]{:S(2)}, u32[]{:S(2)}) collective-permute-start(bf16[4,256,128]{2,1,0:T(8,128)(2,1)S(1)} %slice.48), channel_id=1, source_target_pairs={{0,8},{1,9},{2,10},{3,11},{4,12},{5,13},{6,14},{7,15},{8,16},{9,17... | collective-permute-start | bytes 786440 | tf_op jit(solution)/shard_map/ppermute | solution.py:340
  263.0 31.2 %all-to-all-start.7 = ((bf16[8,256,256]{2,1,0:T(8,128)(2,1)}), bf16[8,256,256]{2,1,0:T(8,128)(2,1)S(1)}, u32[]{:S(2)}, u32[]{:S(2)}) async-start(bf16[8,256,256]{2,1,0:T(8,128)(2,1)} %shard_map.87), calls=%async_computation.7 | async-start | bytes 2097152 | tf_op jit(solution)/shard_map/all_to_all | solution.py:350
  267.0 12.6 %collective-permute-start.7 = (bf16[8,256,128]{2,1,0:T(8,128)(2,1)S(1)}, bf16[8,256,128]{2,1,0:T(8,128)(2,1)S(1)}, u32[]{:S(2)}, u32[]{:S(2)}) collective-permute-start(bf16[8,256,128]{2,1,0:T(8,128)(2,1)S(1)} %get-tuple-element.35.own), channel_id=1, source_target_pairs={{0,24},{1,25},{2,26},{3,27},{4,28},{5,29},{6,30},{7,31},{8,0},{9,1... | collective-permute-start | bytes 1572872 | tf_op jit(solution)/shard_map/ppermute | solution.py:338
  268.9 14.1 %collective-permute-start.9 = (bf16[8,256,128]{2,1,0:T(8,128)(2,1)S(1)}, bf16[8,256,128]{2,1,0:T(8,128)(2,1)S(1)}, u32[]{:S(2)}, u32[]{:S(2)}) collective-permute-start(bf16[8,256,128]{2,1,0:T(8,128)(2,1)S(1)} %get-tuple-element.35.own), channel_id=1, source_target_pairs={{0,8},{1,9},{2,10},{3,11},{4,12},{5,13},{6,14},{7,15},{8,16},{9,17... | collective-permute-start | bytes 1572872 | tf_op jit(solution)/shard_map/ppermute | solution.py:337
  279.6 7.4 %collective-permute-start.8 = (bf16[4,256,128]{2,1,0:T(8,128)(2,1)S(1)}, bf16[4,256,128]{2,1,0:T(8,128)(2,1)S(1)}, u32[]{:S(2)}, u32[]{:S(2)}) collective-permute-start(bf16[4,256,128]{2,1,0:T(8,128)(2,1)S(1)} %slice.45), channel_id=1, source_target_pairs={{0,24},{1,25},{2,26},{3,27},{4,28},{5,29},{6,30},{7,31},{8,0},{9,1... | collective-permute-start | bytes 786440 | tf_op jit(solution)/shard_map/ppermute | solution.py:339
  283.1 8.3 %collective-permute-start.10 = (bf16[4,256,128]{2,1,0:T(8,128)(2,1)S(1)}, bf16[4,256,128]{2,1,0:T(8,128)(2,1)S(1)}, u32[]{:S(2)}, u32[]{:S(2)}) collective-permute-start(bf16[4,256,128]{2,1,0:T(8,128)(2,1)S(1)} %slice.46), channel_id=1, source_target_pairs={{0,8},{1,9},{2,10},{3,11},{4,12},{5,13},{6,14},{7,15},{8,16},{9,17... | collective-permute-start | bytes 786440 | tf_op jit(solution)/shard_map/ppermute | solution.py:340
  294.2 31.3 %all-to-all-start.6 = ((bf16[8,256,256]{2,1,0:T(8,128)(2,1)}), bf16[8,256,256]{2,1,0:T(8,128)(2,1)S(1)}, u32[]{:S(2)}, u32[]{:S(2)}) async-start(bf16[8,256,256]{2,1,0:T(8,128)(2,1)} %shard_map.86), calls=%async_computation.6 | async-start | bytes 2097152 | tf_op jit(solution)/shard_map/all_to_all | solution.py:350
Sparse Core Ops, SparseCore 0:
  10.1 45.3 all-gather.2
